TPU v7x, 32 devices: a whole 2x2x4 slice. The times are simulated.
32 devices in a mesh: groups: 2 (over x), row: 8 (over z, y), col: 2 (over core).
Axes of the slice: x: 2, y: 2, z: 4, core: 2. Of those that a mesh axis runs over, the one named last changes fastest.
Arguments:
- voltages: bfloat16 [256, 263936], P(('groups', 'row', 'col')), parts along dimension 0, may hold values from -6 to 6
- owner_block: int32 [16], replicated, may hold values from 0 to 15, each once
Outputs:
- visibility: float32 [32, 8, 2, 128, 128], P(('groups', 'row', 'col')), parts along dimension 0
- beam: float32 [32, 8, 1024], P(('groups', 'row', 'col')), parts along dimension 0
There are 2 independent parts, one for each index of `groups`. A program takes and returns all parts, laid end to end along the dimension named above; an argument that names none is the same for every part. Nothing has to cross between parts.
Inputs may be any that keep to these rules, and one draw needn't show every extreme that they name: owner_block is a permutation: every channel block has exactly one owner device, device d of a part ending with block owner_block[d].
All inputs are finite; a program needn't handle non-finite values.
Results may differ from a plain program's by a relative error of at most 0.0038.
Values may be sent and summed in bfloat16 or wider, within the bound.
No kernel may reach another device: no remote copies, remote signals or barrier semaphores. Data moves between devices by JAX's collectives and lax.ppermute only.
A program may use at most 128 MiB of HBM per device.

v0:
```python
import math

import jax
import jax.numpy as jnp
from jax import lax
from jax.sharding import PartitionSpec as P

CHANS = 128
TAPS = 8
SPECTRA = 1024


def window_table(tap_count, length):
    total = tap_count * length
    offsets = jnp.arange(total).astype(jnp.float32)
    profile = jnp.sinc((offsets - total / 2 + 0.5) / length) * (
        0.5 - 0.5 * jnp.cos(2 * math.pi * (offsets + 0.5) / total)
    )
    profile = profile * jnp.sqrt(length / jnp.sum(profile * profile))
    return profile.reshape(tap_count, length).astype(jnp.float32)


def dft_table(channels):
    length = 2 * channels
    times = jnp.arange(length, dtype=jnp.int32)
    freqs = jnp.arange(channels, dtype=jnp.int32)
    steps_mod = freqs[:, None] * times[None, :] % length
    phase = 2 * math.pi * steps_mod.astype(jnp.float32) / length
    table = jnp.concatenate([jnp.cos(phase), -jnp.sin(phase)], 0) / math.sqrt(length)
    return table.astype(jnp.bfloat16)


def body(voltages, owner_block):
    in_dev = voltages.shape[0]
    length = 2 * CHANS
    window = window_table(TAPS, length)
    fourier = dft_table(CHANS)
    frames = voltages.reshape(in_dev, SPECTRA + TAPS - 1, length)
    filtered = jnp.zeros((in_dev, SPECTRA, length), jnp.float32)
    for tap_index in range(TAPS):
        filtered = filtered + window[tap_index] * frames[
            :, tap_index : tap_index + SPECTRA, :
        ].astype(jnp.float32)
    filtered = filtered.astype(jnp.bfloat16)
    spectrum = jnp.einsum(
        "ct,ist->cis", fourier, filtered, preferred_element_type=jnp.float32
    ).astype(jnp.bfloat16)
    blocks = lax.axis_size(("row", "col"))
    per_block = CHANS // blocks
    inputs_all = in_dev * blocks
    spectrum = spectrum.reshape(2, blocks, per_block, in_dev, SPECTRA)
    spectrum = jnp.take(spectrum, owner_block, axis=1)
    owned_spectra = spectrum.reshape(2, blocks, per_block, 1, in_dev, SPECTRA)
    owned_spectra = lax.all_to_all(
        owned_spectra, ("row", "col"), split_axis=1, concat_axis=3, tiled=True
    )
    columns = owned_spectra.reshape(2, per_block, inputs_all, SPECTRA)
    real_part = columns[0]
    imag_part = columns[1]
    real_wide = real_part.astype(jnp.float32)
    imag_wide = imag_part.astype(jnp.float32)
    beam = (jnp.sum(real_wide * real_wide + imag_wide * imag_wide, axis=1) / inputs_all)[None]
    row_side = jnp.concatenate([real_part, imag_part], axis=2)
    turned = jnp.concatenate([imag_part, -real_part], axis=2)
    stacked = jnp.stack([row_side, turned], 1)
    visibility = (
        jnp.einsum("cpis,cjs->cpij", stacked, row_side, preferred_element_type=jnp.float32)
        / SPECTRA
    )
    return (visibility[None], beam)


def solution(mesh):
    in_specs = (P(("groups", "row", "col"), None), P())
    out_specs = (
        P(("groups", "row", "col"), None, None, None, None),
        P(("groups", "row", "col"), None, None),
    )
    return jax.shard_map(body, mesh=mesh, in_specs=in_specs, out_specs=out_specs, check_vma=False)
```

profile of v0, /device:TPU:9, one launch (start us, length us, event | category | flops | bytes accessed | tf_op | source)
XLA Modules:
  0.0 177.3 jit_solution(18220939408559893618)
XLA Ops:
  0.6 0.7 multiply_reduce_fusion
  1.3 0.5 sine_negate_fusion
  1.8 0.7 compare_select_fusion
  2.5 0.7 compare_and_fusion
  3.1 23.5 %fusion.44 = (bf16[8,1024,256]{2,0,1:T(8,128)(2,1)}, bf16[8,1024,256]{2,0,1:T(8,128)(2,1)}, bf16[8,1024,256]{2,0,1:T(8,128)(2,1)}, bf16[8,1024,256]{2,0,1:T(8,12...) fusion(bf16[8,1031,256]{2,0,1:T(8,128)(2,1)} %bitcast.37), kind=kLoop, calls=%fused_computation.66 | loop fusion | bytes 67108864 | tf_op jit(solution)/shard_map/slice | solution.py:41
  27.3 0.1 broadcast_multiply_fusion
  27.4 31.7 %fusion.5 = bf16[256,8,1024]{2,0,1:T(8,128)(2,1)} fusion(bf16[8,1024,256]{2,0,1:T(8,128)(2,1)} %get-tuple-element.9, bf16[8,1024,256]{2,0,1:T(8,128)(2,1)} %get-tuple-element.3, bf16[8,1024,256]{2,0,1:T(8,128)(2,1)} %get-tuple-element.4, bf16[8,1024,256]{2,0,1:T(8,128)(2,1)} %get-tuple-element.5, bf16[8,1024,256]{2,0,1:T(8,128)(2,1)} %get-tuple-element.6, ...), kind=kOutput, calls=%fused_computation.12 | convolution fusion | flops 1126367232 | bytes 38019072 | tf_op jit(solution)/shard_map/ct,ist->cis/dot_general | solution.py:45
  59.2 5.0 %gather_fusion = bf16[16,2,8,8,1024]{4,2,1,3,0:T(8,128)(2,1)} fusion(bf16[2,16,8,8,1024]{4,2,1,0,3:T(8,128)(2,1)} %bitcast.44, s32[1024]{0:T(1024)S(1)} %pad_clamp_fusion), kind=kCustom, calls=%fused_computation | custom fusion | bytes 8388672 | tf_op jit(solution)/shard_map/jit(_take)/gather | solution.py:52
  64.1 2.6 %bitcast_select_fusion = bf16[2,16,8,1,8,1024]{5,2,0,4,3,1:T(8,128)(2,1)S(1)} fusion(bf16[16,2,8,8,1024]{4,2,1,3,0:T(8,128)(2,1)} %gather_fusion, pred[16]{0:T(512)(128)(4,1)S(1)} %compare_and_fusion), kind=kLoop, calls=%fused_computation.8 | loop fusion | flops 2097152 | bytes 8388624 | tf_op jit(solution)/shard_map/jit(_take)/select_n | solution.py:52
  66.8 99.2 %all_to_all.15 = bf16[2,16,8,1,8,1024]{5,2,0,4,3,1:T(8,128)(2,1)S(1)} all-to-all(bf16[2,16,8,1,8,1024]{5,2,0,4,3,1:T(8,128)(2,1)S(1)} %bitcast_select_fusion), channel_id=1, replica_groups=mesh['groups'=2,'row'=8,'col'=2] {'row','col'}, dimensions={1} | all-to-all | bytes 8388608 | tf_op jit(solution)/shard_map/all_to_all | solution.py:54
  166.0 0.5 fusion.45
  166.5 1.2 copy.78
  167.6 2.4 %fusion.43 = bf16[8,128,1024]{2,1,0:T(8,128)(2,1)S(1)} fusion(bf16[1,1,8,16,1,8,1024]{6,2,0,5,3,4,1:T(8,128)(2,1)S(1)} %get-tuple-element.10), kind=kLoop, calls=%fused_computation.65 | loop fusion | flops 1048576 | bytes 4194304 | tf_op jit(solution)/shard_map/neg | solution.py:64
  170.1 1.0 add_reduce_fusion
  171.1 1.2 copy.77
  172.2 0.6 multiply_bitcast_fusion
  172.9 0.9 fusion.4
  173.8 3.6 %fusion.11 = f32[1,8,2,128,128]{4,3,2,1,0:T(8,128)} fusion(bf16[8,128,1024]{2,1,0:T(8,128)(2,1)S(1)} %bitcast.43, bf16[8,128,1024]{2,1,0:T(8,128)(2,1)S(1)} %bitcast.41, bf16[8,1,128,2048]{3,2,0,1:T(8,128)(2,1)S(1)} %get-tuple-element.13, bf16[8,1,128,2048]{3,2,0,1:T(8,128)(2,1)S(1)} %get-tuple-element.12), kind=kOutput, calls=%fused_computation.16 | convolution fusion | flops 1086586880 | bytes 13631488 | tf_op jit(solution)/shard_map/cpis,cjs->cpij/dot_general | solution.py:67
  (2 shorter events, 0.0 us)
where the time goes:
time: 178 us; the launch traced here: 177 us
  blocking collectives  99.2 us (56%)
  matrix products  35.3 us (20%)
  local copies, waits for them, and re-layouts  31.2 us (18%)
  other arithmetic  10.2 us (6%)
    all_to_all x1, blocking collectives, body(): lax.all_to_all(owned_spectra, ('row', 'col'), split_axis=1, concat_axis=3...  99.2 us
    dot_general x1, matrix products, body(): jnp.einsum('ct,ist->cis', fourier, filtered, preferred_element_type=jnp.f...  31.7 us
    slice x1, local copies, waits for them, and re-layouts, body(): frames[:, tap_index:tap_index + SPECTRA, :].astype(jnp.float32)  23.5 us
    gather x1, local copies, waits for them, and re-layouts, body(): spectrum = jnp.take(spectrum, owner_block, axis=1)  4.97 us
    dot_general x1, matrix products, body(): jnp.einsum('cpis,cjs->cpij', stacked, row_side, preferred_element_type=jn...  3.58 us

commit v1 on v0

v1 whole, which is shorter than its diff:
```python
import functools
import math

import jax
import jax.numpy as jnp
import numpy as np
from jax import lax
from jax.experimental import pallas as pl
from jax.experimental.pallas import tpu as pltpu
from jax.sharding import PartitionSpec as P

CHANS = 128
TAPS = 8
SPECTRA = 1024
LENGTH = 2 * CHANS
AXES = ("row", "col")
LANES = 128
FRAME_GROUP = 16
VMEM = 48 * 1024 * 1024


def window_table():
    total = TAPS * LENGTH
    offsets = np.arange(total, dtype=np.float64)
    profile = np.sinc((offsets - total / 2 + 0.5) / LENGTH) * (
        0.5 - 0.5 * np.cos(2 * math.pi * (offsets + 0.5) / total)
    )
    profile = profile * np.sqrt(LENGTH / np.sum(profile * profile))
    return profile.reshape(TAPS, LENGTH).astype(np.float32)


def dft_table():
    times = np.arange(LENGTH)
    freqs = np.arange(CHANS)
    phase = 2 * math.pi * ((freqs[:, None] * times[None, :]) % LENGTH) / LENGTH
    table = np.concatenate([np.cos(phase), -np.sin(phase)], 0) / math.sqrt(LENGTH)
    return table.astype(np.float32).astype(jnp.bfloat16)


def spectra_kernel(tile, in_dev, blocks, owner, frames, window, fourier, *rest):
    outs, (filtered, spectra) = rest[:blocks], rest[blocks:]
    per_block = CHANS // blocks
    me = lax.axis_index(AXES)

    @pl.loop(0, tile // FRAME_GROUP)
    def _(group):
        first = group * FRAME_GROUP
        for half in range(LENGTH // LANES):
            cols = slice(half * LANES, (half + 1) * LANES)
            held = frames[pl.ds(first, FRAME_GROUP + TAPS - 1), :, cols].astype(jnp.float32)
            total = window[0:1, cols] * held[0:FRAME_GROUP]
            for tap in range(1, TAPS):
                total = total + window[tap : tap + 1, cols] * held[tap : tap + FRAME_GROUP]
            filtered[half, pl.ds(first * in_dev, FRAME_GROUP * in_dev), :] = total.reshape(
                FRAME_GROUP * in_dev, LANES
            )

    for i in range(in_dev):
        rows = jnp.concatenate(
            [filtered[half, pl.ds(i, tile, stride=in_dev), :] for half in range(LENGTH // LANES)], axis=1
        ).astype(jnp.bfloat16)
        product = lax.dot_general(
            fourier[...], rows, (((1,), (1,)), ((), ())), preferred_element_type=jnp.float32
        )
        for part in range(tile // LANES):
            spectra[part, pl.ds(i * 2 * CHANS, 2 * CHANS), :] = product[:, part * LANES : (part + 1) * LANES]

    for other in range(blocks):
        base = owner[me ^ other] * per_block
        for channel in range(per_block):
            for part in range(tile // LANES):
                pair = [
                    spectra[part, pl.ds(base + plane * CHANS + channel, in_dev, stride=2 * CHANS), :]
                    for plane in range(2)
                ]
                outs[other][channel, :, part * LANES : (part + 1) * LANES] = jnp.concatenate(
                    pair, axis=0
                ).astype(jnp.bfloat16)


def make_spectra(frames, owner_block, window, fourier, start, count, blocks, tile):
    in_dev = frames.shape[1]
    per_block = CHANS // blocks
    return pl.pallas_call(
        functools.partial(spectra_kernel, tile, in_dev, blocks),
        grid_spec=pltpu.PrefetchScalarGridSpec(
            num_scalar_prefetch=1,
            grid=(count // tile,),
            in_specs=[
                pl.BlockSpec(
                    (pl.Element(tile + TAPS - 1), pl.Element(in_dev), pl.Element(LENGTH)),
                    lambda step, owner: (start + step * tile, 0, 0),
                ),
                pl.BlockSpec((TAPS, LENGTH), lambda step, owner: (0, 0)),
                pl.BlockSpec((LENGTH, LENGTH), lambda step, owner: (0, 0)),
            ],
            out_specs=[
                pl.BlockSpec((per_block, 2 * in_dev, tile), lambda step, owner: (0, 0, step))
                for _ in range(blocks)
            ],
            scratch_shapes=[
                pltpu.VMEM((LENGTH // LANES, tile * in_dev, LANES), jnp.float32),
                pltpu.VMEM((tile // LANES, in_dev * 2 * CHANS, LANES), jnp.float32),
            ],
        ),
        out_shape=[
            jax.ShapeDtypeStruct((per_block, 2 * in_dev, count), jnp.bfloat16) for _ in range(blocks)
        ],
        compiler_params=pltpu.CompilerParams(vmem_limit_bytes=VMEM),
        cost_estimate=pl.CostEstimate(
            flops=2 * count * in_dev * LENGTH * LENGTH, bytes_accessed=4 * count * in_dev * LENGTH, transcendentals=0
        ),
    )(owner_block, frames, window, fourier)


def correlate_kernel(in_dev, blocks, scale, *refs):
    parts, (visibility, beam, planes) = refs[:blocks], refs[blocks:]
    count = parts[0].shape[2]
    inputs = in_dev * blocks
    me = lax.axis_index(AXES)
    channel = pl.program_id(0)
    power = jnp.zeros((in_dev, count), jnp.float32)
    for other in range(blocks):
        wide = parts[other][0].astype(jnp.float32)
        real_part, imag_part = wide[:in_dev], wide[in_dev:]
        power = power + (real_part * real_part + imag_part * imag_part)
        source = me ^ other
        planes[0, source] = real_part
        planes[1, source] = imag_part
    beam[pl.ds(channel, 1), :] = jnp.sum(power, axis=0, keepdims=True) * (1.0 / inputs)
    both = planes[...].reshape(2 * inputs, count).astype(jnp.bfloat16)
    gram = lax.dot_general(both, both, (((1,), (1,)), ((), ())), preferred_element_type=jnp.float32)
    visibility[0, 0] = (gram[:inputs, :inputs] + gram[inputs:, inputs:]) * scale
    visibility[0, 1] = (gram[inputs:, :inputs] - gram[:inputs, inputs:]) * scale


def correlate(parts, blocks):
    per_block, rows, count = parts[0].shape
    in_dev = rows // 2
    inputs = in_dev * blocks
    return pl.pallas_call(
        functools.partial(correlate_kernel, in_dev, blocks, 1.0 / SPECTRA),
        grid=(per_block,),
        in_specs=[pl.BlockSpec((1, rows, count), lambda channel: (channel, 0, 0)) for _ in range(blocks)],
        out_specs=[
            pl.BlockSpec((1, 2, inputs, inputs), lambda channel: (channel, 0, 0, 0)),
            pl.BlockSpec((per_block, count), lambda channel: (0, 0)),
        ],
        scratch_shapes=[pltpu.VMEM((2, blocks, in_dev, count), jnp.float32)],
        out_shape=[
            jax.ShapeDtypeStruct((per_block, 2, inputs, inputs), jnp.float32),
            jax.ShapeDtypeStruct((per_block, count), jnp.float32),
        ],
        compiler_params=pltpu.CompilerParams(vmem_limit_bytes=VMEM),
        cost_estimate=pl.CostEstimate(
            flops=8 * per_block * inputs * inputs * count, bytes_accessed=4 * per_block * inputs * count, transcendentals=0
        ),
    )(*parts)


def body(voltages, owner_block):
    in_dev = voltages.shape[0]
    blocks = lax.axis_size(AXES)
    window = jnp.asarray(window_table())
    fourier = jnp.asarray(dft_table())
    frames = voltages.reshape(in_dev, SPECTRA + TAPS - 1, LENGTH).transpose(1, 0, 2)
    own = make_spectra(frames, owner_block, window, fourier, 0, SPECTRA, blocks, 256)
    parts = [own[0]] + [
        lax.ppermute(own[other], AXES, [(source, source ^ other) for source in range(blocks)])
        for other in range(1, blocks)
    ]
    visibility, beam = correlate(parts, blocks)
    return (visibility[None], beam[None])


def solution(mesh):
    in_specs = (P(("groups", "row", "col"), None), P())
    out_specs = (
        P(("groups", "row", "col"), None, None, None, None),
        P(("groups", "row", "col"), None, None),
    )
    return jax.shard_map(body, mesh=mesh, in_specs=in_specs, out_specs=out_specs, check_vma=False)
```

time: 178 us -> 132 us (0.74)
  blocking collectives: 99.2 us -> 0 us
  waiting for transfers between devices: 0 us -> 80.9 us
  matrix products: 35.3 us -> 0 us
  local copies, waits for them, and re-layouts: 31.2 us -> 2.25 us
  starting transfers between devices: 0 us -> 27 us
  Pallas kernels: 0 us -> 19.6 us
  other arithmetic: 10.2 us -> 0 us
    all_to_all x1 -> x0, blocking collectives: 99.2 us -> none  [body(): lax.all_to_all(owned_spectra, ('row', 'col'), split_axis=1, concat_axis=3...]
    ppermute x0 -> x15, waiting for transfers between devices: none -> 80.9 us  [body(): lax.ppermute(own[other], AXES, [(source, source ^ other) for source in ra...]
    dot_general x2 -> x0, matrix products: 35.3 us -> none  [the longest x1 31.7 us: body(): jnp.einsum('ct,ist->cis', fourier, filtered, preferred_element_type=jnp.f...]
    ppermute x0 -> x15, starting transfers between devices: none -> 27 us  [body(): lax.ppermute(own[other], AXES, [(source, source ^ other) for source in ra...]
    slice x5 -> x0, local copies, waits for them, and re-layouts: 26.2 us -> none  [the longest x1 23.5 us: body(): frames[:, tap_index:tap_index + SPECTRA, :].astype(jnp.float32)]
    pallas_call x0 -> x2, Pallas kernels: none -> 19.6 us  [the longest x1 14.6 us: make_spectra(): pl.pallas_call(functools.partial(spectra_kernel, tile, in_dev, blocks), g...]
    gather x1 -> x0, local copies, waits for them, and re-layouts: 4.97 us -> none  [body(): spectrum = jnp.take(spectrum, owner_block, axis=1)]
    select_n x2 -> x0, other arithmetic: 3.31 us -> none  [body(): spectrum = jnp.take(spectrum, owner_block, axis=1)]
  transfers between devices with their start and end apart: 0 -> 15, of which waited for: 0 -> 11; matrix products, arithmetic and copies ran while one was open for 0% -> 0% of each run, Pallas kernels for 0% -> 0%
where the time goes in v1:
time: 132 us; the launch traced here: 130 us
  waiting for transfers between devices  80.9 us (61%)
  starting transfers between devices  27 us (20%)
  Pallas kernels  19.6 us (15%)
  local copies, waits for them, and re-layouts  2.25 us (2%)
    ppermute x15, waiting for transfers between devices, body(): lax.ppermute(own[other], AXES, [(source, source ^ other) for source in ra...  80.9 us
    ppermute x15, starting transfers between devices, body(): lax.ppermute(own[other], AXES, [(source, source ^ other) for source in ra...  27 us
    pallas_call x1, Pallas kernels, make_spectra(): pl.pallas_call(functools.partial(spectra_kernel, tile, in_dev, blocks), g...  14.6 us
    pallas_call x1, Pallas kernels, correlate(): pl.pallas_call(functools.partial(correlate_kernel, in_dev, blocks, 1.0 /...  5 us
  transfers between devices with their start and end apart: 15, of which 11 were waited for; matrix products, arithmetic and copies ran while one was open for 0% of the time, Pallas kernels for 0%

profile of v1, /device:TPU:9, one launch (start us, length us, event | category | flops | bytes accessed | tf_op | source)
XLA Modules:
  0.0 130.4 jit_solution(3515938555650193558)
XLA Ops:
  0.6 0.0 copy-start
  0.6 0.9 copy-done
  1.5 0.7 copy-done.1
  2.2 0.7 copy-done.2
  2.9 14.6 %shard_map.59 = (bf16[8,16,1024]{2,1,0:T(8,128)(2,1)S(1)}, bf16[8,16,1024]{2,1,0:T(8,128)(2,1)S(1)}, bf16[8,16,1024]{2,1,0:T(8,128)(2,1)S(1)}, bf16[8,16,1024]{2...) custom-call(s32[16]{0:T(128)S(1)} %copy-done.2, ...), custom_call_target="tpu_custom_call" | custom-call | flops 1073741824 | bytes 8388608 | tf_op jit(solution)/shard_map/pallas_call | solution.py:84
  17.5 0.7 collective-permute-start
  18.3 1.3 collective-permute-start.1
  19.5 0.5 collective-permute-start.2
  20.0 1.8 %collective-permute-start.4 = (bf16[8,16,1024]{2,1,0:T(8,128)(2,1)S(1)}, bf16[8,16,1024]{2,1,0:T(8,128)(2,1)S(1)}, u32[]{:S(2)}, u32[]{:S(2)}) collective-permute-start(bf16[8,16,1024]{2,1,0:T(8,128)(2,1)S(1)} %get-tuple-element.25), channel_id=1, source_target_pairs={{0,5},{1,4},{2,7},{3,6},{4,1},{5,0},{6,3},{7,2},{8,13},{9,12},{10,... | collective-permute-start | bytes 786440 | tf_op jit(solution)/shard_map/ppermute | solution.py:169
  21.8 1.1 collective-permute-start.5
  22.9 3.2 %collective-permute-done.1.refs_2_ = bf16[8,16,1024]{2,1,0:T(8,128)(2,1)S(1)} collective-permute-done((bf16[8,16,1024]{2,1,0:T(8,128)(2,1)S(1)}, bf16[8,16,1024]{2,1,0:T(8,128)(2,1)S(1)}, u32[]{:S(2)}, u32[]{:S(2)}) %collective-permute-start.1) | collective-permute-done | bytes 262176 | tf_op jit(solution)/shard_map/ppermute | solution.py:169
  26.1 2.3 %collective-permute-start.6 = (bf16[8,16,1024]{2,1,0:T(8,128)(2,1)S(1)}, bf16[8,16,1024]{2,1,0:T(8,128)(2,1)S(1)}, u32[]{:S(2)}, u32[]{:S(2)}) collective-permute-start(bf16[8,16,1024]{2,1,0:T(8,128)(2,1)S(1)} %get-tuple-element.27), channel_id=1, source_target_pairs={{0,7},{1,6},{2,5},{3,4},{4,3},{5,2},{6,1},{7,0},{8,15},{9,14},{10,... | collective-permute-start | bytes 786440 | tf_op jit(solution)/shard_map/ppermute | solution.py:169
  28.5 3.8 %collective-permute-done.2.refs_3_ = bf16[8,16,1024]{2,1,0:T(8,128)(2,1)S(1)} collective-permute-done((bf16[8,16,1024]{2,1,0:T(8,128)(2,1)S(1)}, bf16[8,16,1024]{2,1,0:T(8,128)(2,1)S(1)}, u32[]{:S(2)}, u32[]{:S(2)}) %collective-permute-start.2) | collective-permute-done | bytes 262176 | tf_op jit(solution)/shard_map/ppermute | solution.py:169
  32.2 2.3 %collective-permute-start.7 = (bf16[8,16,1024]{2,1,0:T(8,128)(2,1)S(1)}, bf16[8,16,1024]{2,1,0:T(8,128)(2,1)S(1)}, u32[]{:S(2)}, u32[]{:S(2)}) collective-permute-start(bf16[8,16,1024]{2,1,0:T(8,128)(2,1)S(1)} %get-tuple-element.28), channel_id=1, source_target_pairs={{0,8},{1,9},{2,10},{3,11},{4,12},{5,13},{6,14},{7,15},{8,0},{9,1},... | collective-permute-start | bytes 786440 | tf_op jit(solution)/shard_map/ppermute | solution.py:169
  34.5 0.0 collective-permute-done.3.refs_4_
  34.5 0.2 collective-permute-start.8
  34.7 0.0 collective-permute-done.4.refs_5_
  34.7 3.3 %collective-permute-start.9 = (bf16[8,16,1024]{2,1,0:T(8,128)(2,1)S(1)}, bf16[8,16,1024]{2,1,0:T(8,128)(2,1)S(1)}, u32[]{:S(2)}, u32[]{:S(2)}) collective-permute-start(bf16[8,16,1024]{2,1,0:T(8,128)(2,1)S(1)} %get-tuple-element.30), channel_id=1, source_target_pairs={{0,10},{1,11},{2,8},{3,9},{4,14},{5,15},{6,12},{7,13},{8,2},{9,3},... | collective-permute-start | bytes 786440 | tf_op jit(solution)/shard_map/ppermute | solution.py:169
  38.0 10.3 %collective-permute-done.5.refs_6_ = bf16[8,16,1024]{2,1,0:T(8,128)(2,1)S(1)} collective-permute-done((bf16[8,16,1024]{2,1,0:T(8,128)(2,1)S(1)}, bf16[8,16,1024]{2,1,0:T(8,128)(2,1)S(1)}, u32[]{:S(2)}, u32[]{:S(2)}) %collective-permute-start.5) | collective-permute-done | bytes 262176 | tf_op jit(solution)/shard_map/ppermute | solution.py:169
  48.3 4.5 %collective-permute-start.10 = (bf16[8,16,1024]{2,1,0:T(8,128)(2,1)S(1)}, bf16[8,16,1024]{2,1,0:T(8,128)(2,1)S(1)}, u32[]{:S(2)}, u32[]{:S(2)}) collective-permute-start(bf16[8,16,1024]{2,1,0:T(8,128)(2,1)S(1)} %get-tuple-element.31), channel_id=1, source_target_pairs={{0,11},{1,10},{2,9},{3,8},{4,15},{5,14},{6,13},{7,12},{8,3},{9,2},... | collective-permute-start | bytes 786440 | tf_op jit(solution)/shard_map/ppermute | solution.py:169
  52.7 1.1 collective-permute-done.6.refs_7_
  53.9 0.2 collective-permute-start.11
  54.1 2.3 %collective-permute-start.12 = (bf16[8,16,1024]{2,1,0:T(8,128)(2,1)S(1)}, bf16[8,16,1024]{2,1,0:T(8,128)(2,1)S(1)}, u32[]{:S(2)}, u32[]{:S(2)}) collective-permute-start(bf16[8,16,1024]{2,1,0:T(8,128)(2,1)S(1)} %get-tuple-element.33), channel_id=1, source_target_pairs={{0,13},{1,12},{2,15},{3,14},{4,9},{5,8},{6,11},{7,10},{8,5},{9,4},... | collective-permute-start | bytes 786440 | tf_op jit(solution)/shard_map/ppermute | solution.py:169
  56.4 23.3 %collective-permute-done.8.refs_9_ = bf16[8,16,1024]{2,1,0:T(8,128)(2,1)S(1)} collective-permute-done((bf16[8,16,1024]{2,1,0:T(8,128)(2,1)S(1)}, bf16[8,16,1024]{2,1,0:T(8,128)(2,1)S(1)}, u32[]{:S(2)}, u32[]{:S(2)}) %collective-permute-start.8) | collective-permute-done | bytes 262176 | tf_op jit(solution)/shard_map/ppermute | solution.py:169
  79.7 5.6 %collective-permute-done.9.refs_10_ = bf16[8,16,1024]{2,1,0:T(8,128)(2,1)S(1)} collective-permute-done((bf16[8,16,1024]{2,1,0:T(8,128)(2,1)S(1)}, bf16[8,16,1024]{2,1,0:T(8,128)(2,1)S(1)}, u32[]{:S(2)}, u32[]{:S(2)}) %collective-permute-start.9) | collective-permute-done | bytes 262176 | tf_op jit(solution)/shard_map/ppermute | solution.py:169
  85.3 6.5 %collective-permute-start.14 = (bf16[8,16,1024]{2,1,0:T(8,128)(2,1)S(1)}, bf16[8,16,1024]{2,1,0:T(8,128)(2,1)S(1)}, u32[]{:S(2)}, u32[]{:S(2)}) collective-permute-start(bf16[8,16,1024]{2,1,0:T(8,128)(2,1)S(1)} %get-tuple-element.35), channel_id=1, source_target_pairs={{0,15},{1,14},{2,13},{3,12},{4,11},{5,10},{6,9},{7,8},{8,7},{9,6},... | collective-permute-start | bytes 786440 | tf_op jit(solution)/shard_map/ppermute | solution.py:169
  91.8 10.3 %collective-permute-done.10.refs_11_ = bf16[8,16,1024]{2,1,0:T(8,128)(2,1)S(1)} collective-permute-done((bf16[8,16,1024]{2,1,0:T(8,128)(2,1)S(1)}, bf16[8,16,1024]{2,1,0:T(8,128)(2,1)S(1)}, u32[]{:S(2)}, u32[]{:S(2)}) %collective-permute-start.10) | collective-permute-done | bytes 262176 | tf_op jit(solution)/shard_map/ppermute | solution.py:169
  102.2 5.6 %collective-permute-done.11.refs_12_ = bf16[8,16,1024]{2,1,0:T(8,128)(2,1)S(1)} collective-permute-done((bf16[8,16,1024]{2,1,0:T(8,128)(2,1)S(1)}, bf16[8,16,1024]{2,1,0:T(8,128)(2,1)S(1)}, u32[]{:S(2)}, u32[]{:S(2)}) %collective-permute-start.11) | collective-permute-done | bytes 262176 | tf_op jit(solution)/shard_map/ppermute | solution.py:169
  107.8 5.7 %collective-permute-done.12.refs_13_ = bf16[8,16,1024]{2,1,0:T(8,128)(2,1)S(1)} collective-permute-done((bf16[8,16,1024]{2,1,0:T(8,128)(2,1)S(1)}, bf16[8,16,1024]{2,1,0:T(8,128)(2,1)S(1)}, u32[]{:S(2)}, u32[]{:S(2)}) %collective-permute-start.12) | collective-permute-done | bytes 262176 | tf_op jit(solution)/shard_map/ppermute | solution.py:169
  113.5 6.3 %collective-permute-done.13.refs_14_ = bf16[8,16,1024]{2,1,0:T(8,128)(2,1)S(1)} collective-permute-done((bf16[8,16,1024]{2,1,0:T(8,128)(2,1)S(1)}, bf16[8,16,1024]{2,1,0:T(8,128)(2,1)S(1)}, u32[]{:S(2)}, u32[]{:S(2)}) %collective-permute-start.13) | collective-permute-done | bytes 262176 | tf_op jit(solution)/shard_map/ppermute | solution.py:169
  119.8 5.6 %collective-permute-done.14.refs_15_ = bf16[8,16,1024]{2,1,0:T(8,128)(2,1)S(1)} collective-permute-done((bf16[8,16,1024]{2,1,0:T(8,128)(2,1)S(1)}, bf16[8,16,1024]{2,1,0:T(8,128)(2,1)S(1)}, u32[]{:S(2)}, u32[]{:S(2)}) %collective-permute-start.14) | collective-permute-done | bytes 262176 | tf_op jit(solution)/shard_map/ppermute | solution.py:169
  125.4 5.0 %shard_map.60 = (f32[8,2,128,128]{3,2,1,0:T(8,128)}, f32[8,1024]{1,0:T(8,128)}) custom-call(bf16[8,16,1024]{2,1,0:T(8,128)(2,1)S(1)} %get-tuple-element.20.refs_0_, bf16[8,16,1024]{2,1,0:T(8,128)(2,1)S(1)} %collective-permute-done.refs_1_, bf16[8,16,1024]{2,1,0:T(8,128)(2,1)S(1)} %collective-permute-done.1.refs_2_, ...), custom_call_target="tpu_custom_call" | custom-call | flops 1073741824 | bytes 4194304 | tf_op jit(solution)/shard_map/pallas_call | solution.py:141
  (6 shorter events, 0.0 us)
Async XLA Ops:
  0.6 0.9 copy-start
  1.5 0.7 copy-start.1
  2.2 0.7 copy-start.2
  17.5 4.3 %collective-permute-start = (bf16[8,16,1024]{2,1,0:T(8,128)(2,1)S(1)}, bf16[8,16,1024]{2,1,0:T(8,128)(2,1)S(1)}, u32[]{:S(2)}, u32[]{:S(2)}) collective-permute-start(bf16[8,16,1024]{2,1,0:T(8,128)(2,1)S(1)} %get-tuple-element.21), channel_id=1, source_target_pairs={{0,1},{1,0},{2,3},{3,2},{4,5},{5,4},{6,7},{7,6},{8,9},{9,8},{10,11... | collective-permute-start | bytes 786440 | tf_op jit(solution)/shard_map/ppermute | solution.py:169
  18.3 7.9 %collective-permute-start.1 = (bf16[8,16,1024]{2,1,0:T(8,128)(2,1)S(1)}, bf16[8,16,1024]{2,1,0:T(8,128)(2,1)S(1)}, u32[]{:S(2)}, u32[]{:S(2)}) collective-permute-start(bf16[8,16,1024]{2,1,0:T(8,128)(2,1)S(1)} %get-tuple-element.22), channel_id=1, source_target_pairs={{0,2},{1,3},{2,0},{3,1},{4,6},{5,7},{6,4},{7,5},{8,10},{9,11},{10,... | collective-permute-start | bytes 786440 | tf_op jit(solution)/shard_map/ppermute | solution.py:169
  19.5 12.7 %collective-permute-start.2 = (bf16[8,16,1024]{2,1,0:T(8,128)(2,1)S(1)}, bf16[8,16,1024]{2,1,0:T(8,128)(2,1)S(1)}, u32[]{:S(2)}, u32[]{:S(2)}) collective-permute-start(bf16[8,16,1024]{2,1,0:T(8,128)(2,1)S(1)} %get-tuple-element.23), channel_id=1, source_target_pairs={{0,3},{1,2},{2,1},{3,0},{4,7},{5,6},{6,5},{7,4},{8,11},{9,10},{10,... | collective-permute-start | bytes 786440 | tf_op jit(solution)/shard_map/ppermute | solution.py:169
  20.0 14.6 %collective-permute-start.3 = (bf16[8,16,1024]{2,1,0:T(8,128)(2,1)S(1)}, bf16[8,16,1024]{2,1,0:T(8,128)(2,1)S(1)}, u32[]{:S(2)}, u32[]{:S(2)}) collective-permute-start(bf16[8,16,1024]{2,1,0:T(8,128)(2,1)S(1)} %get-tuple-element.24), channel_id=1, source_target_pairs={{0,4},{1,5},{2,6},{3,7},{4,0},{5,1},{6,2},{7,3},{8,12},{9,13},{10,... | collective-permute-start | bytes 786440 | tf_op jit(solution)/shard_map/ppermute | solution.py:169
  20.0 14.7 %collective-permute-start.4 = (bf16[8,16,1024]{2,1,0:T(8,128)(2,1)S(1)}, bf16[8,16,1024]{2,1,0:T(8,128)(2,1)S(1)}, u32[]{:S(2)}, u32[]{:S(2)}) collective-permute-start(bf16[8,16,1024]{2,1,0:T(8,128)(2,1)S(1)} %get-tuple-element.25), channel_id=1, source_target_pairs={{0,5},{1,4},{2,7},{3,6},{4,1},{5,0},{6,3},{7,2},{8,13},{9,12},{10,... | collective-permute-start | bytes 786440 | tf_op jit(solution)/shard_map/ppermute | solution.py:169
  21.8 26.5 %collective-permute-start.5 = (bf16[8,16,1024]{2,1,0:T(8,128)(2,1)S(1)}, bf16[8,16,1024]{2,1,0:T(8,128)(2,1)S(1)}, u32[]{:S(2)}, u32[]{:S(2)}) collective-permute-start(bf16[8,16,1024]{2,1,0:T(8,128)(2,1)S(1)} %get-tuple-element.26), channel_id=1, source_target_pairs={{0,6},{1,7},{2,4},{3,5},{4,2},{5,3},{6,0},{7,1},{8,14},{9,15},{10,... | collective-permute-start | bytes 786440 | tf_op jit(solution)/shard_map/ppermute | solution.py:169
  26.1 27.7 %collective-permute-start.6 = (bf16[8,16,1024]{2,1,0:T(8,128)(2,1)S(1)}, bf16[8,16,1024]{2,1,0:T(8,128)(2,1)S(1)}, u32[]{:S(2)}, u32[]{:S(2)}) collective-permute-start(bf16[8,16,1024]{2,1,0:T(8,128)(2,1)S(1)} %get-tuple-element.27), channel_id=1, source_target_pairs={{0,7},{1,6},{2,5},{3,4},{4,3},{5,2},{6,1},{7,0},{8,15},{9,14},{10,... | collective-permute-start | bytes 786440 | tf_op jit(solution)/shard_map/ppermute | solution.py:169
  32.2 21.9 %collective-permute-start.7 = (bf16[8,16,1024]{2,1,0:T(8,128)(2,1)S(1)}, bf16[8,16,1024]{2,1,0:T(8,128)(2,1)S(1)}, u32[]{:S(2)}, u32[]{:S(2)}) collective-permute-start(bf16[8,16,1024]{2,1,0:T(8,128)(2,1)S(1)} %get-tuple-element.28), channel_id=1, source_target_pairs={{0,8},{1,9},{2,10},{3,11},{4,12},{5,13},{6,14},{7,15},{8,0},{9,1},... | collective-permute-start | bytes 786440 | tf_op jit(solution)/shard_map/ppermute | solution.py:169
  34.5 45.2 %collective-permute-start.8 = (bf16[8,16,1024]{2,1,0:T(8,128)(2,1)S(1)}, bf16[8,16,1024]{2,1,0:T(8,128)(2,1)S(1)}, u32[]{:S(2)}, u32[]{:S(2)}) collective-permute-start(bf16[8,16,1024]{2,1,0:T(8,128)(2,1)S(1)} %get-tuple-element.29), channel_id=1, source_target_pairs={{0,9},{1,8},{2,11},{3,10},{4,13},{5,12},{6,15},{7,14},{8,1},{9,0},... | collective-permute-start | bytes 786440 | tf_op jit(solution)/shard_map/ppermute | solution.py:169
  34.7 50.6 %collective-permute-start.9 = (bf16[8,16,1024]{2,1,0:T(8,128)(2,1)S(1)}, bf16[8,16,1024]{2,1,0:T(8,128)(2,1)S(1)}, u32[]{:S(2)}, u32[]{:S(2)}) collective-permute-start(bf16[8,16,1024]{2,1,0:T(8,128)(2,1)S(1)} %get-tuple-element.30), channel_id=1, source_target_pairs={{0,10},{1,11},{2,8},{3,9},{4,14},{5,15},{6,12},{7,13},{8,2},{9,3},... | collective-permute-start | bytes 786440 | tf_op jit(solution)/shard_map/ppermute | solution.py:169
  48.3 53.9 %collective-permute-start.10 = (bf16[8,16,1024]{2,1,0:T(8,128)(2,1)S(1)}, bf16[8,16,1024]{2,1,0:T(8,128)(2,1)S(1)}, u32[]{:S(2)}, u32[]{:S(2)}) collective-permute-start(bf16[8,16,1024]{2,1,0:T(8,128)(2,1)S(1)} %get-tuple-element.31), channel_id=1, source_target_pairs={{0,11},{1,10},{2,9},{3,8},{4,15},{5,14},{6,13},{7,12},{8,3},{9,2},... | collective-permute-start | bytes 786440 | tf_op jit(solution)/shard_map/ppermute | solution.py:169
  53.9 53.9 %collective-permute-start.11 = (bf16[8,16,1024]{2,1,0:T(8,128)(2,1)S(1)}, bf16[8,16,1024]{2,1,0:T(8,128)(2,1)S(1)}, u32[]{:S(2)}, u32[]{:S(2)}) collective-permute-start(bf16[8,16,1024]{2,1,0:T(8,128)(2,1)S(1)} %get-tuple-element.32), channel_id=1, source_target_pairs={{0,12},{1,13},{2,14},{3,15},{4,8},{5,9},{6,10},{7,11},{8,4},{9,5},... | collective-permute-start | bytes 786440 | tf_op jit(solution)/shard_map/ppermute | solution.py:169
  54.1 59.4 %collective-permute-start.12 = (bf16[8,16,1024]{2,1,0:T(8,128)(2,1)S(1)}, bf16[8,16,1024]{2,1,0:T(8,128)(2,1)S(1)}, u32[]{:S(2)}, u32[]{:S(2)}) collective-permute-start(bf16[8,16,1024]{2,1,0:T(8,128)(2,1)S(1)} %get-tuple-element.33), channel_id=1, source_target_pairs={{0,13},{1,12},{2,15},{3,14},{4,9},{5,8},{6,11},{7,10},{8,5},{9,4},... | collective-permute-start | bytes 786440 | tf_op jit(solution)/shard_map/ppermute | solution.py:169
  79.7 40.1 %collective-permute-start.13 = (bf16[8,16,1024]{2,1,0:T(8,128)(2,1)S(1)}, bf16[8,16,1024]{2,1,0:T(8,128)(2,1)S(1)}, u32[]{:S(2)}, u32[]{:S(2)}) collective-permute-start(bf16[8,16,1024]{2,1,0:T(8,128)(2,1)S(1)} %get-tuple-element.34), channel_id=1, source_target_pairs={{0,14},{1,15},{2,12},{3,13},{4,10},{5,11},{6,8},{7,9},{8,6},{9,7},... | collective-permute-start | bytes 786440 | tf_op jit(solution)/shard_map/ppermute | solution.py:169
  85.3 40.1 %collective-permute-start.14 = (bf16[8,16,1024]{2,1,0:T(8,128)(2,1)S(1)}, bf16[8,16,1024]{2,1,0:T(8,128)(2,1)S(1)}, u32[]{:S(2)}, u32[]{:S(2)}) collective-permute-start(bf16[8,16,1024]{2,1,0:T(8,128)(2,1)S(1)} %get-tuple-element.35), channel_id=1, source_target_pairs={{0,15},{1,14},{2,13},{3,12},{4,11},{5,10},{6,9},{7,8},{8,7},{9,6},... | collective-permute-start | bytes 786440 | tf_op jit(solution)/shard_map/ppermute | solution.py:169

commit v2 on v1

--- a/solution.py
+++ b/solution.py
@@ -37,8 +37,8 @@
     return table.astype(np.float32).astype(jnp.bfloat16)
 
 
-def spectra_kernel(tile, in_dev, blocks, owner, frames, window, fourier, *rest):
-    outs, (filtered, spectra) = rest[:blocks], rest[blocks:]
+def spectra_kernel(tile, in_dev, blocks, others, held_back, owner, frames, window, fourier, *rest):
+    outs, (filtered, spectra) = rest[held_back:-2], rest[-2:]
     per_block = CHANS // blocks
     me = lax.axis_index(AXES)
 
@@ -65,7 +65,7 @@
         for part in range(tile // LANES):
             spectra[part, pl.ds(i * 2 * CHANS, 2 * CHANS), :] = product[:, part * LANES : (part + 1) * LANES]
 
-    for other in range(blocks):
+    for other, out in zip(others, outs):
         base = owner[me ^ other] * per_block
         for channel in range(per_block):
             for part in range(tile // LANES):
@@ -73,16 +73,17 @@
                     spectra[part, pl.ds(base + plane * CHANS + channel, in_dev, stride=2 * CHANS), :]
                     for plane in range(2)
                 ]
-                outs[other][channel, :, part * LANES : (part + 1) * LANES] = jnp.concatenate(
+                out[channel, :, part * LANES : (part + 1) * LANES] = jnp.concatenate(
                     pair, axis=0
                 ).astype(jnp.bfloat16)
 
 
-def make_spectra(frames, owner_block, window, fourier, start, count, blocks, tile):
+def make_spectra(tables, frames, owner_block, start, count, blocks, fresh, whole, kept=(), tile=256):
     in_dev = frames.shape[1]
     per_block = CHANS // blocks
+    rows = 2 * in_dev
     return pl.pallas_call(
-        functools.partial(spectra_kernel, tile, in_dev, blocks),
+        functools.partial(spectra_kernel, tile, in_dev, blocks, fresh + whole, len(kept)),
         grid_spec=pltpu.PrefetchScalarGridSpec(
             num_scalar_prefetch=1,
             grid=(count // tile,),
@@ -93,28 +94,30 @@
                 ),
                 pl.BlockSpec((TAPS, LENGTH), lambda step, owner: (0, 0)),
                 pl.BlockSpec((LENGTH, LENGTH), lambda step, owner: (0, 0)),
-            ],
-            out_specs=[
-                pl.BlockSpec((per_block, 2 * in_dev, tile), lambda step, owner: (0, 0, step))
-                for _ in range(blocks)
+            ]
+            + [pl.BlockSpec(memory_space=pl.ANY) for _ in kept],
+            out_specs=[pl.BlockSpec((per_block, rows, tile), lambda step, owner: (0, 0, step)) for _ in fresh]
+            + [
+                pl.BlockSpec((per_block, rows, tile), lambda step, owner: (0, 0, start // tile + step))
+                for _ in whole
             ],
             scratch_shapes=[
                 pltpu.VMEM((LENGTH // LANES, tile * in_dev, LANES), jnp.float32),
                 pltpu.VMEM((tile // LANES, in_dev * 2 * CHANS, LANES), jnp.float32),
             ],
         ),
-        out_shape=[
-            jax.ShapeDtypeStruct((per_block, 2 * in_dev, count), jnp.bfloat16) for _ in range(blocks)
-        ],
+        out_shape=[jax.ShapeDtypeStruct((per_block, rows, count), jnp.bfloat16) for _ in fresh]
+        + [jax.ShapeDtypeStruct((per_block, rows, SPECTRA), jnp.bfloat16) for _ in whole],
+        input_output_aliases={4 + index: len(fresh) + index for index in range(len(kept))},
         compiler_params=pltpu.CompilerParams(vmem_limit_bytes=VMEM),
         cost_estimate=pl.CostEstimate(
             flops=2 * count * in_dev * LENGTH * LENGTH, bytes_accessed=4 * count * in_dev * LENGTH, transcendentals=0
         ),
-    )(owner_block, frames, window, fourier)
-
-
-def correlate_kernel(in_dev, blocks, scale, *refs):
-    parts, (visibility, beam, planes) = refs[:blocks], refs[blocks:]
+    )(owner_block, frames, *tables, *kept)
+
+
+def correlate_kernel(in_dev, blocks, scale, held_back, *refs):
+    parts, (visibility, beam, planes) = refs[:blocks], refs[-3:]
     count = parts[0].shape[2]
     inputs = in_dev * blocks
     me = lax.axis_index(AXES)
@@ -130,46 +133,85 @@
     beam[pl.ds(channel, 1), :] = jnp.sum(power, axis=0, keepdims=True) * (1.0 / inputs)
     both = planes[...].reshape(2 * inputs, count).astype(jnp.bfloat16)
     gram = lax.dot_general(both, both, (((1,), (1,)), ((), ())), preferred_element_type=jnp.float32)
-    visibility[0, 0] = (gram[:inputs, :inputs] + gram[inputs:, inputs:]) * scale
-    visibility[0, 1] = (gram[inputs:, :inputs] - gram[:inputs, inputs:]) * scale
-
-
-def correlate(parts, blocks):
-    per_block, rows, count = parts[0].shape
+    straight = (gram[:inputs, :inputs] + gram[inputs:, inputs:]) * scale
+    crossed = (gram[inputs:, :inputs] - gram[:inputs, inputs:]) * scale
+    if held_back:
+        before = refs[blocks]
+        straight = before[0, 0] + straight
+        crossed = before[0, 1] + crossed
+    visibility[0, 0] = straight
+    visibility[0, 1] = crossed
+
+
+def correlate(parts, start, count, blocks, kept=()):
+    per_block, rows, _ = parts[0].shape
     in_dev = rows // 2
     inputs = in_dev * blocks
+
+    def part_spec(part):
+        place = start // count if part.shape[2] == SPECTRA else 0
+        return pl.BlockSpec((1, rows, count), lambda channel: (channel, 0, place))
+
+    visibility_spec = pl.BlockSpec((1, 2, inputs, inputs), lambda channel: (channel, 0, 0, 0))
     return pl.pallas_call(
-        functools.partial(correlate_kernel, in_dev, blocks, 1.0 / SPECTRA),
+        functools.partial(correlate_kernel, in_dev, blocks, 1.0 / SPECTRA, len(kept)),
         grid=(per_block,),
-        in_specs=[pl.BlockSpec((1, rows, count), lambda channel: (channel, 0, 0)) for _ in range(blocks)],
-        out_specs=[
-            pl.BlockSpec((1, 2, inputs, inputs), lambda channel: (channel, 0, 0, 0)),
-            pl.BlockSpec((per_block, count), lambda channel: (0, 0)),
-        ],
+        in_specs=[part_spec(part) for part in parts]
+        + ([visibility_spec, pl.BlockSpec(memory_space=pl.ANY)] if kept else []),
+        out_specs=[visibility_spec, pl.BlockSpec((per_block, count), lambda channel: (0, start // count))],
         scratch_shapes=[pltpu.VMEM((2, blocks, in_dev, count), jnp.float32)],
         out_shape=[
             jax.ShapeDtypeStruct((per_block, 2, inputs, inputs), jnp.float32),
-            jax.ShapeDtypeStruct((per_block, count), jnp.float32),
+            jax.ShapeDtypeStruct((per_block, SPECTRA), jnp.float32),
         ],
+        input_output_aliases={blocks: 0, blocks + 1: 1} if kept else {},
         compiler_params=pltpu.CompilerParams(vmem_limit_bytes=VMEM),
         cost_estimate=pl.CostEstimate(
             flops=8 * per_block * inputs * inputs * count, bytes_accessed=4 * per_block * inputs * count, transcendentals=0
         ),
-    )(*parts)
+    )(*parts, *kept)
+
+
+FIRST, MIDDLE, LAST = (768, 256), (0, 512), (512, 256)
+IN_FLIGHT = 5
 
 
 def body(voltages, owner_block):
     in_dev = voltages.shape[0]
     blocks = lax.axis_size(AXES)
-    window = jnp.asarray(window_table())
-    fourier = jnp.asarray(dft_table())
+    tables = (jnp.asarray(window_table()), jnp.asarray(dft_table()))
     frames = voltages.reshape(in_dev, SPECTRA + TAPS - 1, LENGTH).transpose(1, 0, 2)
-    own = make_spectra(frames, owner_block, window, fourier, 0, SPECTRA, blocks, 256)
-    parts = [own[0]] + [
-        lax.ppermute(own[other], AXES, [(source, source ^ other) for source in range(blocks)])
-        for other in range(1, blocks)
-    ]
-    visibility, beam = correlate(parts, blocks)
+    far, near = tuple(range(blocks // 2, blocks)), tuple(range(blocks // 2))
+    spectra = functools.partial(make_spectra, tables, frames, owner_block, blocks=blocks)
+
+    sent, taken = [], {}
+
+    def send(name, other, block):
+        if len(sent) >= IN_FLIGHT:
+            block, taken[sent[-IN_FLIGHT]] = lax.optimization_barrier((block, taken[sent[-IN_FLIGHT]]))
+        taken[name, other] = lax.ppermute(block, AXES, [(s, s ^ other) for s in range(blocks)])
+        sent.append((name, other))
+
+    made = spectra(*FIRST, fresh=far, whole=near)
+    first, kept = made[: len(far)], made[len(far) :]
+    for other, block in zip(far, first):
+        send("first", other, block)
+    made = spectra(*MIDDLE, fresh=far, whole=near, kept=kept)
+    middle, kept = made[: len(far)], made[len(far) :]
+    made = spectra(*LAST, fresh=far, whole=near, kept=kept)
+    last, kept = made[: len(far)], made[len(far) :]
+    taken["near", 0] = kept[0]
+    for index, other in enumerate(far):
+        send("middle", other, middle[index])
+        if index + 1 < len(near):
+            send("near", near[index + 1], kept[index + 1])
+    for other, block in zip(far, last):
+        send("last", other, block)
+    result = ()
+    for name, chunk in (("first", FIRST), ("middle", MIDDLE), ("last", LAST)):
+        parts = [taken["near", other] for other in near] + [taken[name, other] for other in far]
+        result = correlate(parts, *chunk, blocks, result)
+    visibility, beam = result
     return (visibility[None], beam[None])
 
 

time: 132 us -> 136 us (1.030)
  waiting for transfers between devices: 80.9 us -> 25.6 us
  starting transfers between devices: 27 us -> 71 us
  Pallas kernels: 19.6 us -> 34.8 us
    ppermute x15 -> x31, waiting for transfers between devices: 80.9 us -> 25.6 us  [send(): lax.ppermute(block, AXES, [(s, s ^ other) for s in range(blocks)])]
    ppermute x15 -> x31, starting transfers between devices: 27 us -> 71 us  [send(): lax.ppermute(block, AXES, [(s, s ^ other) for s in range(blocks)])]
    pallas_call x1 -> x3, Pallas kernels: 5 us -> 17 us  [correlate(): pl.pallas_call(functools.partial(correlate_kernel, in_dev, blocks, 1.0 /...]
    pallas_call x1 -> x3, Pallas kernels: 14.6 us -> 17.8 us  [make_spectra(): pl.pallas_call(functools.partial(spectra_kernel, tile, in_dev, blocks, fr...]
  transfers between devices with their start and end apart: 15 -> 31, of which waited for: 11 -> 7; matrix products, arithmetic and copies ran while one was open for 0% -> 0% of each run, Pallas kernels for 0% -> 18%
where the time goes in v2:
time: 136 us; the launch traced here: 134 us
  starting transfers between devices  71 us (52%)
  Pallas kernels  34.8 us (26%)
  waiting for transfers between devices  25.6 us (19%)
  local copies, waits for them, and re-layouts  2.25 us (2%)
    ppermute x31, starting transfers between devices, send(): lax.ppermute(block, AXES, [(s, s ^ other) for s in range(blocks)])  71 us
    ppermute x31, waiting for transfers between devices, send(): lax.ppermute(block, AXES, [(s, s ^ other) for s in range(blocks)])  25.6 us
    pallas_call x3, Pallas kernels, make_spectra(): pl.pallas_call(functools.partial(spectra_kernel, tile, in_dev, blocks, fr...  17.8 us
    pallas_call x3, Pallas kernels, correlate(): pl.pallas_call(functools.partial(correlate_kernel, in_dev, blocks, 1.0 /...  17 us
  transfers between devices with their start and end apart: 31, of which 7 were waited for; matrix products, arithmetic and copies ran while one was open for 0% of the time, Pallas kernels for 18%

profile of v2, /device:TPU:9, one launch (start us, length us, event | category | flops | bytes accessed | tf_op | source)
XLA Modules:
  0.0 134.4 jit_solution(14043661230470649029)
XLA Ops:
  2.9 4.8 %shard_map.59 = (bf16[8,16,256]{2,1,0:T(8,128)(2,1)S(1)}, bf16[8,16,256]{2,1,0:T(8,128)(2,1)S(1)}, bf16[8,16,256]{2,1,0:T(8,128)(2,1)S(1)}, bf16[8,16,256]{2,1,0...) custom-call(s32[16]{0:T(128)S(1)} %copy-done.2, ...), custom_call_target="tpu_custom_call" | custom-call | flops 268435456 | bytes 2097152 | tf_op jit(solution)/shard_map/pallas_call | solution.py:85
  7.7 2.9 %collective-permute-start.2 = (bf16[8,16,256]{2,1,0:T(8,128)(2,1)S(1)}, bf16[8,16,256]{2,1,0:T(8,128)(2,1)S(1)}, u32[]{:S(2)}, u32[]{:S(2)}) collective-permute-start(bf16[8,16,256]{2,1,0:T(8,128)(2,1)S(1)} %get-tuple-element.133), channel_id=1, source_target_pairs={{0,9},{1,8},{2,11},{3,10},{4,13},{5,12},{6,15},{7,14},{8,1},{9,0},... | collective-permute-start | bytes 196616 | tf_op jit(solution)/shard_map/ppermute | solution.py:192
  10.7 2.3 %collective-permute-start.8 = (bf16[8,16,256]{2,1,0:T(8,128)(2,1)S(1)}, bf16[8,16,256]{2,1,0:T(8,128)(2,1)S(1)}, u32[]{:S(2)}, u32[]{:S(2)}) collective-permute-start(bf16[8,16,256]{2,1,0:T(8,128)(2,1)S(1)} %get-tuple-element.148), channel_id=1, source_target_pairs={{0,8},{1,9},{2,10},{3,11},{4,12},{5,13},{6,14},{7,15},{8,0},{9,1},... | collective-permute-start | bytes 196616 | tf_op jit(solution)/shard_map/ppermute | solution.py:192
  12.9 8.2 %shard_map.60 = (bf16[8,16,512]{2,1,0:T(8,128)(2,1)S(1)}, bf16[8,16,512]{2,1,0:T(8,128)(2,1)S(1)}, bf16[8,16,512]{2,1,0:T(8,128)(2,1)S(1)}, bf16[8,16,512]{2,1,0...) custom-call(s32[16]{0:T(128)S(1)} %copy-done.2, ...), custom_call_target="tpu_custom_call", output_to_operand_aliasing={{8}: (4, {}), {9}: (5, {}), {10}: (6, {}), {11}: (7, {}), {... | custom-call | flops 536870912 | bytes 4194304 | tf_op jit(solution)/shard_map/pallas_call | solution.py:85
  22.3 4.8 %shard_map.61 = (bf16[8,16,256]{2,1,0:T(8,128)(2,1)S(1)}, bf16[8,16,256]{2,1,0:T(8,128)(2,1)S(1)}, bf16[8,16,256]{2,1,0:T(8,128)(2,1)S(1)}, bf16[8,16,256]{2,1,0...) custom-call(s32[16]{0:T(128)S(1)} %copy-done.2, ...), custom_call_target="tpu_custom_call", output_to_operand_aliasing={{8}: (4, {}), {9}: (5, {}), {10}: (6, {}), {11}: (7, {}), {... | custom-call | flops 268435456 | bytes 2097152 | tf_op jit(solution)/shard_map/pallas_call | solution.py:85
  28.2 2.0 %collective-permute-start.12 = (bf16[8,16,256]{2,1,0:T(8,128)(2,1)S(1)}, bf16[8,16,256]{2,1,0:T(8,128)(2,1)S(1)}, u32[]{:S(2)}, u32[]{:S(2)}) collective-permute-start(bf16[8,16,256]{2,1,0:T(8,128)(2,1)S(1)} %get-tuple-element.157), channel_id=1, source_target_pairs={{0,10},{1,11},{2,8},{3,9},{4,14},{5,15},{6,12},{7,13},{8,2},{9,3},... | collective-permute-start | bytes 196616 | tf_op jit(solution)/shard_map/ppermute | solution.py:192
  30.1 1.5 %collective-permute-start.5 = (bf16[8,16,256]{2,1,0:T(8,128)(2,1)S(1)}, bf16[8,16,256]{2,1,0:T(8,128)(2,1)S(1)}, u32[]{:S(2)}, u32[]{:S(2)}) collective-permute-start(bf16[8,16,256]{2,1,0:T(8,128)(2,1)S(1)} %get-tuple-element.140), channel_id=1, source_target_pairs={{0,11},{1,10},{2,9},{3,8},{4,15},{5,14},{6,13},{7,12},{8,3},{9,2},... | collective-permute-start | bytes 196616 | tf_op jit(solution)/shard_map/ppermute | solution.py:192
  32.9 1.6 %collective-permute-done.12.refs_10_ = bf16[8,16,256]{2,1,0:T(8,128)(2,1)S(1)} collective-permute-done((bf16[8,16,256]{2,1,0:T(8,128)(2,1)S(1)}, bf16[8,16,256]{2,1,0:T(8,128)(2,1)S(1)}, u32[]{:S(2)}, u32[]{:S(2)}) %collective-permute-start.12) | collective-permute-done | bytes 65568 | tf_op jit(solution)/shard_map/ppermute | solution.py:192
  34.5 3.0 %collective-permute-start.13 = (bf16[8,16,256]{2,1,0:T(8,128)(2,1)S(1)}, bf16[8,16,256]{2,1,0:T(8,128)(2,1)S(1)}, u32[]{:S(2)}, u32[]{:S(2)}) collective-permute-start(bf16[8,16,256]{2,1,0:T(8,128)(2,1)S(1)} %get-tuple-element.158), channel_id=1, source_target_pairs={{0,15},{1,14},{2,13},{3,12},{4,11},{5,10},{6,9},{7,8},{8,7},{9,6},... | collective-permute-start | bytes 196616 | tf_op jit(solution)/shard_map/ppermute | solution.py:192
  37.6 4.0 %collective-permute-start.6 = (bf16[8,16,512]{2,1,0:T(8,128)(2,1)S(1)}, bf16[8,16,512]{2,1,0:T(8,128)(2,1)S(1)}, u32[]{:S(2)}, u32[]{:S(2)}) collective-permute-start(bf16[8,16,512]{2,1,0:T(8,128)(2,1)S(1)} %get-tuple-element.141), channel_id=1, source_target_pairs={{0,8},{1,9},{2,10},{3,11},{4,12},{5,13},{6,14},{7,15},{8,0},{9,1},... | collective-permute-start | bytes 393224 | tf_op jit(solution)/shard_map/ppermute | solution.py:192
  42.4 3.5 %collective-permute-start.14 = (bf16[8,16,512]{2,1,0:T(8,128)(2,1)S(1)}, bf16[8,16,512]{2,1,0:T(8,128)(2,1)S(1)}, u32[]{:S(2)}, u32[]{:S(2)}) collective-permute-start(bf16[8,16,512]{2,1,0:T(8,128)(2,1)S(1)} %get-tuple-element.159), channel_id=1, source_target_pairs={{0,10},{1,11},{2,8},{3,9},{4,14},{5,15},{6,12},{7,13},{8,2},{9,3},... | collective-permute-start | bytes 393224 | tf_op jit(solution)/shard_map/ppermute | solution.py:192
  45.9 7.2 %collective-permute-done.6.refs_8_ = bf16[8,16,512]{2,1,0:T(8,128)(2,1)S(1)} collective-permute-done((bf16[8,16,512]{2,1,0:T(8,128)(2,1)S(1)}, bf16[8,16,512]{2,1,0:T(8,128)(2,1)S(1)}, u32[]{:S(2)}, u32[]{:S(2)}) %collective-permute-start.6) | collective-permute-done | bytes 131104 | tf_op jit(solution)/shard_map/ppermute | solution.py:192
  53.1 3.0 %collective-permute-start.7 = (bf16[8,16,1024]{2,1,0:T(8,128)(2,1)S(1)}, bf16[8,16,1024]{2,1,0:T(8,128)(2,1)S(1)}, u32[]{:S(2)}, u32[]{:S(2)}) collective-permute-start(bf16[8,16,1024]{2,1,0:T(8,128)(2,1)S(1)} %get-tuple-element.142), channel_id=1, source_target_pairs={{0,3},{1,2},{2,1},{3,0},{4,7},{5,6},{6,5},{7,4},{8,11},{9,10},{10,... | collective-permute-start | bytes 786440 | tf_op jit(solution)/shard_map/ppermute | solution.py:192
  56.1 2.0 %collective-permute-start.11 = (bf16[8,16,1024]{2,1,0:T(8,128)(2,1)S(1)}, bf16[8,16,1024]{2,1,0:T(8,128)(2,1)S(1)}, u32[]{:S(2)}, u32[]{:S(2)}) collective-permute-start(bf16[8,16,1024]{2,1,0:T(8,128)(2,1)S(1)} %get-tuple-element.151), channel_id=1, source_target_pairs={{0,4},{1,5},{2,6},{3,7},{4,0},{5,1},{6,2},{7,3},{8,12},{9,13},{10,... | collective-permute-start | bytes 786440 | tf_op jit(solution)/shard_map/ppermute | solution.py:192
  58.2 3.6 %collective-permute-start.16 = (bf16[8,16,512]{2,1,0:T(8,128)(2,1)S(1)}, bf16[8,16,512]{2,1,0:T(8,128)(2,1)S(1)}, u32[]{:S(2)}, u32[]{:S(2)}) collective-permute-start(bf16[8,16,512]{2,1,0:T(8,128)(2,1)S(1)} %get-tuple-element.164), channel_id=1, source_target_pairs={{0,11},{1,10},{2,9},{3,8},{4,15},{5,14},{6,13},{7,12},{8,3},{9,2},... | collective-permute-start | bytes 393224 | tf_op jit(solution)/shard_map/ppermute | solution.py:192
  61.8 1.4 %collective-permute-start.15 = (bf16[8,16,1024]{2,1,0:T(8,128)(2,1)S(1)}, bf16[8,16,1024]{2,1,0:T(8,128)(2,1)S(1)}, u32[]{:S(2)}, u32[]{:S(2)}) collective-permute-start(bf16[8,16,1024]{2,1,0:T(8,128)(2,1)S(1)} %get-tuple-element.160), channel_id=1, source_target_pairs={{0,5},{1,4},{2,7},{3,6},{4,1},{5,0},{6,3},{7,2},{8,13},{9,12},{10,... | collective-permute-start | bytes 786440 | tf_op jit(solution)/shard_map/ppermute | solution.py:192
  63.2 1.7 %collective-permute-start.18 = (bf16[8,16,512]{2,1,0:T(8,128)(2,1)S(1)}, bf16[8,16,512]{2,1,0:T(8,128)(2,1)S(1)}, u32[]{:S(2)}, u32[]{:S(2)}) collective-permute-start(bf16[8,16,512]{2,1,0:T(8,128)(2,1)S(1)} %get-tuple-element.169), channel_id=1, source_target_pairs={{0,12},{1,13},{2,14},{3,15},{4,8},{5,9},{6,10},{7,11},{8,4},{9,5},... | collective-permute-start | bytes 393224 | tf_op jit(solution)/shard_map/ppermute | solution.py:192
  65.0 6.5 %collective-permute-done.16.refs_11_ = bf16[8,16,512]{2,1,0:T(8,128)(2,1)S(1)} collective-permute-done((bf16[8,16,512]{2,1,0:T(8,128)(2,1)S(1)}, bf16[8,16,512]{2,1,0:T(8,128)(2,1)S(1)}, u32[]{:S(2)}, u32[]{:S(2)}) %collective-permute-start.16) | collective-permute-done | bytes 131104 | tf_op jit(solution)/shard_map/ppermute | solution.py:192
  71.5 10.2 %collective-permute-start.19 = (bf16[8,16,1024]{2,1,0:T(8,128)(2,1)S(1)}, bf16[8,16,1024]{2,1,0:T(8,128)(2,1)S(1)}, u32[]{:S(2)}, u32[]{:S(2)}) collective-permute-start(bf16[8,16,1024]{2,1,0:T(8,128)(2,1)S(1)} %get-tuple-element.170), channel_id=1, source_target_pairs={{0,7},{1,6},{2,5},{3,4},{4,3},{5,2},{6,1},{7,0},{8,15},{9,14},{10,... | collective-permute-start | bytes 786440 | tf_op jit(solution)/shard_map/ppermute | solution.py:192
  81.7 2.7 %collective-permute-start.26 = (bf16[8,16,512]{2,1,0:T(8,128)(2,1)S(1)}, bf16[8,16,512]{2,1,0:T(8,128)(2,1)S(1)}, u32[]{:S(2)}, u32[]{:S(2)}) collective-permute-start(bf16[8,16,512]{2,1,0:T(8,128)(2,1)S(1)} %get-tuple-element.187), channel_id=1, source_target_pairs={{0,15},{1,14},{2,13},{3,12},{4,11},{5,10},{6,9},{7,8},{8,7},{9,6},... | collective-permute-start | bytes 393224 | tf_op jit(solution)/shard_map/ppermute | solution.py:192
  84.4 3.2 %collective-permute-done.20.refs_13_ = bf16[8,16,512]{2,1,0:T(8,128)(2,1)S(1)} collective-permute-done((bf16[8,16,512]{2,1,0:T(8,128)(2,1)S(1)}, bf16[8,16,512]{2,1,0:T(8,128)(2,1)S(1)}, u32[]{:S(2)}, u32[]{:S(2)}) %collective-permute-start.20) | collective-permute-done | bytes 131104 | tf_op jit(solution)/shard_map/ppermute | solution.py:192
  87.6 6.0 %collective-permute-start.21 = (bf16[8,16,256]{2,1,0:T(8,128)(2,1)S(1)}, bf16[8,16,256]{2,1,0:T(8,128)(2,1)S(1)}, u32[]{:S(2)}, u32[]{:S(2)}) collective-permute-start(bf16[8,16,256]{2,1,0:T(8,128)(2,1)S(1)} %get-tuple-element.175), channel_id=1, source_target_pairs={{0,8},{1,9},{2,10},{3,11},{4,12},{5,13},{6,14},{7,15},{8,0},{9,1},... | collective-permute-start | bytes 196616 | tf_op jit(solution)/shard_map/ppermute | solution.py:192
  93.6 4.3 %collective-permute-done.23.refs_14_ = bf16[8,16,512]{2,1,0:T(8,128)(2,1)S(1)} collective-permute-done((bf16[8,16,512]{2,1,0:T(8,128)(2,1)S(1)}, bf16[8,16,512]{2,1,0:T(8,128)(2,1)S(1)}, u32[]{:S(2)}, u32[]{:S(2)}) %collective-permute-start.23) | collective-permute-done | bytes 131104 | tf_op jit(solution)/shard_map/ppermute | solution.py:192
  97.9 1.2 collective-permute-start.24
  99.2 5.4 %collective-permute-start.22 = (bf16[8,16,256]{2,1,0:T(8,128)(2,1)S(1)}, bf16[8,16,256]{2,1,0:T(8,128)(2,1)S(1)}, u32[]{:S(2)}, u32[]{:S(2)}) collective-permute-start(bf16[8,16,256]{2,1,0:T(8,128)(2,1)S(1)} %get-tuple-element.178), channel_id=1, source_target_pairs={{0,9},{1,8},{2,11},{3,10},{4,13},{5,12},{6,15},{7,14},{8,1},{9,0},... | collective-permute-start | bytes 196616 | tf_op jit(solution)/shard_map/ppermute | solution.py:192
  105.4 2.3 %collective-permute-done.24.refs_10_ = bf16[8,16,256]{2,1,0:T(8,128)(2,1)S(1)} collective-permute-done((bf16[8,16,256]{2,1,0:T(8,128)(2,1)S(1)}, bf16[8,16,256]{2,1,0:T(8,128)(2,1)S(1)}, u32[]{:S(2)}, u32[]{:S(2)}) %collective-permute-start.24) | collective-permute-done | bytes 65568 | tf_op jit(solution)/shard_map/ppermute | solution.py:192
  107.8 3.5 %collective-permute-start.30 = (bf16[8,16,256]{2,1,0:T(8,128)(2,1)S(1)}, bf16[8,16,256]{2,1,0:T(8,128)(2,1)S(1)}, u32[]{:S(2)}, u32[]{:S(2)}) collective-permute-start(bf16[8,16,256]{2,1,0:T(8,128)(2,1)S(1)} %get-tuple-element.191), channel_id=1, source_target_pairs={{0,15},{1,14},{2,13},{3,12},{4,11},{5,10},{6,9},{7,8},{8,7},{9,6},... | collective-permute-start | bytes 196616 | tf_op jit(solution)/shard_map/ppermute | solution.py:192
  111.2 4.9 %collective-permute-start.25 = (bf16[8,16,256]{2,1,0:T(8,128)(2,1)S(1)}, bf16[8,16,256]{2,1,0:T(8,128)(2,1)S(1)}, u32[]{:S(2)}, u32[]{:S(2)}) collective-permute-start(bf16[8,16,256]{2,1,0:T(8,128)(2,1)S(1)} %get-tuple-element.185), channel_id=1, source_target_pairs={{0,11},{1,10},{2,9},{3,8},{4,15},{5,14},{6,13},{7,12},{8,3},{9,2},... | collective-permute-start | bytes 196616 | tf_op jit(solution)/shard_map/ppermute | solution.py:192
  116.1 1.3 collective-permute-start.29
  117.4 4.2 %shard_map.62 = (f32[8,2,128,128]{3,2,1,0:T(8,128)}, f32[8,1024]{1,0:T(8,128)}) custom-call(bf16[8,16,1024]{2,1,0:T(8,128)(2,1)S(1)} %get-tuple-element.124.refs_0_, bf16[8,16,1024]{2,1,0:T(8,128)(2,1)S(1)} %collective-permute-done.1.refs_1_, bf16[8,16,1024]{2,1,0:T(8,128)(2,1)S(1)} %collective-permute-done.4.refs_2_, ...), custom_call_target="tpu_custom_call" | custom-call | flops 268435456 | bytes 1048576 | tf_op jit(solution)/shard_map/pallas_call | solution.py:156
  121.6 6.5 %shard_map.63 = (f32[8,2,128,128]{3,2,1,0:T(8,128)}, f32[8,1024]{1,0:T(8,128)}) custom-call(bf16[8,16,1024]{2,1,0:T(8,128)(2,1)S(1)} %get-tuple-element.124.refs_0_, bf16[8,16,1024]{2,1,0:T(8,128)(2,1)S(1)} %collective-permute-done.1.refs_1_, ...), custom_call_target="tpu_custom_call", output_to_operand_aliasing={{0}: (16, {}), {1}: (17, {})} | custom-call | flops 536870912 | bytes 2097152 | tf_op jit(solution)/shard_map/pallas_call | solution.py:156
  128.1 6.3 %shard_map.64 = (f32[8,2,128,128]{3,2,1,0:T(8,128)}, f32[8,1024]{1,0:T(8,128)}) custom-call(bf16[8,16,1024]{2,1,0:T(8,128)(2,1)S(1)} %get-tuple-element.124.refs_0_, bf16[8,16,1024]{2,1,0:T(8,128)(2,1)S(1)} %collective-permute-done.1.refs_1_, ...), custom_call_target="tpu_custom_call", output_to_operand_aliasing={{0}: (16, {}), {1}: (17, {})} | custom-call | flops 268435456 | bytes 1048576 | tf_op jit(solution)/shard_map/pallas_call | solution.py:156
  (42 shorter events, 7.6 us)
Async XLA Ops:
  0.6 0.9 copy-start
  7.7 13.4 %collective-permute-start.2 = (bf16[8,16,256]{2,1,0:T(8,128)(2,1)S(1)}, bf16[8,16,256]{2,1,0:T(8,128)(2,1)S(1)}, u32[]{:S(2)}, u32[]{:S(2)}) collective-permute-start(bf16[8,16,256]{2,1,0:T(8,128)(2,1)S(1)} %get-tuple-element.133), channel_id=1, source_target_pairs={{0,9},{1,8},{2,11},{3,10},{4,13},{5,12},{6,15},{7,14},{8,1},{9,0},... | collective-permute-start | bytes 196616 | tf_op jit(solution)/shard_map/ppermute | solution.py:192
  10.6 16.5 %collective-permute-start = (bf16[8,16,256]{2,1,0:T(8,128)(2,1)S(1)}, bf16[8,16,256]{2,1,0:T(8,128)(2,1)S(1)}, u32[]{:S(2)}, u32[]{:S(2)}) collective-permute-start(bf16[8,16,256]{2,1,0:T(8,128)(2,1)S(1)} %get-tuple-element.127), channel_id=1, source_target_pairs={{0,12},{1,13},{2,14},{3,15},{4,8},{5,9},{6,10},{7,11},{8,4},{9,5},... | collective-permute-start | bytes 196616 | tf_op jit(solution)/shard_map/ppermute | solution.py:192
  10.7 21.0 %collective-permute-start.8 = (bf16[8,16,256]{2,1,0:T(8,128)(2,1)S(1)}, bf16[8,16,256]{2,1,0:T(8,128)(2,1)S(1)}, u32[]{:S(2)}, u32[]{:S(2)}) collective-permute-start(bf16[8,16,256]{2,1,0:T(8,128)(2,1)S(1)} %get-tuple-element.148), channel_id=1, source_target_pairs={{0,8},{1,9},{2,10},{3,11},{4,12},{5,13},{6,14},{7,15},{8,0},{9,1},... | collective-permute-start | bytes 196616 | tf_op jit(solution)/shard_map/ppermute | solution.py:192
  21.1 11.6 %collective-permute-start.3 = (bf16[8,16,256]{2,1,0:T(8,128)(2,1)S(1)}, bf16[8,16,256]{2,1,0:T(8,128)(2,1)S(1)}, u32[]{:S(2)}, u32[]{:S(2)}) collective-permute-start(bf16[8,16,256]{2,1,0:T(8,128)(2,1)S(1)} %get-tuple-element.134), channel_id=1, source_target_pairs={{0,14},{1,15},{2,12},{3,13},{4,10},{5,11},{6,8},{7,9},{8,6},{9,7},... | collective-permute-start | bytes 196616 | tf_op jit(solution)/shard_map/ppermute | solution.py:192
  27.1 31.0 %collective-permute-start.1 = (bf16[8,16,1024]{2,1,0:T(8,128)(2,1)S(1)}, bf16[8,16,1024]{2,1,0:T(8,128)(2,1)S(1)}, u32[]{:S(2)}, u32[]{:S(2)}) collective-permute-start(bf16[8,16,1024]{2,1,0:T(8,128)(2,1)S(1)} %get-tuple-element.128), channel_id=1, source_target_pairs={{0,1},{1,0},{2,3},{3,2},{4,5},{5,4},{6,7},{7,6},{8,9},{9,8},{10,11... | collective-permute-start | bytes 786440 | tf_op jit(solution)/shard_map/ppermute | solution.py:192
  28.2 6.4 %collective-permute-start.12 = (bf16[8,16,256]{2,1,0:T(8,128)(2,1)S(1)}, bf16[8,16,256]{2,1,0:T(8,128)(2,1)S(1)}, u32[]{:S(2)}, u32[]{:S(2)}) collective-permute-start(bf16[8,16,256]{2,1,0:T(8,128)(2,1)S(1)} %get-tuple-element.157), channel_id=1, source_target_pairs={{0,10},{1,11},{2,8},{3,9},{4,14},{5,15},{6,12},{7,13},{8,2},{9,3},... | collective-permute-start | bytes 196616 | tf_op jit(solution)/shard_map/ppermute | solution.py:192
  30.1 7.4 %collective-permute-start.5 = (bf16[8,16,256]{2,1,0:T(8,128)(2,1)S(1)}, bf16[8,16,256]{2,1,0:T(8,128)(2,1)S(1)}, u32[]{:S(2)}, u32[]{:S(2)}) collective-permute-start(bf16[8,16,256]{2,1,0:T(8,128)(2,1)S(1)} %get-tuple-element.140), channel_id=1, source_target_pairs={{0,11},{1,10},{2,9},{3,8},{4,15},{5,14},{6,13},{7,12},{8,3},{9,2},... | collective-permute-start | bytes 196616 | tf_op jit(solution)/shard_map/ppermute | solution.py:192
  31.7 9.9 %collective-permute-start.9 = (bf16[8,16,256]{2,1,0:T(8,128)(2,1)S(1)}, bf16[8,16,256]{2,1,0:T(8,128)(2,1)S(1)}, u32[]{:S(2)}, u32[]{:S(2)}) collective-permute-start(bf16[8,16,256]{2,1,0:T(8,128)(2,1)S(1)} %get-tuple-element.149), channel_id=1, source_target_pairs={{0,13},{1,12},{2,15},{3,14},{4,9},{5,8},{6,11},{7,10},{8,5},{9,4},... | collective-permute-start | bytes 196616 | tf_op jit(solution)/shard_map/ppermute | solution.py:192
  32.8 30.5 %collective-permute-start.4 = (bf16[8,16,1024]{2,1,0:T(8,128)(2,1)S(1)}, bf16[8,16,1024]{2,1,0:T(8,128)(2,1)S(1)}, u32[]{:S(2)}, u32[]{:S(2)}) collective-permute-start(bf16[8,16,1024]{2,1,0:T(8,128)(2,1)S(1)} %get-tuple-element.135), channel_id=1, source_target_pairs={{0,2},{1,3},{2,0},{3,1},{4,6},{5,7},{6,4},{7,5},{8,10},{9,11},{10,... | collective-permute-start | bytes 786440 | tf_op jit(solution)/shard_map/ppermute | solution.py:192
  34.5 7.9 %collective-permute-start.13 = (bf16[8,16,256]{2,1,0:T(8,128)(2,1)S(1)}, bf16[8,16,256]{2,1,0:T(8,128)(2,1)S(1)}, u32[]{:S(2)}, u32[]{:S(2)}) collective-permute-start(bf16[8,16,256]{2,1,0:T(8,128)(2,1)S(1)} %get-tuple-element.158), channel_id=1, source_target_pairs={{0,15},{1,14},{2,13},{3,12},{4,11},{5,10},{6,9},{7,8},{8,7},{9,6},... | collective-permute-start | bytes 196616 | tf_op jit(solution)/shard_map/ppermute | solution.py:192
  37.6 15.6 %collective-permute-start.6 = (bf16[8,16,512]{2,1,0:T(8,128)(2,1)S(1)}, bf16[8,16,512]{2,1,0:T(8,128)(2,1)S(1)}, u32[]{:S(2)}, u32[]{:S(2)}) collective-permute-start(bf16[8,16,512]{2,1,0:T(8,128)(2,1)S(1)} %get-tuple-element.141), channel_id=1, source_target_pairs={{0,8},{1,9},{2,10},{3,11},{4,12},{5,13},{6,14},{7,15},{8,0},{9,1},... | collective-permute-start | bytes 393224 | tf_op jit(solution)/shard_map/ppermute | solution.py:192
  41.6 14.6 %collective-permute-start.10 = (bf16[8,16,512]{2,1,0:T(8,128)(2,1)S(1)}, bf16[8,16,512]{2,1,0:T(8,128)(2,1)S(1)}, u32[]{:S(2)}, u32[]{:S(2)}) collective-permute-start(bf16[8,16,512]{2,1,0:T(8,128)(2,1)S(1)} %get-tuple-element.150), channel_id=1, source_target_pairs={{0,9},{1,8},{2,11},{3,10},{4,13},{5,12},{6,15},{7,14},{8,1},{9,0},... | collective-permute-start | bytes 393224 | tf_op jit(solution)/shard_map/ppermute | solution.py:192
  42.4 19.4 %collective-permute-start.14 = (bf16[8,16,512]{2,1,0:T(8,128)(2,1)S(1)}, bf16[8,16,512]{2,1,0:T(8,128)(2,1)S(1)}, u32[]{:S(2)}, u32[]{:S(2)}) collective-permute-start(bf16[8,16,512]{2,1,0:T(8,128)(2,1)S(1)} %get-tuple-element.159), channel_id=1, source_target_pairs={{0,10},{1,11},{2,8},{3,9},{4,14},{5,15},{6,12},{7,13},{8,2},{9,3},... | collective-permute-start | bytes 393224 | tf_op jit(solution)/shard_map/ppermute | solution.py:192
  53.1 28.5 %collective-permute-start.7 = (bf16[8,16,1024]{2,1,0:T(8,128)(2,1)S(1)}, bf16[8,16,1024]{2,1,0:T(8,128)(2,1)S(1)}, u32[]{:S(2)}, u32[]{:S(2)}) collective-permute-start(bf16[8,16,1024]{2,1,0:T(8,128)(2,1)S(1)} %get-tuple-element.142), channel_id=1, source_target_pairs={{0,3},{1,2},{2,1},{3,0},{4,7},{5,6},{6,5},{7,4},{8,11},{9,10},{10,... | collective-permute-start | bytes 786440 | tf_op jit(solution)/shard_map/ppermute | solution.py:192
  56.1 25.5 %collective-permute-start.11 = (bf16[8,16,1024]{2,1,0:T(8,128)(2,1)S(1)}, bf16[8,16,1024]{2,1,0:T(8,128)(2,1)S(1)}, u32[]{:S(2)}, u32[]{:S(2)}) collective-permute-start(bf16[8,16,1024]{2,1,0:T(8,128)(2,1)S(1)} %get-tuple-element.151), channel_id=1, source_target_pairs={{0,4},{1,5},{2,6},{3,7},{4,0},{5,1},{6,2},{7,3},{8,12},{9,13},{10,... | collective-permute-start | bytes 786440 | tf_op jit(solution)/shard_map/ppermute | solution.py:192
  58.2 13.3 %collective-permute-start.16 = (bf16[8,16,512]{2,1,0:T(8,128)(2,1)S(1)}, bf16[8,16,512]{2,1,0:T(8,128)(2,1)S(1)}, u32[]{:S(2)}, u32[]{:S(2)}) collective-permute-start(bf16[8,16,512]{2,1,0:T(8,128)(2,1)S(1)} %get-tuple-element.164), channel_id=1, source_target_pairs={{0,11},{1,10},{2,9},{3,8},{4,15},{5,14},{6,13},{7,12},{8,3},{9,2},... | collective-permute-start | bytes 393224 | tf_op jit(solution)/shard_map/ppermute | solution.py:192
  61.8 19.9 %collective-permute-start.15 = (bf16[8,16,1024]{2,1,0:T(8,128)(2,1)S(1)}, bf16[8,16,1024]{2,1,0:T(8,128)(2,1)S(1)}, u32[]{:S(2)}, u32[]{:S(2)}) collective-permute-start(bf16[8,16,1024]{2,1,0:T(8,128)(2,1)S(1)} %get-tuple-element.160), channel_id=1, source_target_pairs={{0,5},{1,4},{2,7},{3,6},{4,1},{5,0},{6,3},{7,2},{8,13},{9,12},{10,... | collective-permute-start | bytes 786440 | tf_op jit(solution)/shard_map/ppermute | solution.py:192
  63.2 8.2 %collective-permute-start.18 = (bf16[8,16,512]{2,1,0:T(8,128)(2,1)S(1)}, bf16[8,16,512]{2,1,0:T(8,128)(2,1)S(1)}, u32[]{:S(2)}, u32[]{:S(2)}) collective-permute-start(bf16[8,16,512]{2,1,0:T(8,128)(2,1)S(1)} %get-tuple-element.169), channel_id=1, source_target_pairs={{0,12},{1,13},{2,14},{3,15},{4,8},{5,9},{6,10},{7,11},{8,4},{9,5},... | collective-permute-start | bytes 393224 | tf_op jit(solution)/shard_map/ppermute | solution.py:192
  71.4 27.7 %collective-permute-start.17 = (bf16[8,16,1024]{2,1,0:T(8,128)(2,1)S(1)}, bf16[8,16,1024]{2,1,0:T(8,128)(2,1)S(1)}, u32[]{:S(2)}, u32[]{:S(2)}) collective-permute-start(bf16[8,16,1024]{2,1,0:T(8,128)(2,1)S(1)} %get-tuple-element.165), channel_id=1, source_target_pairs={{0,6},{1,7},{2,4},{3,5},{4,2},{5,3},{6,0},{7,1},{8,14},{9,15},{10,... | collective-permute-start | bytes 786440 | tf_op jit(solution)/shard_map/ppermute | solution.py:192
  71.5 39.7 %collective-permute-start.19 = (bf16[8,16,1024]{2,1,0:T(8,128)(2,1)S(1)}, bf16[8,16,1024]{2,1,0:T(8,128)(2,1)S(1)}, u32[]{:S(2)}, u32[]{:S(2)}) collective-permute-start(bf16[8,16,1024]{2,1,0:T(8,128)(2,1)S(1)} %get-tuple-element.170), channel_id=1, source_target_pairs={{0,7},{1,6},{2,5},{3,4},{4,3},{5,2},{6,1},{7,0},{8,15},{9,14},{10,... | collective-permute-start | bytes 786440 | tf_op jit(solution)/shard_map/ppermute | solution.py:192
  81.6 6.0 %collective-permute-start.20 = (bf16[8,16,512]{2,1,0:T(8,128)(2,1)S(1)}, bf16[8,16,512]{2,1,0:T(8,128)(2,1)S(1)}, u32[]{:S(2)}, u32[]{:S(2)}) collective-permute-start(bf16[8,16,512]{2,1,0:T(8,128)(2,1)S(1)} %get-tuple-element.174), channel_id=1, source_target_pairs={{0,13},{1,12},{2,15},{3,14},{4,9},{5,8},{6,11},{7,10},{8,5},{9,4},... | collective-permute-start | bytes 393224 | tf_op jit(solution)/shard_map/ppermute | solution.py:192
  81.6 16.3 %collective-permute-start.23 = (bf16[8,16,512]{2,1,0:T(8,128)(2,1)S(1)}, bf16[8,16,512]{2,1,0:T(8,128)(2,1)S(1)}, u32[]{:S(2)}, u32[]{:S(2)}) collective-permute-start(bf16[8,16,512]{2,1,0:T(8,128)(2,1)S(1)} %get-tuple-element.182), channel_id=1, source_target_pairs={{0,14},{1,15},{2,12},{3,13},{4,10},{5,11},{6,8},{7,9},{8,6},{9,7},... | collective-permute-start | bytes 393224 | tf_op jit(solution)/shard_map/ppermute | solution.py:192
  81.7 22.8 %collective-permute-start.26 = (bf16[8,16,512]{2,1,0:T(8,128)(2,1)S(1)}, bf16[8,16,512]{2,1,0:T(8,128)(2,1)S(1)}, u32[]{:S(2)}, u32[]{:S(2)}) collective-permute-start(bf16[8,16,512]{2,1,0:T(8,128)(2,1)S(1)} %get-tuple-element.187), channel_id=1, source_target_pairs={{0,15},{1,14},{2,13},{3,12},{4,11},{5,10},{6,9},{7,8},{8,7},{9,6},... | collective-permute-start | bytes 393224 | tf_op jit(solution)/shard_map/ppermute | solution.py:192
  87.6 17.8 %collective-permute-start.21 = (bf16[8,16,256]{2,1,0:T(8,128)(2,1)S(1)}, bf16[8,16,256]{2,1,0:T(8,128)(2,1)S(1)}, u32[]{:S(2)}, u32[]{:S(2)}) collective-permute-start(bf16[8,16,256]{2,1,0:T(8,128)(2,1)S(1)} %get-tuple-element.175), channel_id=1, source_target_pairs={{0,8},{1,9},{2,10},{3,11},{4,12},{5,13},{6,14},{7,15},{8,0},{9,1},... | collective-permute-start | bytes 196616 | tf_op jit(solution)/shard_map/ppermute | solution.py:192
  97.9 9.8 %collective-permute-start.24 = (bf16[8,16,256]{2,1,0:T(8,128)(2,1)S(1)}, bf16[8,16,256]{2,1,0:T(8,128)(2,1)S(1)}, u32[]{:S(2)}, u32[]{:S(2)}) collective-permute-start(bf16[8,16,256]{2,1,0:T(8,128)(2,1)S(1)} %get-tuple-element.183), channel_id=1, source_target_pairs={{0,10},{1,11},{2,8},{3,9},{4,14},{5,15},{6,12},{7,13},{8,2},{9,3},... | collective-permute-start | bytes 196616 | tf_op jit(solution)/shard_map/ppermute | solution.py:192
  99.2 16.9 %collective-permute-start.22 = (bf16[8,16,256]{2,1,0:T(8,128)(2,1)S(1)}, bf16[8,16,256]{2,1,0:T(8,128)(2,1)S(1)}, u32[]{:S(2)}, u32[]{:S(2)}) collective-permute-start(bf16[8,16,256]{2,1,0:T(8,128)(2,1)S(1)} %get-tuple-element.178), channel_id=1, source_target_pairs={{0,9},{1,8},{2,11},{3,10},{4,13},{5,12},{6,15},{7,14},{8,1},{9,0},... | collective-permute-start | bytes 196616 | tf_op jit(solution)/shard_map/ppermute | solution.py:192
  104.6 23.5 %collective-permute-start.27 = (bf16[8,16,256]{2,1,0:T(8,128)(2,1)S(1)}, bf16[8,16,256]{2,1,0:T(8,128)(2,1)S(1)}, u32[]{:S(2)}, u32[]{:S(2)}) collective-permute-start(bf16[8,16,256]{2,1,0:T(8,128)(2,1)S(1)} %get-tuple-element.188), channel_id=1, source_target_pairs={{0,12},{1,13},{2,14},{3,15},{4,8},{5,9},{6,10},{7,11},{8,4},{9,5},... | collective-permute-start | bytes 196616 | tf_op jit(solution)/shard_map/ppermute | solution.py:192
  105.4 22.7 %collective-permute-start.28 = (bf16[8,16,256]{2,1,0:T(8,128)(2,1)S(1)}, bf16[8,16,256]{2,1,0:T(8,128)(2,1)S(1)}, u32[]{:S(2)}, u32[]{:S(2)}) collective-permute-start(bf16[8,16,256]{2,1,0:T(8,128)(2,1)S(1)} %get-tuple-element.189), channel_id=1, source_target_pairs={{0,13},{1,12},{2,15},{3,14},{4,9},{5,8},{6,11},{7,10},{8,5},{9,4},... | collective-permute-start | bytes 196616 | tf_op jit(solution)/shard_map/ppermute | solution.py:192
  107.8 20.4 %collective-permute-start.30 = (bf16[8,16,256]{2,1,0:T(8,128)(2,1)S(1)}, bf16[8,16,256]{2,1,0:T(8,128)(2,1)S(1)}, u32[]{:S(2)}, u32[]{:S(2)}) collective-permute-start(bf16[8,16,256]{2,1,0:T(8,128)(2,1)S(1)} %get-tuple-element.191), channel_id=1, source_target_pairs={{0,15},{1,14},{2,13},{3,12},{4,11},{5,10},{6,9},{7,8},{8,7},{9,6},... | collective-permute-start | bytes 196616 | tf_op jit(solution)/shard_map/ppermute | solution.py:192
  111.2 16.9 %collective-permute-start.25 = (bf16[8,16,256]{2,1,0:T(8,128)(2,1)S(1)}, bf16[8,16,256]{2,1,0:T(8,128)(2,1)S(1)}, u32[]{:S(2)}, u32[]{:S(2)}) collective-permute-start(bf16[8,16,256]{2,1,0:T(8,128)(2,1)S(1)} %get-tuple-element.185), channel_id=1, source_target_pairs={{0,11},{1,10},{2,9},{3,8},{4,15},{5,14},{6,13},{7,12},{8,3},{9,2},... | collective-permute-start | bytes 196616 | tf_op jit(solution)/shard_map/ppermute | solution.py:192
  116.1 12.0 %collective-permute-start.29 = (bf16[8,16,256]{2,1,0:T(8,128)(2,1)S(1)}, bf16[8,16,256]{2,1,0:T(8,128)(2,1)S(1)}, u32[]{:S(2)}, u32[]{:S(2)}) collective-permute-start(bf16[8,16,256]{2,1,0:T(8,128)(2,1)S(1)} %get-tuple-element.190), channel_id=1, source_target_pairs={{0,14},{1,15},{2,12},{3,13},{4,10},{5,11},{6,8},{7,9},{8,6},{9,7},... | collective-permute-start | bytes 196616 | tf_op jit(solution)/shard_map/ppermute | solution.py:192
  (2 other events, 1.4 us)

commit v3 on v1

v3 whole, which is shorter than its diff:
```python
import functools
import math

import jax
import jax.numpy as jnp
import numpy as np
from jax import lax
from jax.experimental import pallas as pl
from jax.experimental.pallas import tpu as pltpu
from jax.sharding import PartitionSpec as P

CHANS = 128
TAPS = 8
SPECTRA = 1024
LENGTH = 2 * CHANS
AXES = ("row", "col")
LANES = 128
FRAME_GROUP = 16
TILE = 128
VMEM = 40 * 1024 * 1024


def window_table():
    total = TAPS * LENGTH
    offsets = np.arange(total, dtype=np.float64)
    profile = np.sinc((offsets - total / 2 + 0.5) / LENGTH) * (
        0.5 - 0.5 * np.cos(2 * math.pi * (offsets + 0.5) / total)
    )
    profile = profile * np.sqrt(LENGTH / np.sum(profile * profile))
    return profile.reshape(TAPS, LENGTH).astype(np.float32)


def dft_table():
    times = np.arange(LENGTH)
    freqs = np.arange(CHANS)
    phase = 2 * math.pi * ((freqs[:, None] * times[None, :]) % LENGTH) / LENGTH
    table = np.concatenate([np.cos(phase), -np.sin(phase)], 0) / math.sqrt(LENGTH)
    return table.astype(np.float32).astype(jnp.bfloat16)


def spectra_tile(start, first_row, in_dev, targets, base_of, outs, frames, window, fourier, filtered, spectra):
    @pl.loop(0, TILE // FRAME_GROUP)
    def _(group):
        first = start + group * FRAME_GROUP
        for half in range(LENGTH // LANES):
            cols = slice(half * LANES, (half + 1) * LANES)
            held = frames[pl.ds(first, FRAME_GROUP + TAPS - 1), :, cols].astype(jnp.float32)
            total = window[0:1, cols] * held[0:FRAME_GROUP]
            for tap in range(1, TAPS):
                total = total + window[tap : tap + 1, cols] * held[tap : tap + FRAME_GROUP]
            filtered[half, pl.ds(group * FRAME_GROUP * in_dev, FRAME_GROUP * in_dev), :] = total.reshape(
                FRAME_GROUP * in_dev, LANES
            )

    first_row()
    for i in range(in_dev):
        rows = jnp.concatenate(
            [filtered[half, pl.ds(i, TILE, stride=in_dev), :] for half in range(LENGTH // LANES)], axis=1
        ).astype(jnp.bfloat16)
        product = lax.dot_general(
            fourier[...], rows, (((1,), (1,)), ((), ())), preferred_element_type=jnp.float32
        )
        for part in range(TILE // LANES):
            spectra[part, pl.ds(i * 2 * CHANS, 2 * CHANS), :] = product[:, part * LANES : (part + 1) * LANES]
    for (other, low, width), out in zip(targets, outs):
        if not low <= start < low + width:
            continue
        base = base_of(other)
        offset = start - low
        for channel in range(out.shape[0]):
            for part in range(TILE // LANES):
                pair = [
                    spectra[part, pl.ds(base + plane * CHANS + channel, in_dev, stride=2 * CHANS), :]
                    for plane in range(2)
                ]
                out[channel, :, offset + part * LANES : offset + (part + 1) * LANES] = jnp.concatenate(
                    pair, axis=0
                ).astype(jnp.bfloat16)


def first_spectra_kernel(count, in_dev, blocks, targets, *refs):
    owner_in, frames_in, window_in, fourier_in = refs[:4]
    outs = refs[4 : 4 + len(targets)]
    frames, window, fourier, owner_held, filtered, spectra, owner, arrived = refs[4 + len(targets) :]
    me = lax.axis_index(AXES)
    needed, total = count + TAPS - 1, SPECTRA + TAPS - 1
    window_copy = pltpu.make_async_copy(window_in, window, arrived.at[0])
    fourier_copy = pltpu.make_async_copy(fourier_in, fourier, arrived.at[1])
    owner_copy = pltpu.make_async_copy(owner_in, owner, arrived.at[2])
    held_copy = pltpu.make_async_copy(owner_in, owner_held, arrived.at[3])
    edges = [0, TILE + TAPS - 1, needed, total]
    frame_copies = [
        pltpu.make_async_copy(frames_in.at[pl.ds(low, high - low)], frames.at[pl.ds(low, high - low)], arrived.at[4 + index])
        for index, (low, high) in enumerate(zip(edges, edges[1:]))
    ]
    copies = [window_copy, frame_copies[0], fourier_copy, owner_copy, *frame_copies[1:], held_copy]
    for copy in copies:
        copy.start()
    window_copy.wait()
    for start in range(0, count, TILE):
        if start < 2 * TILE:
            frame_copies[start // TILE].wait()

        def tables_here():
            if start == 0:
                fourier_copy.wait()
                owner_copy.wait()

        spectra_tile(
            start, tables_here, in_dev, targets, lambda other: owner[me ^ other] * (CHANS // blocks),
            outs, frames, window, fourier, filtered, spectra,
        )
    held_copy.wait()
    frame_copies[2].wait()


def spectra_kernel(first, count, in_dev, blocks, targets, kept, *refs):
    frames, window, fourier, owner_held = refs[:4]
    outs = refs[4 + kept : 4 + kept + len(targets)]
    filtered, spectra, owner, arrived = refs[4 + kept + len(targets) :]
    me = lax.axis_index(AXES)
    owner_copy = pltpu.make_async_copy(owner_held, owner, arrived.at[0])
    owner_copy.start()
    owner_copy.wait()
    for start in range(first, first + count, TILE):
        spectra_tile(
            start, lambda: None, in_dev, targets, lambda other: owner[me ^ other] * (CHANS // blocks),
            outs, frames, window, fourier, filtered, spectra,
        )


def make_spectra(inputs, start, count, in_dev, blocks, targets, kept=()):
    per_block = CHANS // blocks
    rows = 2 * in_dev
    vmem, hbm = pl.BlockSpec(memory_space=pltpu.VMEM), pl.BlockSpec(memory_space=pltpu.HBM)
    out_shape = [jax.ShapeDtypeStruct((per_block, rows, width), jnp.bfloat16) for _, _, width in targets]
    scratch = [
        pltpu.VMEM((LENGTH // LANES, TILE * in_dev, LANES), jnp.float32),
        pltpu.VMEM((TILE // LANES, in_dev * 2 * CHANS, LANES), jnp.float32),
        pltpu.SMEM((blocks,), jnp.int32),
    ]
    if start == 0:
        owner_block, frames, window, fourier = inputs
        kernel = functools.partial(first_spectra_kernel, count, in_dev, blocks, targets)
        out_shape += [jax.ShapeDtypeStruct(x.shape, x.dtype) for x in (frames, window, fourier, owner_block)]
        in_specs = [hbm] * 4
        inputs = [pltpu.with_memory_space_constraint(x, pltpu.HBM) for x in inputs]
        scratch.append(pltpu.SemaphoreType.DMA((7,)))
    else:
        kernel = functools.partial(spectra_kernel, start, count, in_dev, blocks, targets, len(kept))
        in_specs = [vmem] * (4 + len(kept))
        scratch.append(pltpu.SemaphoreType.DMA((1,)))
    return pl.pallas_call(
        kernel,
        in_specs=in_specs,
        out_specs=[vmem] * len(out_shape),
        out_shape=out_shape,
        scratch_shapes=scratch,
        input_output_aliases={4 + index: len(targets) - len(kept) + index for index in range(len(kept))},
        compiler_params=pltpu.CompilerParams(vmem_limit_bytes=VMEM),
    )(*inputs, *kept)


def correlate_kernel(in_dev, blocks, start, count, chunks, *refs):
    parts = refs[:blocks]
    per_block = parts[0].shape[0]
    inputs = in_dev * blocks
    me = lax.axis_index(AXES)
    if chunks:
        before, beams = refs[blocks], refs[blocks + 1 : blocks + 1 + len(chunks)]
        visibility_out, beam_out, visibility, beam, left = refs[blocks + 1 + len(chunks) : blocks + 6 + len(chunks)]
        planes = refs[blocks + 6 + len(chunks) :]
        copies = [
            pltpu.make_async_copy(held, beam_out.at[:, pl.ds(first, size)], left.at[per_block + 1 + index])
            for index, ((first, size), held) in enumerate(zip(chunks, beams))
        ]
        for copy in copies:
            copy.start()
    else:
        before = refs[blocks] if len(refs) == blocks + 3 + per_block else None
        visibility, beam = refs[-per_block - 2 : -per_block]
        planes = refs[-per_block:]
    for channel in range(per_block):
        power = jnp.zeros((in_dev, count), jnp.float32)
        for other in range(blocks):
            place = start if parts[other].shape[2] == SPECTRA else 0
            wide = parts[other][channel, :, place : place + count].astype(jnp.float32)
            real_part, imag_part = wide[:in_dev], wide[in_dev:]
            power = power + (real_part * real_part + imag_part * imag_part)
            source = me ^ other
            planes[channel][0, source] = real_part
            planes[channel][1, source] = imag_part
        beam[channel : channel + 1, :] = jnp.sum(power, axis=0, keepdims=True) * (1.0 / inputs)
        both = planes[channel][...].reshape(2 * inputs, count).astype(jnp.bfloat16)
        gram = lax.dot_general(both, both, (((1,), (1,)), ((), ())), preferred_element_type=jnp.float32)
        straight = (gram[:inputs, :inputs] + gram[inputs:, inputs:]) * (1.0 / SPECTRA)
        crossed = (gram[inputs:, :inputs] - gram[:inputs, inputs:]) * (1.0 / SPECTRA)
        if before is not None:
            straight = before[channel, 0] + straight
            crossed = before[channel, 1] + crossed
        visibility[channel, 0] = straight
        visibility[channel, 1] = crossed
        if chunks:
            copies.append(
                pltpu.make_async_copy(visibility.at[channel], visibility_out.at[channel], left.at[channel])
            )
            copies[-1].start()
    if chunks:
        copies.append(pltpu.make_async_copy(beam, beam_out.at[:, pl.ds(start, count)], left.at[per_block]))
        copies[-1].start()
        for copy in copies:
            copy.wait()


def correlate(parts, start, count, blocks, before=None, chunks=(), beams=()):
    per_block, rows, _ = parts[0].shape
    in_dev = rows // 2
    inputs = in_dev * blocks
    visibility = (per_block, 2, inputs, inputs)
    space = pltpu.HBM if chunks else pltpu.VMEM
    staged = [
        pltpu.VMEM(visibility, jnp.float32),
        pltpu.VMEM((per_block, count), jnp.float32),
        pltpu.SemaphoreType.DMA((per_block + 1 + len(chunks),)),
    ]
    operands = [*parts, *([] if before is None else [before]), *beams]
    return pl.pallas_call(
        functools.partial(correlate_kernel, in_dev, blocks, start, count, chunks),
        in_specs=[pl.BlockSpec(memory_space=pltpu.VMEM)] * len(operands),
        out_specs=[pl.BlockSpec(memory_space=space)] * 2,
        scratch_shapes=(staged if chunks else [])
        + [pltpu.VMEM((2, blocks, in_dev, count), jnp.float32) for _ in range(per_block)],
        out_shape=[
            jax.ShapeDtypeStruct(visibility, jnp.float32),
            jax.ShapeDtypeStruct((per_block, SPECTRA if chunks else count), jnp.float32),
        ],
        compiler_params=pltpu.CompilerParams(vmem_limit_bytes=VMEM),
    )(*operands)


FAR_CHUNKS = ((0, 384), (384, 384), (768, 256))
FIRST_FRAMES = 384
IN_FLIGHT = 5


def body(voltages, owner_block):
    in_dev = voltages.shape[0]
    blocks = lax.axis_size(AXES)
    frames = voltages.reshape(in_dev, SPECTRA + TAPS - 1, LENGTH).transpose(1, 0, 2)
    inputs = (owner_block, frames, jnp.asarray(window_table()), jnp.asarray(dft_table()))
    far, near = tuple(range(blocks // 2, blocks)), tuple(range(blocks // 2))
    sent, taken = [], {}

    def after(value, key):
        value, taken[key] = lax.optimization_barrier((value, taken[key]))
        return value

    def send(name, other, block):
        if len(sent) >= IN_FLIGHT:
            block = after(block, sent[-IN_FLIGHT])
        taken[name, other] = lax.ppermute(block, AXES, [(s, s ^ other) for s in range(blocks)])
        sent.append((name, other))

    outgoing = {}
    near_targets = [(other, 0, SPECTRA) for other in near]
    chunks = [c for c in FAR_CHUNKS if c[0] < FIRST_FRAMES]
    targets = [(other, *chunk) for chunk in chunks for other in far] + near_targets
    made = make_spectra(inputs, 0, FIRST_FRAMES, in_dev, blocks, targets)
    inputs, kept = made[len(targets) :], made[len(targets) - len(near) : len(targets)]
    outgoing.update(((low, other), block) for (other, low, _), block in zip(targets, made))
    for low, _ in chunks:
        for other in far:
            send(low, other, outgoing[low, other])
    chunks = [c for c in FAR_CHUNKS if c[0] >= FIRST_FRAMES]
    targets = [(other, *chunk) for chunk in chunks for other in far] + near_targets
    made = make_spectra(inputs, FIRST_FRAMES, SPECTRA - FIRST_FRAMES, in_dev, blocks, targets, kept)
    outgoing.update(((low, other), block) for (other, low, _), block in zip(targets, made))
    taken["near", 0] = outgoing[0, 0]
    others = list(near[1:])
    for low, _ in chunks:
        for other in far:
            send(low, other, outgoing[low, other])
            if others:
                send("near", others[0], outgoing[0, others.pop(0)])

    visibility, beams = None, ()
    for index, (low, count) in enumerate(FAR_CHUNKS):
        parts = [taken["near", other] for other in near] + [taken[low, other] for other in far]
        done = FAR_CHUNKS[:index] if index + 1 == len(FAR_CHUNKS) else ()
        visibility, beam = correlate(parts, low, count, blocks, visibility, done, beams if done else ())
        beams += (beam,)
    return (visibility[None], beam[None])


def solution(mesh):
    in_specs = (P(("groups", "row", "col"), None), P())
    out_specs = (
        P(("groups", "row", "col"), None, None, None, None),
        P(("groups", "row", "col"), None, None),
    )
    return jax.shard_map(body, mesh=mesh, in_specs=in_specs, out_specs=out_specs, check_vma=False)
```

time: 132 us -> 126 us (0.955)
  waiting for transfers between devices: 80.9 us -> 32.4 us
  starting transfers between devices: 27 us -> 72.1 us
  local copies, waits for them, and re-layouts: 2.25 us -> 0 us
    ppermute x15 -> x31, waiting for transfers between devices: 80.9 us -> 32.4 us  [send(): lax.ppermute(block, AXES, [(s, s ^ other) for s in range(blocks)])]
    ppermute x15 -> x31, starting transfers between devices: 27 us -> 72.1 us  [send(): lax.ppermute(block, AXES, [(s, s ^ other) for s in range(blocks)])]
    unnamed x6 -> x0, local copies, waits for them, and re-layouts: 2.25 us -> none
    pallas_call x2 -> x5, Pallas kernels: 19.6 us -> 18.6 us  [the longest x2 15.2 us: make_spectra(): pl.pallas_call(kernel, in_specs=in_specs, out_specs=[vmem] * len(out_shap...]
  transfers between devices with their start and end apart: 15 -> 31, of which waited for: 11 -> 12; matrix products, arithmetic and copies ran while one was open for 0% -> 0% of each run, Pallas kernels for 0% -> 9%
where the time goes in v3:
time: 126 us; the launch traced here: 124 us
  starting transfers between devices  72.1 us (57%)
  waiting for transfers between devices  32.4 us (26%)
  Pallas kernels  18.6 us (15%)
    ppermute x31, starting transfers between devices, send(): lax.ppermute(block, AXES, [(s, s ^ other) for s in range(blocks)])  72.1 us
    ppermute x31, waiting for transfers between devices, send(): lax.ppermute(block, AXES, [(s, s ^ other) for s in range(blocks)])  32.4 us
    pallas_call x2, Pallas kernels, make_spectra(): pl.pallas_call(kernel, in_specs=in_specs, out_specs=[vmem] * len(out_shap...  15.2 us
    pallas_call x3, Pallas kernels, correlate(): pl.pallas_call(functools.partial(correlate_kernel, in_dev, blocks, start,...  3.45 us
  transfers between devices with their start and end apart: 31, of which 12 were waited for; matrix products, arithmetic and copies ran while one was open for 0% of the time, Pallas kernels for 9%

profile of v3, /device:TPU:9, one launch (start us, length us, event | category | flops | bytes accessed | tf_op | source)
XLA Modules:
  0.0 124.1 jit_solution(14621922502544744556)
XLA Ops:
  0.6 6.1 %shard_map.59 = (bf16[8,16,384]{2,1,0:T(8,128)(2,1)S(1)}, bf16[8,16,384]{2,1,0:T(8,128)(2,1)S(1)}, bf16[8,16,384]{2,1,0:T(8,128)(2,1)S(1)}, bf16[8,16,384]{2,1,0...) custom-call(s32[16]{0:T(128)} %refs_0_.1, ...), custom_call_target="tpu_custom_call" | custom-call | tf_op jit(solution)/shard_map/pallas_call | solution.py:153
  6.8 2.9 %collective-permute-start.2 = (bf16[8,16,384]{2,1,0:T(8,128)(2,1)S(1)}, bf16[8,16,384]{2,1,0:T(8,128)(2,1)S(1)}, u32[]{:S(2)}, u32[]{:S(2)}) collective-permute-start(bf16[8,16,384]{2,1,0:T(8,128)(2,1)S(1)} %get-tuple-element.125), channel_id=1, source_target_pairs={{0,9},{1,8},{2,11},{3,10},{4,13},{5,12},{6,15},{7,14},{8,1},{9,0},... | collective-permute-start | bytes 294920 | tf_op jit(solution)/shard_map/ppermute | solution.py:261
  9.7 2.3 %collective-permute-start.8 = (bf16[8,16,384]{2,1,0:T(8,128)(2,1)S(1)}, bf16[8,16,384]{2,1,0:T(8,128)(2,1)S(1)}, u32[]{:S(2)}, u32[]{:S(2)}) collective-permute-start(bf16[8,16,384]{2,1,0:T(8,128)(2,1)S(1)} %get-tuple-element.140), channel_id=1, source_target_pairs={{0,8},{1,9},{2,10},{3,11},{4,12},{5,13},{6,14},{7,15},{8,0},{9,1},... | collective-permute-start | bytes 294920 | tf_op jit(solution)/shard_map/ppermute | solution.py:261
  12.0 6.5 %collective-permute-done.2.refs_9_ = bf16[8,16,384]{2,1,0:T(8,128)(2,1)S(1)} collective-permute-done((bf16[8,16,384]{2,1,0:T(8,128)(2,1)S(1)}, bf16[8,16,384]{2,1,0:T(8,128)(2,1)S(1)}, u32[]{:S(2)}, u32[]{:S(2)}) %collective-permute-start.2) | collective-permute-done | bytes 98336 | tf_op jit(solution)/shard_map/ppermute | solution.py:261
  18.5 9.0 %shard_map.60 = (bf16[8,16,384]{2,1,0:T(8,128)(2,1)S(1)}, bf16[8,16,384]{2,1,0:T(8,128)(2,1)S(1)}, bf16[8,16,384]{2,1,0:T(8,128)(2,1)S(1)}, bf16[8,16,384]{2,1,0...) custom-call(bf16[1031,8,256]{2,1,0:T(8,128)(2,1)S(1)} %get-tuple-ele, ...), custom_call_target="tpu_custom_call", output_to_operand_aliasing={{16}: (4, {}), {17}: (5, {}), {18}: (6, {}), {19}: (7, {}),... | custom-call | tf_op jit(solution)/shard_map/pallas_call | solution.py:153
  27.6 1.1 collective-permute-start.1
  28.7 3.5 %collective-permute-start.12 = (bf16[8,16,384]{2,1,0:T(8,128)(2,1)S(1)}, bf16[8,16,384]{2,1,0:T(8,128)(2,1)S(1)}, u32[]{:S(2)}, u32[]{:S(2)}) collective-permute-start(bf16[8,16,384]{2,1,0:T(8,128)(2,1)S(1)} %get-tuple-element.149), channel_id=1, source_target_pairs={{0,10},{1,11},{2,8},{3,9},{4,14},{5,15},{6,12},{7,13},{8,2},{9,3},... | collective-permute-start | bytes 294920 | tf_op jit(solution)/shard_map/ppermute | solution.py:261
  32.2 2.8 %collective-permute-start.9 = (bf16[8,16,384]{2,1,0:T(8,128)(2,1)S(1)}, bf16[8,16,384]{2,1,0:T(8,128)(2,1)S(1)}, u32[]{:S(2)}, u32[]{:S(2)}) collective-permute-start(bf16[8,16,384]{2,1,0:T(8,128)(2,1)S(1)} %get-tuple-element.141), channel_id=1, source_target_pairs={{0,13},{1,12},{2,15},{3,14},{4,9},{5,8},{6,11},{7,10},{8,5},{9,4},... | collective-permute-start | bytes 294920 | tf_op jit(solution)/shard_map/ppermute | solution.py:261
  35.0 1.2 collective-permute-start.4
  36.2 6.5 %collective-permute-start.13 = (bf16[8,16,384]{2,1,0:T(8,128)(2,1)S(1)}, bf16[8,16,384]{2,1,0:T(8,128)(2,1)S(1)}, u32[]{:S(2)}, u32[]{:S(2)}) collective-permute-start(bf16[8,16,384]{2,1,0:T(8,128)(2,1)S(1)} %get-tuple-element.150), channel_id=1, source_target_pairs={{0,15},{1,14},{2,13},{3,12},{4,11},{5,10},{6,9},{7,8},{8,7},{9,6},... | collective-permute-start | bytes 294920 | tf_op jit(solution)/shard_map/ppermute | solution.py:261
  42.8 4.5 %collective-permute-start.6 = (bf16[8,16,384]{2,1,0:T(8,128)(2,1)S(1)}, bf16[8,16,384]{2,1,0:T(8,128)(2,1)S(1)}, u32[]{:S(2)}, u32[]{:S(2)}) collective-permute-start(bf16[8,16,384]{2,1,0:T(8,128)(2,1)S(1)} %get-tuple-element.133), channel_id=1, source_target_pairs={{0,8},{1,9},{2,10},{3,11},{4,12},{5,13},{6,14},{7,15},{8,0},{9,1},... | collective-permute-start | bytes 294920 | tf_op jit(solution)/shard_map/ppermute | solution.py:261
  47.4 8.4 %collective-permute-done.13.refs_15_ = bf16[8,16,384]{2,1,0:T(8,128)(2,1)S(1)} collective-permute-done((bf16[8,16,384]{2,1,0:T(8,128)(2,1)S(1)}, bf16[8,16,384]{2,1,0:T(8,128)(2,1)S(1)}, u32[]{:S(2)}, u32[]{:S(2)}) %collective-permute-start.13) | collective-permute-done | bytes 98336 | tf_op jit(solution)/shard_map/ppermute | solution.py:261
  55.8 1.8 %collective-permute-start.7 = (bf16[8,16,1024]{2,1,0:T(8,128)(2,1)S(1)}, bf16[8,16,1024]{2,1,0:T(8,128)(2,1)S(1)}, u32[]{:S(2)}, u32[]{:S(2)}) collective-permute-start(bf16[8,16,1024]{2,1,0:T(8,128)(2,1)S(1)} %get-tuple-element.134), channel_id=1, source_target_pairs={{0,3},{1,2},{2,1},{3,0},{4,7},{5,6},{6,5},{7,4},{8,11},{9,10},{10,... | collective-permute-start | bytes 786440 | tf_op jit(solution)/shard_map/ppermute | solution.py:261
  57.6 1.8 %collective-permute-done.10.refs_9_ = bf16[8,16,384]{2,1,0:T(8,128)(2,1)S(1)} collective-permute-done((bf16[8,16,384]{2,1,0:T(8,128)(2,1)S(1)}, bf16[8,16,384]{2,1,0:T(8,128)(2,1)S(1)}, u32[]{:S(2)}, u32[]{:S(2)}) %collective-permute-start.10) | collective-permute-done | bytes 98336 | tf_op jit(solution)/shard_map/ppermute | solution.py:261
  59.4 3.4 %collective-permute-start.11 = (bf16[8,16,1024]{2,1,0:T(8,128)(2,1)S(1)}, bf16[8,16,1024]{2,1,0:T(8,128)(2,1)S(1)}, u32[]{:S(2)}, u32[]{:S(2)}) collective-permute-start(bf16[8,16,1024]{2,1,0:T(8,128)(2,1)S(1)} %get-tuple-element.143), channel_id=1, source_target_pairs={{0,4},{1,5},{2,6},{3,7},{4,0},{5,1},{6,2},{7,3},{8,12},{9,13},{10,... | collective-permute-start | bytes 786440 | tf_op jit(solution)/shard_map/ppermute | solution.py:261
  62.9 3.0 %collective-permute-start.15 = (bf16[8,16,1024]{2,1,0:T(8,128)(2,1)S(1)}, bf16[8,16,1024]{2,1,0:T(8,128)(2,1)S(1)}, u32[]{:S(2)}, u32[]{:S(2)}) collective-permute-start(bf16[8,16,1024]{2,1,0:T(8,128)(2,1)S(1)} %get-tuple-element.152), channel_id=1, source_target_pairs={{0,5},{1,4},{2,7},{3,6},{4,1},{5,0},{6,3},{7,2},{8,13},{9,12},{10,... | collective-permute-start | bytes 786440 | tf_op jit(solution)/shard_map/ppermute | solution.py:261
  65.9 1.0 collective-permute-start.18
  66.9 4.0 %collective-permute-done.16.refs_11_ = bf16[8,16,384]{2,1,0:T(8,128)(2,1)S(1)} collective-permute-done((bf16[8,16,384]{2,1,0:T(8,128)(2,1)S(1)}, bf16[8,16,384]{2,1,0:T(8,128)(2,1)S(1)}, u32[]{:S(2)}, u32[]{:S(2)}) %collective-permute-start.16) | collective-permute-done | bytes 98336 | tf_op jit(solution)/shard_map/ppermute | solution.py:261
  70.9 1.6 %collective-permute-done.18.refs_12_ = bf16[8,16,384]{2,1,0:T(8,128)(2,1)S(1)} collective-permute-done((bf16[8,16,384]{2,1,0:T(8,128)(2,1)S(1)}, bf16[8,16,384]{2,1,0:T(8,128)(2,1)S(1)}, u32[]{:S(2)}, u32[]{:S(2)}) %collective-permute-start.18) | collective-permute-done | bytes 98336 | tf_op jit(solution)/shard_map/ppermute | solution.py:261
  72.5 7.9 %collective-permute-start.19 = (bf16[8,16,1024]{2,1,0:T(8,128)(2,1)S(1)}, bf16[8,16,1024]{2,1,0:T(8,128)(2,1)S(1)}, u32[]{:S(2)}, u32[]{:S(2)}) collective-permute-start(bf16[8,16,1024]{2,1,0:T(8,128)(2,1)S(1)} %get-tuple-element.162), channel_id=1, source_target_pairs={{0,7},{1,6},{2,5},{3,4},{4,3},{5,2},{6,1},{7,0},{8,15},{9,14},{10,... | collective-permute-start | bytes 786440 | tf_op jit(solution)/shard_map/ppermute | solution.py:261
  80.4 3.4 %collective-permute-start.23 = (bf16[8,16,384]{2,1,0:T(8,128)(2,1)S(1)}, bf16[8,16,384]{2,1,0:T(8,128)(2,1)S(1)}, u32[]{:S(2)}, u32[]{:S(2)}) collective-permute-start(bf16[8,16,384]{2,1,0:T(8,128)(2,1)S(1)} %get-tuple-element.174), channel_id=1, source_target_pairs={{0,14},{1,15},{2,12},{3,13},{4,10},{5,11},{6,8},{7,9},{8,6},{9,7},... | collective-permute-start | bytes 294920 | tf_op jit(solution)/shard_map/ppermute | solution.py:261
  84.8 14.1 %collective-permute-start.21 = (bf16[8,16,256]{2,1,0:T(8,128)(2,1)S(1)}, bf16[8,16,256]{2,1,0:T(8,128)(2,1)S(1)}, u32[]{:S(2)}, u32[]{:S(2)}) collective-permute-start(bf16[8,16,256]{2,1,0:T(8,128)(2,1)S(1)} %get-tuple-element.167), channel_id=1, source_target_pairs={{0,8},{1,9},{2,10},{3,11},{4,12},{5,13},{6,14},{7,15},{8,0},{9,1},... | collective-permute-start | bytes 196616 | tf_op jit(solution)/shard_map/ppermute | solution.py:261
  98.9 3.0 %collective-permute-start.24 = (bf16[8,16,256]{2,1,0:T(8,128)(2,1)S(1)}, bf16[8,16,256]{2,1,0:T(8,128)(2,1)S(1)}, u32[]{:S(2)}, u32[]{:S(2)}) collective-permute-start(bf16[8,16,256]{2,1,0:T(8,128)(2,1)S(1)} %get-tuple-element.175), channel_id=1, source_target_pairs={{0,10},{1,11},{2,8},{3,9},{4,14},{5,15},{6,12},{7,13},{8,2},{9,3},... | collective-permute-start | bytes 196616 | tf_op jit(solution)/shard_map/ppermute | solution.py:261
  101.9 2.3 %collective-permute-done.21.refs_8_ = bf16[8,16,256]{2,1,0:T(8,128)(2,1)S(1)} collective-permute-done((bf16[8,16,256]{2,1,0:T(8,128)(2,1)S(1)}, bf16[8,16,256]{2,1,0:T(8,128)(2,1)S(1)}, u32[]{:S(2)}, u32[]{:S(2)}) %collective-permute-start.21) | collective-permute-done | bytes 65568 | tf_op jit(solution)/shard_map/ppermute | solution.py:261
  107.0 1.4 %collective-permute-done.22.refs_9_ = bf16[8,16,256]{2,1,0:T(8,128)(2,1)S(1)} collective-permute-done((bf16[8,16,256]{2,1,0:T(8,128)(2,1)S(1)}, bf16[8,16,256]{2,1,0:T(8,128)(2,1)S(1)}, u32[]{:S(2)}, u32[]{:S(2)}) %collective-permute-start.22) | collective-permute-done | bytes 65568 | tf_op jit(solution)/shard_map/ppermute | solution.py:261
  108.4 1.4 %collective-permute-start.29 = (bf16[8,16,256]{2,1,0:T(8,128)(2,1)S(1)}, bf16[8,16,256]{2,1,0:T(8,128)(2,1)S(1)}, u32[]{:S(2)}, u32[]{:S(2)}) collective-permute-start(bf16[8,16,256]{2,1,0:T(8,128)(2,1)S(1)} %get-tuple-element.182), channel_id=1, source_target_pairs={{0,14},{1,15},{2,12},{3,13},{4,10},{5,11},{6,8},{7,9},{8,6},{9,7},... | collective-permute-start | bytes 196616 | tf_op jit(solution)/shard_map/ppermute | solution.py:261
  109.8 5.9 %collective-permute-start.25 = (bf16[8,16,256]{2,1,0:T(8,128)(2,1)S(1)}, bf16[8,16,256]{2,1,0:T(8,128)(2,1)S(1)}, u32[]{:S(2)}, u32[]{:S(2)}) collective-permute-start(bf16[8,16,256]{2,1,0:T(8,128)(2,1)S(1)} %get-tuple-element.177), channel_id=1, source_target_pairs={{0,11},{1,10},{2,9},{3,8},{4,15},{5,14},{6,13},{7,12},{8,3},{9,2},... | collective-permute-start | bytes 196616 | tf_op jit(solution)/shard_map/ppermute | solution.py:261
  116.7 1.0 shard_map.62
  117.7 1.9 %collective-permute-done.30.refs_15_ = bf16[8,16,256]{2,1,0:T(8,128)(2,1)S(1)} collective-permute-done((bf16[8,16,256]{2,1,0:T(8,128)(2,1)S(1)}, bf16[8,16,256]{2,1,0:T(8,128)(2,1)S(1)}, u32[]{:S(2)}, u32[]{:S(2)}) %collective-permute-start.30) | collective-permute-done | bytes 65568 | tf_op jit(solution)/shard_map/ppermute | solution.py:261
  119.6 1.4 %collective-permute-done.29.refs_14_ = bf16[8,16,256]{2,1,0:T(8,128)(2,1)S(1)} collective-permute-done((bf16[8,16,256]{2,1,0:T(8,128)(2,1)S(1)}, bf16[8,16,256]{2,1,0:T(8,128)(2,1)S(1)}, u32[]{:S(2)}, u32[]{:S(2)}) %collective-permute-start.29) | collective-permute-done | bytes 65568 | tf_op jit(solution)/shard_map/ppermute | solution.py:261
  121.0 1.4 %collective-permute-done.25.refs_11_ = bf16[8,16,256]{2,1,0:T(8,128)(2,1)S(1)} collective-permute-done((bf16[8,16,256]{2,1,0:T(8,128)(2,1)S(1)}, bf16[8,16,256]{2,1,0:T(8,128)(2,1)S(1)}, u32[]{:S(2)}, u32[]{:S(2)}) %collective-permute-start.25) | collective-permute-done | bytes 65568 | tf_op jit(solution)/shard_map/ppermute | solution.py:261
  122.4 1.5 %shard_map.63 = (f32[8,2,128,128]{3,2,1,0:T(8,128)}, f32[8,1024]{1,0:T(8,128)}) custom-call(bf16[8,16,1024]{2,1,0:T(8,128)(2,1)S(1)} %get-tuple-element.116.refs_0_, bf16[8,16,1024]{2,1,0:T(8,128)(2,1)S(1)} %collective-permute-done.1.refs_1_, bf16[8,16,1024]{2,1,0:T(8,128)(2,1)S(1)} %collective-permute-done.4.refs_2_, ...), custom_call_target="tpu_custom_call" | custom-call | tf_op jit(solution)/shard_map/pallas_call | solution.py:227
  (35 shorter events, 5.0 us)
Async XLA Ops:
  6.8 11.8 %collective-permute-start.2 = (bf16[8,16,384]{2,1,0:T(8,128)(2,1)S(1)}, bf16[8,16,384]{2,1,0:T(8,128)(2,1)S(1)}, u32[]{:S(2)}, u32[]{:S(2)}) collective-permute-start(bf16[8,16,384]{2,1,0:T(8,128)(2,1)S(1)} %get-tuple-element.125), channel_id=1, source_target_pairs={{0,9},{1,8},{2,11},{3,10},{4,13},{5,12},{6,15},{7,14},{8,1},{9,0},... | collective-permute-start | bytes 294920 | tf_op jit(solution)/shard_map/ppermute | solution.py:261
  9.7 17.9 %collective-permute-start = (bf16[8,16,384]{2,1,0:T(8,128)(2,1)S(1)}, bf16[8,16,384]{2,1,0:T(8,128)(2,1)S(1)}, u32[]{:S(2)}, u32[]{:S(2)}) collective-permute-start(bf16[8,16,384]{2,1,0:T(8,128)(2,1)S(1)} %get-tuple-element.119), channel_id=1, source_target_pairs={{0,12},{1,13},{2,14},{3,15},{4,8},{5,9},{6,10},{7,11},{8,4},{9,5},... | collective-permute-start | bytes 294920 | tf_op jit(solution)/shard_map/ppermute | solution.py:261
  9.7 22.5 %collective-permute-start.8 = (bf16[8,16,384]{2,1,0:T(8,128)(2,1)S(1)}, bf16[8,16,384]{2,1,0:T(8,128)(2,1)S(1)}, u32[]{:S(2)}, u32[]{:S(2)}) collective-permute-start(bf16[8,16,384]{2,1,0:T(8,128)(2,1)S(1)} %get-tuple-element.140), channel_id=1, source_target_pairs={{0,8},{1,9},{2,10},{3,11},{4,12},{5,13},{6,14},{7,15},{8,0},{9,1},... | collective-permute-start | bytes 294920 | tf_op jit(solution)/shard_map/ppermute | solution.py:261
  18.5 16.5 %collective-permute-start.3 = (bf16[8,16,384]{2,1,0:T(8,128)(2,1)S(1)}, bf16[8,16,384]{2,1,0:T(8,128)(2,1)S(1)}, u32[]{:S(2)}, u32[]{:S(2)}) collective-permute-start(bf16[8,16,384]{2,1,0:T(8,128)(2,1)S(1)} %get-tuple-element.126), channel_id=1, source_target_pairs={{0,14},{1,15},{2,12},{3,13},{4,10},{5,11},{6,8},{7,9},{8,6},{9,7},... | collective-permute-start | bytes 294920 | tf_op jit(solution)/shard_map/ppermute | solution.py:261
  27.6 35.3 %collective-permute-start.1 = (bf16[8,16,1024]{2,1,0:T(8,128)(2,1)S(1)}, bf16[8,16,1024]{2,1,0:T(8,128)(2,1)S(1)}, u32[]{:S(2)}, u32[]{:S(2)}) collective-permute-start(bf16[8,16,1024]{2,1,0:T(8,128)(2,1)S(1)} %get-tuple-element.120), channel_id=1, source_target_pairs={{0,1},{1,0},{2,3},{3,2},{4,5},{5,4},{6,7},{7,6},{8,9},{9,8},{10,11... | collective-permute-start | bytes 786440 | tf_op jit(solution)/shard_map/ppermute | solution.py:261
  28.7 7.6 %collective-permute-start.12 = (bf16[8,16,384]{2,1,0:T(8,128)(2,1)S(1)}, bf16[8,16,384]{2,1,0:T(8,128)(2,1)S(1)}, u32[]{:S(2)}, u32[]{:S(2)}) collective-permute-start(bf16[8,16,384]{2,1,0:T(8,128)(2,1)S(1)} %get-tuple-element.149), channel_id=1, source_target_pairs={{0,10},{1,11},{2,8},{3,9},{4,14},{5,15},{6,12},{7,13},{8,2},{9,3},... | collective-permute-start | bytes 294920 | tf_op jit(solution)/shard_map/ppermute | solution.py:261
  32.1 10.7 %collective-permute-start.5 = (bf16[8,16,384]{2,1,0:T(8,128)(2,1)S(1)}, bf16[8,16,384]{2,1,0:T(8,128)(2,1)S(1)}, u32[]{:S(2)}, u32[]{:S(2)}) collective-permute-start(bf16[8,16,384]{2,1,0:T(8,128)(2,1)S(1)} %get-tuple-element.132), channel_id=1, source_target_pairs={{0,11},{1,10},{2,9},{3,8},{4,15},{5,14},{6,13},{7,12},{8,3},{9,2},... | collective-permute-start | bytes 294920 | tf_op jit(solution)/shard_map/ppermute | solution.py:261
  32.2 15.1 %collective-permute-start.9 = (bf16[8,16,384]{2,1,0:T(8,128)(2,1)S(1)}, bf16[8,16,384]{2,1,0:T(8,128)(2,1)S(1)}, u32[]{:S(2)}, u32[]{:S(2)}) collective-permute-start(bf16[8,16,384]{2,1,0:T(8,128)(2,1)S(1)} %get-tuple-element.141), channel_id=1, source_target_pairs={{0,13},{1,12},{2,15},{3,14},{4,9},{5,8},{6,11},{7,10},{8,5},{9,4},... | collective-permute-start | bytes 294920 | tf_op jit(solution)/shard_map/ppermute | solution.py:261
  35.0 30.9 %collective-permute-start.4 = (bf16[8,16,1024]{2,1,0:T(8,128)(2,1)S(1)}, bf16[8,16,1024]{2,1,0:T(8,128)(2,1)S(1)}, u32[]{:S(2)}, u32[]{:S(2)}) collective-permute-start(bf16[8,16,1024]{2,1,0:T(8,128)(2,1)S(1)} %get-tuple-element.127), channel_id=1, source_target_pairs={{0,2},{1,3},{2,0},{3,1},{4,6},{5,7},{6,4},{7,5},{8,10},{9,11},{10,... | collective-permute-start | bytes 786440 | tf_op jit(solution)/shard_map/ppermute | solution.py:261
  36.2 19.5 %collective-permute-start.13 = (bf16[8,16,384]{2,1,0:T(8,128)(2,1)S(1)}, bf16[8,16,384]{2,1,0:T(8,128)(2,1)S(1)}, u32[]{:S(2)}, u32[]{:S(2)}) collective-permute-start(bf16[8,16,384]{2,1,0:T(8,128)(2,1)S(1)} %get-tuple-element.150), channel_id=1, source_target_pairs={{0,15},{1,14},{2,13},{3,12},{4,11},{5,10},{6,9},{7,8},{8,7},{9,6},... | collective-permute-start | bytes 294920 | tf_op jit(solution)/shard_map/ppermute | solution.py:261
  42.8 13.0 %collective-permute-start.6 = (bf16[8,16,384]{2,1,0:T(8,128)(2,1)S(1)}, bf16[8,16,384]{2,1,0:T(8,128)(2,1)S(1)}, u32[]{:S(2)}, u32[]{:S(2)}) collective-permute-start(bf16[8,16,384]{2,1,0:T(8,128)(2,1)S(1)} %get-tuple-element.133), channel_id=1, source_target_pairs={{0,8},{1,9},{2,10},{3,11},{4,12},{5,13},{6,14},{7,15},{8,0},{9,1},... | collective-permute-start | bytes 294920 | tf_op jit(solution)/shard_map/ppermute | solution.py:261
  47.3 12.1 %collective-permute-start.10 = (bf16[8,16,384]{2,1,0:T(8,128)(2,1)S(1)}, bf16[8,16,384]{2,1,0:T(8,128)(2,1)S(1)}, u32[]{:S(2)}, u32[]{:S(2)}) collective-permute-start(bf16[8,16,384]{2,1,0:T(8,128)(2,1)S(1)} %get-tuple-element.142), channel_id=1, source_target_pairs={{0,9},{1,8},{2,11},{3,10},{4,13},{5,12},{6,15},{7,14},{8,1},{9,0},... | collective-permute-start | bytes 294920 | tf_op jit(solution)/shard_map/ppermute | solution.py:261
  55.8 7.1 %collective-permute-start.14 = (bf16[8,16,384]{2,1,0:T(8,128)(2,1)S(1)}, bf16[8,16,384]{2,1,0:T(8,128)(2,1)S(1)}, u32[]{:S(2)}, u32[]{:S(2)}) collective-permute-start(bf16[8,16,384]{2,1,0:T(8,128)(2,1)S(1)} %get-tuple-element.151), channel_id=1, source_target_pairs={{0,10},{1,11},{2,8},{3,9},{4,14},{5,15},{6,12},{7,13},{8,2},{9,3},... | collective-permute-start | bytes 294920 | tf_op jit(solution)/shard_map/ppermute | solution.py:261
  55.8 24.6 %collective-permute-start.7 = (bf16[8,16,1024]{2,1,0:T(8,128)(2,1)S(1)}, bf16[8,16,1024]{2,1,0:T(8,128)(2,1)S(1)}, u32[]{:S(2)}, u32[]{:S(2)}) collective-permute-start(bf16[8,16,1024]{2,1,0:T(8,128)(2,1)S(1)} %get-tuple-element.134), channel_id=1, source_target_pairs={{0,3},{1,2},{2,1},{3,0},{4,7},{5,6},{6,5},{7,4},{8,11},{9,10},{10,... | collective-permute-start | bytes 786440 | tf_op jit(solution)/shard_map/ppermute | solution.py:261
  59.4 21.0 %collective-permute-start.11 = (bf16[8,16,1024]{2,1,0:T(8,128)(2,1)S(1)}, bf16[8,16,1024]{2,1,0:T(8,128)(2,1)S(1)}, u32[]{:S(2)}, u32[]{:S(2)}) collective-permute-start(bf16[8,16,1024]{2,1,0:T(8,128)(2,1)S(1)} %get-tuple-element.143), channel_id=1, source_target_pairs={{0,4},{1,5},{2,6},{3,7},{4,0},{5,1},{6,2},{7,3},{8,12},{9,13},{10,... | collective-permute-start | bytes 786440 | tf_op jit(solution)/shard_map/ppermute | solution.py:261
  62.9 8.1 %collective-permute-start.16 = (bf16[8,16,384]{2,1,0:T(8,128)(2,1)S(1)}, bf16[8,16,384]{2,1,0:T(8,128)(2,1)S(1)}, u32[]{:S(2)}, u32[]{:S(2)}) collective-permute-start(bf16[8,16,384]{2,1,0:T(8,128)(2,1)S(1)} %get-tuple-element.156), channel_id=1, source_target_pairs={{0,11},{1,10},{2,9},{3,8},{4,15},{5,14},{6,13},{7,12},{8,3},{9,2},... | collective-permute-start | bytes 294920 | tf_op jit(solution)/shard_map/ppermute | solution.py:261
  62.9 20.9 %collective-permute-start.15 = (bf16[8,16,1024]{2,1,0:T(8,128)(2,1)S(1)}, bf16[8,16,1024]{2,1,0:T(8,128)(2,1)S(1)}, u32[]{:S(2)}, u32[]{:S(2)}) collective-permute-start(bf16[8,16,1024]{2,1,0:T(8,128)(2,1)S(1)} %get-tuple-element.152), channel_id=1, source_target_pairs={{0,5},{1,4},{2,7},{3,6},{4,1},{5,0},{6,3},{7,2},{8,13},{9,12},{10,... | collective-permute-start | bytes 786440 | tf_op jit(solution)/shard_map/ppermute | solution.py:261
  65.9 6.6 %collective-permute-start.18 = (bf16[8,16,384]{2,1,0:T(8,128)(2,1)S(1)}, bf16[8,16,384]{2,1,0:T(8,128)(2,1)S(1)}, u32[]{:S(2)}, u32[]{:S(2)}) collective-permute-start(bf16[8,16,384]{2,1,0:T(8,128)(2,1)S(1)} %get-tuple-element.161), channel_id=1, source_target_pairs={{0,12},{1,13},{2,14},{3,15},{4,8},{5,9},{6,10},{7,11},{8,4},{9,5},... | collective-permute-start | bytes 294920 | tf_op jit(solution)/shard_map/ppermute | solution.py:261
  70.9 31.0 %collective-permute-start.17 = (bf16[8,16,1024]{2,1,0:T(8,128)(2,1)S(1)}, bf16[8,16,1024]{2,1,0:T(8,128)(2,1)S(1)}, u32[]{:S(2)}, u32[]{:S(2)}) collective-permute-start(bf16[8,16,1024]{2,1,0:T(8,128)(2,1)S(1)} %get-tuple-element.157), channel_id=1, source_target_pairs={{0,6},{1,7},{2,4},{3,5},{4,2},{5,3},{6,0},{7,1},{8,14},{9,15},{10,... | collective-permute-start | bytes 786440 | tf_op jit(solution)/shard_map/ppermute | solution.py:261
  72.5 37.3 %collective-permute-start.19 = (bf16[8,16,1024]{2,1,0:T(8,128)(2,1)S(1)}, bf16[8,16,1024]{2,1,0:T(8,128)(2,1)S(1)}, u32[]{:S(2)}, u32[]{:S(2)}) collective-permute-start(bf16[8,16,1024]{2,1,0:T(8,128)(2,1)S(1)} %get-tuple-element.162), channel_id=1, source_target_pairs={{0,7},{1,6},{2,5},{3,4},{4,3},{5,2},{6,1},{7,0},{8,15},{9,14},{10,... | collective-permute-start | bytes 786440 | tf_op jit(solution)/shard_map/ppermute | solution.py:261
  80.4 4.3 %collective-permute-start.20 = (bf16[8,16,384]{2,1,0:T(8,128)(2,1)S(1)}, bf16[8,16,384]{2,1,0:T(8,128)(2,1)S(1)}, u32[]{:S(2)}, u32[]{:S(2)}) collective-permute-start(bf16[8,16,384]{2,1,0:T(8,128)(2,1)S(1)} %get-tuple-element.166), channel_id=1, source_target_pairs={{0,13},{1,12},{2,15},{3,14},{4,9},{5,8},{6,11},{7,10},{8,5},{9,4},... | collective-permute-start | bytes 294920 | tf_op jit(solution)/shard_map/ppermute | solution.py:261
  80.4 18.5 %collective-permute-start.23 = (bf16[8,16,384]{2,1,0:T(8,128)(2,1)S(1)}, bf16[8,16,384]{2,1,0:T(8,128)(2,1)S(1)}, u32[]{:S(2)}, u32[]{:S(2)}) collective-permute-start(bf16[8,16,384]{2,1,0:T(8,128)(2,1)S(1)} %get-tuple-element.174), channel_id=1, source_target_pairs={{0,14},{1,15},{2,12},{3,13},{4,10},{5,11},{6,8},{7,9},{8,6},{9,7},... | collective-permute-start | bytes 294920 | tf_op jit(solution)/shard_map/ppermute | solution.py:261
  83.8 21.3 %collective-permute-start.26 = (bf16[8,16,384]{2,1,0:T(8,128)(2,1)S(1)}, bf16[8,16,384]{2,1,0:T(8,128)(2,1)S(1)}, u32[]{:S(2)}, u32[]{:S(2)}) collective-permute-start(bf16[8,16,384]{2,1,0:T(8,128)(2,1)S(1)} %get-tuple-element.179), channel_id=1, source_target_pairs={{0,15},{1,14},{2,13},{3,12},{4,11},{5,10},{6,9},{7,8},{8,7},{9,6},... | collective-permute-start | bytes 294920 | tf_op jit(solution)/shard_map/ppermute | solution.py:261
  84.8 19.4 %collective-permute-start.21 = (bf16[8,16,256]{2,1,0:T(8,128)(2,1)S(1)}, bf16[8,16,256]{2,1,0:T(8,128)(2,1)S(1)}, u32[]{:S(2)}, u32[]{:S(2)}) collective-permute-start(bf16[8,16,256]{2,1,0:T(8,128)(2,1)S(1)} %get-tuple-element.167), channel_id=1, source_target_pairs={{0,8},{1,9},{2,10},{3,11},{4,12},{5,13},{6,14},{7,15},{8,0},{9,1},... | collective-permute-start | bytes 196616 | tf_op jit(solution)/shard_map/ppermute | solution.py:261
  98.9 8.1 %collective-permute-start.24 = (bf16[8,16,256]{2,1,0:T(8,128)(2,1)S(1)}, bf16[8,16,256]{2,1,0:T(8,128)(2,1)S(1)}, u32[]{:S(2)}, u32[]{:S(2)}) collective-permute-start(bf16[8,16,256]{2,1,0:T(8,128)(2,1)S(1)} %get-tuple-element.175), channel_id=1, source_target_pairs={{0,10},{1,11},{2,8},{3,9},{4,14},{5,15},{6,12},{7,13},{8,2},{9,3},... | collective-permute-start | bytes 196616 | tf_op jit(solution)/shard_map/ppermute | solution.py:261
  101.9 6.5 %collective-permute-start.22 = (bf16[8,16,256]{2,1,0:T(8,128)(2,1)S(1)}, bf16[8,16,256]{2,1,0:T(8,128)(2,1)S(1)}, u32[]{:S(2)}, u32[]{:S(2)}) collective-permute-start(bf16[8,16,256]{2,1,0:T(8,128)(2,1)S(1)} %get-tuple-element.170), channel_id=1, source_target_pairs={{0,9},{1,8},{2,11},{3,10},{4,13},{5,12},{6,15},{7,14},{8,1},{9,0},... | collective-permute-start | bytes 196616 | tf_op jit(solution)/shard_map/ppermute | solution.py:261
  104.2 13.5 %collective-permute-start.28 = (bf16[8,16,256]{2,1,0:T(8,128)(2,1)S(1)}, bf16[8,16,256]{2,1,0:T(8,128)(2,1)S(1)}, u32[]{:S(2)}, u32[]{:S(2)}) collective-permute-start(bf16[8,16,256]{2,1,0:T(8,128)(2,1)S(1)} %get-tuple-element.181), channel_id=1, source_target_pairs={{0,13},{1,12},{2,15},{3,14},{4,9},{5,8},{6,11},{7,10},{8,5},{9,4},... | collective-permute-start | bytes 196616 | tf_op jit(solution)/shard_map/ppermute | solution.py:261
  105.0 12.7 %collective-permute-start.27 = (bf16[8,16,256]{2,1,0:T(8,128)(2,1)S(1)}, bf16[8,16,256]{2,1,0:T(8,128)(2,1)S(1)}, u32[]{:S(2)}, u32[]{:S(2)}) collective-permute-start(bf16[8,16,256]{2,1,0:T(8,128)(2,1)S(1)} %get-tuple-element.180), channel_id=1, source_target_pairs={{0,12},{1,13},{2,14},{3,15},{4,8},{5,9},{6,10},{7,11},{8,4},{9,5},... | collective-permute-start | bytes 196616 | tf_op jit(solution)/shard_map/ppermute | solution.py:261
  107.0 12.6 %collective-permute-start.30 = (bf16[8,16,256]{2,1,0:T(8,128)(2,1)S(1)}, bf16[8,16,256]{2,1,0:T(8,128)(2,1)S(1)}, u32[]{:S(2)}, u32[]{:S(2)}) collective-permute-start(bf16[8,16,256]{2,1,0:T(8,128)(2,1)S(1)} %get-tuple-element.183), channel_id=1, source_target_pairs={{0,15},{1,14},{2,13},{3,12},{4,11},{5,10},{6,9},{7,8},{8,7},{9,6},... | collective-permute-start | bytes 196616 | tf_op jit(solution)/shard_map/ppermute | solution.py:261
  108.4 12.6 %collective-permute-start.29 = (bf16[8,16,256]{2,1,0:T(8,128)(2,1)S(1)}, bf16[8,16,256]{2,1,0:T(8,128)(2,1)S(1)}, u32[]{:S(2)}, u32[]{:S(2)}) collective-permute-start(bf16[8,16,256]{2,1,0:T(8,128)(2,1)S(1)} %get-tuple-element.182), channel_id=1, source_target_pairs={{0,14},{1,15},{2,12},{3,13},{4,10},{5,11},{6,8},{7,9},{8,6},{9,7},... | collective-permute-start | bytes 196616 | tf_op jit(solution)/shard_map/ppermute | solution.py:261
  109.8 12.6 %collective-permute-start.25 = (bf16[8,16,256]{2,1,0:T(8,128)(2,1)S(1)}, bf16[8,16,256]{2,1,0:T(8,128)(2,1)S(1)}, u32[]{:S(2)}, u32[]{:S(2)}) collective-permute-start(bf16[8,16,256]{2,1,0:T(8,128)(2,1)S(1)} %get-tuple-element.177), channel_id=1, source_target_pairs={{0,11},{1,10},{2,9},{3,8},{4,15},{5,14},{6,13},{7,12},{8,3},{9,2},... | collective-permute-start | bytes 196616 | tf_op jit(solution)/shard_map/ppermute | solution.py:261

commit v4 on v3

--- a/solution.py
+++ b/solution.py
@@ -80,15 +80,16 @@
 
 def first_spectra_kernel(count, in_dev, blocks, targets, *refs):
     owner_in, frames_in, window_in, fourier_in = refs[:4]
-    outs = refs[4 : 4 + len(targets)]
-    frames, window, fourier, owner_held, filtered, spectra, owner, arrived = refs[4 + len(targets) :]
+    per_block = CHANS // blocks
+    outs = [refs[4].at[pl.ds(index * per_block, per_block)] for index in range(len(targets))]
+    frames, window, fourier, owner_held, filtered, spectra, owner, arrived = refs[5:]
     me = lax.axis_index(AXES)
     needed, total = count + TAPS - 1, SPECTRA + TAPS - 1
     window_copy = pltpu.make_async_copy(window_in, window, arrived.at[0])
     fourier_copy = pltpu.make_async_copy(fourier_in, fourier, arrived.at[1])
     owner_copy = pltpu.make_async_copy(owner_in, owner, arrived.at[2])
     held_copy = pltpu.make_async_copy(owner_in, owner_held, arrived.at[3])
-    edges = [0, TILE + TAPS - 1, needed, total]
+    edges = sorted({0, TILE + TAPS - 1, needed, total})
     frame_copies = [
         pltpu.make_async_copy(frames_in.at[pl.ds(low, high - low)], frames.at[pl.ds(low, high - low)], arrived.at[4 + index])
         for index, (low, high) in enumerate(zip(edges, edges[1:]))
@@ -111,25 +112,25 @@
             outs, frames, window, fourier, filtered, spectra,
         )
     held_copy.wait()
-    frame_copies[2].wait()
-
-
-def spectra_kernel(first, count, in_dev, blocks, targets, kept, *refs):
+    frame_copies[-1].wait()
+
+
+def spectra_kernel(count, in_dev, blocks, targets, *refs):
     frames, window, fourier, owner_held = refs[:4]
-    outs = refs[4 + kept : 4 + kept + len(targets)]
-    filtered, spectra, owner, arrived = refs[4 + kept + len(targets) :]
+    outs = refs[4 : 4 + len(targets)]
+    filtered, spectra, owner, arrived = refs[4 + len(targets) :]
     me = lax.axis_index(AXES)
     owner_copy = pltpu.make_async_copy(owner_held, owner, arrived.at[0])
     owner_copy.start()
     owner_copy.wait()
-    for start in range(first, first + count, TILE):
+    for start in range(0, count, TILE):
         spectra_tile(
             start, lambda: None, in_dev, targets, lambda other: owner[me ^ other] * (CHANS // blocks),
             outs, frames, window, fourier, filtered, spectra,
         )
 
 
-def make_spectra(inputs, start, count, in_dev, blocks, targets, kept=()):
+def make_spectra(inputs, count, in_dev, blocks, targets, first):
     per_block = CHANS // blocks
     rows = 2 * in_dev
     vmem, hbm = pl.BlockSpec(memory_space=pltpu.VMEM), pl.BlockSpec(memory_space=pltpu.HBM)
@@ -139,16 +140,17 @@
         pltpu.VMEM((TILE // LANES, in_dev * 2 * CHANS, LANES), jnp.float32),
         pltpu.SMEM((blocks,), jnp.int32),
     ]
-    if start == 0:
+    if first:
         owner_block, frames, window, fourier = inputs
         kernel = functools.partial(first_spectra_kernel, count, in_dev, blocks, targets)
+        out_shape = [jax.ShapeDtypeStruct((len(targets) * per_block, rows, count), jnp.bfloat16)]
         out_shape += [jax.ShapeDtypeStruct(x.shape, x.dtype) for x in (frames, window, fourier, owner_block)]
         in_specs = [hbm] * 4
         inputs = [pltpu.with_memory_space_constraint(x, pltpu.HBM) for x in inputs]
         scratch.append(pltpu.SemaphoreType.DMA((7,)))
     else:
-        kernel = functools.partial(spectra_kernel, start, count, in_dev, blocks, targets, len(kept))
-        in_specs = [vmem] * (4 + len(kept))
+        kernel = functools.partial(spectra_kernel, count, in_dev, blocks, targets)
+        in_specs = [vmem] * 4
         scratch.append(pltpu.SemaphoreType.DMA((1,)))
     return pl.pallas_call(
         kernel,
@@ -156,9 +158,8 @@
         out_specs=[vmem] * len(out_shape),
         out_shape=out_shape,
         scratch_shapes=scratch,
-        input_output_aliases={4 + index: len(targets) - len(kept) + index for index in range(len(kept))},
         compiler_params=pltpu.CompilerParams(vmem_limit_bytes=VMEM),
-    )(*inputs, *kept)
+    )(*inputs)
 
 
 def correlate_kernel(in_dev, blocks, start, count, chunks, *refs):
@@ -238,57 +239,51 @@
     )(*operands)
 
 
-FAR_CHUNKS = ((0, 384), (384, 384), (768, 256))
-FIRST_FRAMES = 384
+LEAD = 4
+LEAD_FRAMES = 384
 IN_FLIGHT = 5
 
 
 def body(voltages, owner_block):
     in_dev = voltages.shape[0]
     blocks = lax.axis_size(AXES)
+    half, per_block = blocks // 2, CHANS // blocks
     frames = voltages.reshape(in_dev, SPECTRA + TAPS - 1, LENGTH).transpose(1, 0, 2)
     inputs = (owner_block, frames, jnp.asarray(window_table()), jnp.asarray(dft_table()))
-    far, near = tuple(range(blocks // 2, blocks)), tuple(range(blocks // 2))
+    far, near = tuple(range(half, blocks)), tuple(range(half))
     sent, taken = [], {}
 
-    def after(value, key):
-        value, taken[key] = lax.optimization_barrier((value, taken[key]))
-        return value
-
-    def send(name, other, block):
+    def send(target, block, other):
         if len(sent) >= IN_FLIGHT:
-            block = after(block, sent[-IN_FLIGHT])
-        taken[name, other] = lax.ppermute(block, AXES, [(s, s ^ other) for s in range(blocks)])
-        sent.append((name, other))
-
-    outgoing = {}
-    near_targets = [(other, 0, SPECTRA) for other in near]
-    chunks = [c for c in FAR_CHUNKS if c[0] < FIRST_FRAMES]
-    targets = [(other, *chunk) for chunk in chunks for other in far] + near_targets
-    made = make_spectra(inputs, 0, FIRST_FRAMES, in_dev, blocks, targets)
-    inputs, kept = made[len(targets) :], made[len(targets) - len(near) : len(targets)]
-    outgoing.update(((low, other), block) for (other, low, _), block in zip(targets, made))
-    for low, _ in chunks:
-        for other in far:
-            send(low, other, outgoing[low, other])
-    chunks = [c for c in FAR_CHUNKS if c[0] >= FIRST_FRAMES]
-    targets = [(other, *chunk) for chunk in chunks for other in far] + near_targets
-    made = make_spectra(inputs, FIRST_FRAMES, SPECTRA - FIRST_FRAMES, in_dev, blocks, targets, kept)
-    outgoing.update(((low, other), block) for (other, low, _), block in zip(targets, made))
-    taken["near", 0] = outgoing[0, 0]
-    others = list(near[1:])
-    for low, _ in chunks:
-        for other in far:
-            send(low, other, outgoing[low, other])
-            if others:
-                send("near", others[0], outgoing[0, others.pop(0)])
-
-    visibility, beams = None, ()
-    for index, (low, count) in enumerate(FAR_CHUNKS):
-        parts = [taken["near", other] for other in near] + [taken[low, other] for other in far]
-        done = FAR_CHUNKS[:index] if index + 1 == len(FAR_CHUNKS) else ()
-        visibility, beam = correlate(parts, low, count, blocks, visibility, done, beams if done else ())
-        beams += (beam,)
+            before = sent[-IN_FLIGHT]
+            block, taken[before] = lax.optimization_barrier((block, taken[before]))
+        taken[target] = lax.ppermute(block, AXES, [(s, s ^ other) for s in range(blocks)])
+        sent.append(target)
+
+    first = [(other, 0, LEAD_FRAMES) for other in far[:LEAD]]
+    made = make_spectra(inputs, LEAD_FRAMES, in_dev, blocks, first, True)
+    send(first[0], made[0], half)
+    last = [(other, LEAD_FRAMES, SPECTRA - LEAD_FRAMES) for other in far[:LEAD]]
+    across = [(other, 0, SPECTRA) for other in far[LEAD:]]
+    close = [(other, 0, SPECTRA) for other in near]
+    targets = across + last + close
+    ready = dict(zip(targets, make_spectra(made[1:], SPECTRA, in_dev, blocks, targets, False)))
+    taken[close[0]] = ready[close[0]]
+    distant, others = across + last, close[1:]
+    handed = first[1:]
+    for index, target in enumerate(distant):
+        send(target, ready[target], target[0])
+        if index < len(others):
+            send(others[index], ready[others[index]], others[index][0])
+        if index >= 1 and index - 1 < len(handed):
+            offset = index * per_block
+            send(handed[index - 1], taken[first[0]][offset : offset + per_block], handed[index - 1][0] - half)
+
+    visibility, beam = correlate([taken[target] for target in close + first + across], 0, LEAD_FRAMES, blocks)
+    visibility, beam = correlate(
+        [taken[target] for target in close + last + across], LEAD_FRAMES, SPECTRA - LEAD_FRAMES, blocks,
+        visibility, ((0, LEAD_FRAMES),), (beam,),
+    )
     return (visibility[None], beam[None])
 
 

time: 126 us -> 113 us (0.90)
  the two profiles are of different devices: /device:TPU:9 before, /device:TPU:0 now
where the time goes in v4:
time: 113 us
  starting transfers between devices  58.9 us (52%)
  waiting for transfers between devices  31.4 us (28%)
  Pallas kernels  21.8 us (19%)
    ppermute x19, starting transfers between devices, send(): lax.ppermute(block, AXES, [(s, s ^ other) for s in range(blocks)])  58.9 us
    ppermute x19, waiting for transfers between devices, send(): lax.ppermute(block, AXES, [(s, s ^ other) for s in range(blocks)])  31.4 us
    pallas_call x2, Pallas kernels, make_spectra(): pl.pallas_call(kernel, in_specs=in_specs, out_specs=[vmem] * len(out_shap...  18.4 us
    pallas_call x2, Pallas kernels, correlate(): pl.pallas_call(functools.partial(correlate_kernel, in_dev, blocks, start,...  3.39 us
  transfers between devices with their start and end apart: 19, of which 6 were waited for; matrix products, arithmetic and copies ran while one was open for 0% of the time, Pallas kernels for 13%

profile of v4, /device:TPU:0, one launch (start us, length us, event | category | flops | bytes accessed | tf_op | source)
XLA Modules:
  0.0 113.1 jit_solution(3932162167457176090)
XLA Ops:
  0.6 4.8 %shard_map.59 = (bf16[32,16,384]{2,1,0:T(8,128)(2,1)S(1)}, bf16[1031,8,256]{2,1,0:T(8,128)(2,1)S(1)}, f32[8,256]{1,0:T(8,128)S(1)}, bf16[256,256]{1,0:T(8,128)(2,1)S(1)}, s32[16]{0:T(128)S(1)}) custom-call(s32[16]{0:T(128)} %refs_0_.1, bf16[1031,8,256]{2,1,0:T(8,128)(2,1)} %bitcast.5, f32[8,256]{1,0:T(8,128)} %constant.4.clone.refs_2_, ...), custom_call_target="tpu_custom_call" | custom-call | tf_op jit(solution)/shard_map/pallas_call | solution.py:155
  5.4 4.1 %collective-permute-start.3 = (bf16[32,16,384]{2,1,0:T(8,128)(2,1)S(1)}, bf16[32,16,384]{2,1,0:T(8,128)(2,1)S(1)}, u32[]{:S(2)}, u32[]{:S(2)}) collective-permute-start(bf16[32,16,384]{2,1,0:T(8,128)(2,1)S(1)} %get-tuple-element.71), channel_id=1, source_target_pairs={{0,8},{1,9},{2,10},{3,11},{4,12},{5,13},{6,14},{7,15},{8,0},{9,1},... | collective-permute-start | bytes 1179656 | tf_op jit(solution)/shard_map/ppermute | solution.py:260
  9.5 13.7 %shard_map.60 = (bf16[8,16,1024]{2,1,0:T(8,128)(2,1)S(1)}, bf16[8,16,1024]{2,1,0:T(8,128)(2,1)S(1)}, bf16[8,16,1024]{2,1,0:T(8,128)(2,1)S(1)}, bf16[8,16,1024]{2...) custom-call(bf16[1031,8,256]{2,1,0:T(8,128)(2,1)S(1)} %get-tuple-ele, ...), custom_call_target="tpu_custom_call" | custom-call | tf_op jit(solution)/shard_map/pallas_call | solution.py:155
  23.2 0.1 collective-permute-start
  23.3 1.4 %collective-permute-start.14 = (bf16[8,16,1024]{2,1,0:T(8,128)(2,1)S(1)}, bf16[8,16,1024]{2,1,0:T(8,128)(2,1)S(1)}, u32[]{:S(2)}, u32[]{:S(2)}) collective-permute-start(bf16[8,16,1024]{2,1,0:T(8,128)(2,1)S(1)} %get-tuple-element.92), channel_id=1, source_target_pairs={{0,12},{1,13},{2,14},{3,15},{4,8},{5,9},{6,10},{7,11},{8,4},{9,5},... | collective-permute-start | bytes 786440 | tf_op jit(solution)/shard_map/ppermute | solution.py:260
  24.7 2.4 %collective-permute-done.3.refs_8_ = bf16[32,16,384]{2,1,0:T(8,128)(2,1)S(1)} collective-permute-done((bf16[32,16,384]{2,1,0:T(8,128)(2,1)S(1)}, bf16[32,16,384]{2,1,0:T(8,128)(2,1)S(1)}, u32[]{:S(2)}, u32[]{:S(2)}) %collective-permute-start.3) | collective-permute-done | bytes 393248 | tf_op jit(solution)/shard_map/ppermute | solution.py:260
  27.1 0.1 collective-permute-start.4
  27.1 9.4 %collective-permute-start.6 = (bf16[8,16,1024]{2,1,0:T(8,128)(2,1)S(1)}, bf16[8,16,1024]{2,1,0:T(8,128)(2,1)S(1)}, u32[]{:S(2)}, u32[]{:S(2)}) collective-permute-start(bf16[8,16,1024]{2,1,0:T(8,128)(2,1)S(1)} %get-tuple-element.78), channel_id=1, source_target_pairs={{0,13},{1,12},{2,15},{3,14},{4,9},{5,8},{6,11},{7,10},{8,5},{9,4},... | collective-permute-start | bytes 786440 | tf_op jit(solution)/shard_map/ppermute | solution.py:260
  36.5 1.5 %collective-permute-start.1 = (bf16[8,16,1024]{2,1,0:T(8,128)(2,1)S(1)}, bf16[8,16,1024]{2,1,0:T(8,128)(2,1)S(1)}, u32[]{:S(2)}, u32[]{:S(2)}) collective-permute-start(bf16[8,16,1024]{2,1,0:T(8,128)(2,1)S(1)} %get-tuple-element.64), channel_id=1, source_target_pairs={{0,2},{1,3},{2,0},{3,1},{4,6},{5,7},{6,4},{7,5},{8,10},{9,11},{10,... | collective-permute-start | bytes 786440 | tf_op jit(solution)/shard_map/ppermute | solution.py:260
  38.0 0.0 collective-permute-done.refs_1_
  38.0 1.2 %collective-permute-start.15 = (bf16[8,16,1024]{2,1,0:T(8,128)(2,1)S(1)}, bf16[8,16,1024]{2,1,0:T(8,128)(2,1)S(1)}, u32[]{:S(2)}, u32[]{:S(2)}) collective-permute-start(bf16[8,16,1024]{2,1,0:T(8,128)(2,1)S(1)} %get-tuple-element.93), channel_id=1, source_target_pairs={{0,14},{1,15},{2,12},{3,13},{4,10},{5,11},{6,8},{7,9},{8,6},{9,7},... | collective-permute-start | bytes 786440 | tf_op jit(solution)/shard_map/ppermute | solution.py:260
  39.2 0.0 collective-permute-done.4.refs_9_
  39.2 14.6 %collective-permute-start.5 = (bf16[8,16,1024]{2,1,0:T(8,128)(2,1)S(1)}, bf16[8,16,1024]{2,1,0:T(8,128)(2,1)S(1)}, u32[]{:S(2)}, u32[]{:S(2)}) collective-permute-start(bf16[8,16,1024]{2,1,0:T(8,128)(2,1)S(1)} %get-tuple-element.73), channel_id=1, source_target_pairs={{0,4},{1,5},{2,6},{3,7},{4,0},{5,1},{6,2},{7,3},{8,12},{9,13},{10,... | collective-permute-start | bytes 786440 | tf_op jit(solution)/shard_map/ppermute | solution.py:260
  53.8 0.6 collective-permute-start.7
  54.4 1.6 %collective-permute-done.2.refs_3_ = bf16[8,16,1024]{2,1,0:T(8,128)(2,1)S(1)} collective-permute-done((bf16[8,16,1024]{2,1,0:T(8,128)(2,1)S(1)}, bf16[8,16,1024]{2,1,0:T(8,128)(2,1)S(1)}, u32[]{:S(2)}, u32[]{:S(2)}) %collective-permute-start.2) | collective-permute-done | bytes 262176 | tf_op jit(solution)/shard_map/ppermute | solution.py:260
  55.9 3.3 %collective-permute-start.10 = (bf16[8,16,640]{2,1,0:T(8,128)(2,1)S(1)}, bf16[8,16,640]{2,1,0:T(8,128)(2,1)S(1)}, u32[]{:S(2)}, u32[]{:S(2)}) collective-permute-start(bf16[8,16,640]{2,1,0:T(8,128)(2,1)S(1)} %get-tuple-element.84), channel_id=1, source_target_pairs={{0,8},{1,9},{2,10},{3,11},{4,12},{5,13},{6,14},{7,15},{8,0},{9,1},... | collective-permute-start | bytes 491528 | tf_op jit(solution)/shard_map/ppermute | solution.py:260
  59.2 0.1 collective-permute-start.12
  59.2 0.0 collective-permute-done.7.refs_10_
  59.3 3.9 %collective-permute-start.8 = (bf16[8,16,1024]{2,1,0:T(8,128)(2,1)S(1)}, bf16[8,16,1024]{2,1,0:T(8,128)(2,1)S(1)}, u32[]{:S(2)}, u32[]{:S(2)}) collective-permute-start(bf16[8,16,1024]{2,1,0:T(8,128)(2,1)S(1)} %get-tuple-element.80), channel_id=1, source_target_pairs={{0,5},{1,4},{2,7},{3,6},{4,1},{5,0},{6,3},{7,2},{8,13},{9,12},{10,... | collective-permute-start | bytes 786440 | tf_op jit(solution)/shard_map/ppermute | solution.py:260
  63.2 11.1 %collective-permute-done.10.refs_8_ = bf16[8,16,640]{2,1,0:T(8,128)(2,1)S(1)} collective-permute-done((bf16[8,16,640]{2,1,0:T(8,128)(2,1)S(1)}, bf16[8,16,640]{2,1,0:T(8,128)(2,1)S(1)}, u32[]{:S(2)}, u32[]{:S(2)}) %collective-permute-start.10) | collective-permute-done | bytes 163872 | tf_op jit(solution)/shard_map/ppermute | solution.py:260
  74.3 0.5 collective-permute-start.11
  74.8 1.2 %collective-permute-start.9 = (bf16[8,16,1024]{2,1,0:T(8,128)(2,1)S(1)}, bf16[8,16,1024]{2,1,0:T(8,128)(2,1)S(1)}, u32[]{:S(2)}, u32[]{:S(2)}) collective-permute-start(bf16[8,16,1024]{2,1,0:T(8,128)(2,1)S(1)} %get-tuple-element.82), channel_id=1, source_target_pairs={{0,6},{1,7},{2,4},{3,5},{4,2},{5,3},{6,0},{7,1},{8,14},{9,15},{10,... | collective-permute-start | bytes 786440 | tf_op jit(solution)/shard_map/ppermute | solution.py:260
  76.0 0.0 collective-permute-done.15.refs_14_
  76.0 2.1 %collective-permute-start.16 = (bf16[8,16,384]{2,1,0:T(8,128)(2,1)S(1)}, bf16[8,16,384]{2,1,0:T(8,128)(2,1)S(1)}, u32[]{:S(2)}, u32[]{:S(2)}) collective-permute-start(bf16[8,16,384]{2,1,0:T(8,128)(2,1)S(1)} %get-tuple-element.94), channel_id=1, source_target_pairs={{0,3},{1,2},{2,1},{3,0},{4,7},{5,6},{6,5},{7,4},{8,11},{9,10},{10,... | collective-permute-start | bytes 294920 | tf_op jit(solution)/shard_map/ppermute | solution.py:260
  78.1 7.4 %collective-permute-start.13 = (bf16[8,16,640]{2,1,0:T(8,128)(2,1)S(1)}, bf16[8,16,640]{2,1,0:T(8,128)(2,1)S(1)}, u32[]{:S(2)}, u32[]{:S(2)}) collective-permute-start(bf16[8,16,640]{2,1,0:T(8,128)(2,1)S(1)} %get-tuple-element.89), channel_id=1, source_target_pairs={{0,9},{1,8},{2,11},{3,10},{4,13},{5,12},{6,15},{7,14},{8,1},{9,0},... | collective-permute-start | bytes 491528 | tf_op jit(solution)/shard_map/ppermute | solution.py:260
  85.5 2.8 %collective-permute-done.16.refs_11_ = bf16[8,16,384]{2,1,0:T(8,128)(2,1)S(1)} collective-permute-done((bf16[8,16,384]{2,1,0:T(8,128)(2,1)S(1)}, bf16[8,16,384]{2,1,0:T(8,128)(2,1)S(1)}, u32[]{:S(2)}, u32[]{:S(2)}) %collective-permute-start.16) | collective-permute-done | bytes 98336 | tf_op jit(solution)/shard_map/ppermute | solution.py:260
  88.3 7.6 %collective-permute-start.17 = (bf16[8,16,640]{2,1,0:T(8,128)(2,1)S(1)}, bf16[8,16,640]{2,1,0:T(8,128)(2,1)S(1)}, u32[]{:S(2)}, u32[]{:S(2)}) collective-permute-start(bf16[8,16,640]{2,1,0:T(8,128)(2,1)S(1)} %get-tuple-element.95), channel_id=1, source_target_pairs={{0,10},{1,11},{2,8},{3,9},{4,14},{5,15},{6,12},{7,13},{8,2},{9,3},... | collective-permute-start | bytes 491528 | tf_op jit(solution)/shard_map/ppermute | solution.py:260
  95.9 0.0 collective-permute-done.8.refs_5_
  95.9 1.0 shard_map.61
  96.9 11.0 %collective-permute-done.17.refs_10_ = bf16[8,16,640]{2,1,0:T(8,128)(2,1)S(1)} collective-permute-done((bf16[8,16,640]{2,1,0:T(8,128)(2,1)S(1)}, bf16[8,16,640]{2,1,0:T(8,128)(2,1)S(1)}, u32[]{:S(2)}, u32[]{:S(2)}) %collective-permute-start.17) | collective-permute-done | bytes 163872 | tf_op jit(solution)/shard_map/ppermute | solution.py:260
  107.9 2.6 %collective-permute-done.18.refs_11_ = bf16[8,16,640]{2,1,0:T(8,128)(2,1)S(1)} collective-permute-done((bf16[8,16,640]{2,1,0:T(8,128)(2,1)S(1)}, bf16[8,16,640]{2,1,0:T(8,128)(2,1)S(1)}, u32[]{:S(2)}, u32[]{:S(2)}) %collective-permute-start.18) | collective-permute-done | bytes 163872 | tf_op jit(solution)/shard_map/ppermute | solution.py:260
  110.5 2.4 %shard_map.62 = (f32[8,2,128,128]{3,2,1,0:T(8,128)}, f32[8,1024]{1,0:T(8,128)}) custom-call(bf16[8,16,1024]{2,1,0:T(8,128)(2,1)S(1)} %get-tuple-element.59.refs_0_, bf16[8,16,1024]{2,1,0:T(8,128)(2,1)S(1)} %collective-permute-done.refs_1_, bf16[8,16,1024]{2,1,0:T(8,128)(2,1)S(1)} %collective-permute-done.1.refs_2_, ...), custom_call_target="tpu_custom_call" | custom-call | tf_op jit(solution)/shard_map/pallas_call | solution.py:228
  (12 shorter events, 0.1 us)
Async XLA Ops:
  5.4 21.6 %collective-permute-start.3 = (bf16[32,16,384]{2,1,0:T(8,128)(2,1)S(1)}, bf16[32,16,384]{2,1,0:T(8,128)(2,1)S(1)}, u32[]{:S(2)}, u32[]{:S(2)}) collective-permute-start(bf16[32,16,384]{2,1,0:T(8,128)(2,1)S(1)} %get-tuple-element.71), channel_id=1, source_target_pairs={{0,8},{1,9},{2,10},{3,11},{4,12},{5,13},{6,14},{7,15},{8,0},{9,1},... | collective-permute-start | bytes 1179656 | tf_op jit(solution)/shard_map/ppermute | solution.py:260
  23.2 14.8 %collective-permute-start = (bf16[8,16,1024]{2,1,0:T(8,128)(2,1)S(1)}, bf16[8,16,1024]{2,1,0:T(8,128)(2,1)S(1)}, u32[]{:S(2)}, u32[]{:S(2)}) collective-permute-start(bf16[8,16,1024]{2,1,0:T(8,128)(2,1)S(1)} %get-tuple-element.61), channel_id=1, source_target_pairs={{0,1},{1,0},{2,3},{3,2},{4,5},{5,4},{6,7},{7,6},{8,9},{9,8},{10,11... | collective-permute-start | bytes 786440 | tf_op jit(solution)/shard_map/ppermute | solution.py:260
  23.3 14.8 %collective-permute-start.14 = (bf16[8,16,1024]{2,1,0:T(8,128)(2,1)S(1)}, bf16[8,16,1024]{2,1,0:T(8,128)(2,1)S(1)}, u32[]{:S(2)}, u32[]{:S(2)}) collective-permute-start(bf16[8,16,1024]{2,1,0:T(8,128)(2,1)S(1)} %get-tuple-element.92), channel_id=1, source_target_pairs={{0,12},{1,13},{2,14},{3,15},{4,8},{5,9},{6,10},{7,11},{8,4},{9,5},... | collective-permute-start | bytes 786440 | tf_op jit(solution)/shard_map/ppermute | solution.py:260
  27.1 12.1 %collective-permute-start.4 = (bf16[8,16,384]{2,1,0:T(8,128)(2,1)S(1)}, bf16[8,16,384]{2,1,0:T(8,128)(2,1)S(1)}, u32[]{:S(2)}, u32[]{:S(2)}) collective-permute-start(bf16[8,16,384]{2,1,0:T(8,128)(2,1)S(1)} %slice.12), channel_id=1, source_target_pairs={{0,1},{1,0},{2,3},{3,2},{4,5},{5,4},{6,7},{7,6},{8,9},{9,8},{10,11... | collective-permute-start | bytes 294920 | tf_op jit(solution)/shard_map/ppermute | solution.py:260
  27.1 26.7 %collective-permute-start.6 = (bf16[8,16,1024]{2,1,0:T(8,128)(2,1)S(1)}, bf16[8,16,1024]{2,1,0:T(8,128)(2,1)S(1)}, u32[]{:S(2)}, u32[]{:S(2)}) collective-permute-start(bf16[8,16,1024]{2,1,0:T(8,128)(2,1)S(1)} %get-tuple-element.78), channel_id=1, source_target_pairs={{0,13},{1,12},{2,15},{3,14},{4,9},{5,8},{6,11},{7,10},{8,5},{9,4},... | collective-permute-start | bytes 786440 | tf_op jit(solution)/shard_map/ppermute | solution.py:260
  36.5 22.7 %collective-permute-start.1 = (bf16[8,16,1024]{2,1,0:T(8,128)(2,1)S(1)}, bf16[8,16,1024]{2,1,0:T(8,128)(2,1)S(1)}, u32[]{:S(2)}, u32[]{:S(2)}) collective-permute-start(bf16[8,16,1024]{2,1,0:T(8,128)(2,1)S(1)} %get-tuple-element.64), channel_id=1, source_target_pairs={{0,2},{1,3},{2,0},{3,1},{4,6},{5,7},{6,4},{7,5},{8,10},{9,11},{10,... | collective-permute-start | bytes 786440 | tf_op jit(solution)/shard_map/ppermute | solution.py:260
  38.0 17.9 %collective-permute-start.2 = (bf16[8,16,1024]{2,1,0:T(8,128)(2,1)S(1)}, bf16[8,16,1024]{2,1,0:T(8,128)(2,1)S(1)}, u32[]{:S(2)}, u32[]{:S(2)}) collective-permute-start(bf16[8,16,1024]{2,1,0:T(8,128)(2,1)S(1)} %get-tuple-element.67), channel_id=1, source_target_pairs={{0,3},{1,2},{2,1},{3,0},{4,7},{5,6},{6,5},{7,4},{8,11},{9,10},{10,... | collective-permute-start | bytes 786440 | tf_op jit(solution)/shard_map/ppermute | solution.py:260
  38.0 38.0 %collective-permute-start.15 = (bf16[8,16,1024]{2,1,0:T(8,128)(2,1)S(1)}, bf16[8,16,1024]{2,1,0:T(8,128)(2,1)S(1)}, u32[]{:S(2)}, u32[]{:S(2)}) collective-permute-start(bf16[8,16,1024]{2,1,0:T(8,128)(2,1)S(1)} %get-tuple-element.93), channel_id=1, source_target_pairs={{0,14},{1,15},{2,12},{3,13},{4,10},{5,11},{6,8},{7,9},{8,6},{9,7},... | collective-permute-start | bytes 786440 | tf_op jit(solution)/shard_map/ppermute | solution.py:260
  39.2 35.6 %collective-permute-start.5 = (bf16[8,16,1024]{2,1,0:T(8,128)(2,1)S(1)}, bf16[8,16,1024]{2,1,0:T(8,128)(2,1)S(1)}, u32[]{:S(2)}, u32[]{:S(2)}) collective-permute-start(bf16[8,16,1024]{2,1,0:T(8,128)(2,1)S(1)} %get-tuple-element.73), channel_id=1, source_target_pairs={{0,4},{1,5},{2,6},{3,7},{4,0},{5,1},{6,2},{7,3},{8,12},{9,13},{10,... | collective-permute-start | bytes 786440 | tf_op jit(solution)/shard_map/ppermute | solution.py:260
  53.8 5.5 %collective-permute-start.7 = (bf16[8,16,384]{2,1,0:T(8,128)(2,1)S(1)}, bf16[8,16,384]{2,1,0:T(8,128)(2,1)S(1)}, u32[]{:S(2)}, u32[]{:S(2)}) collective-permute-start(bf16[8,16,384]{2,1,0:T(8,128)(2,1)S(1)} %get-tuple-element.79), channel_id=1, source_target_pairs={{0,2},{1,3},{2,0},{3,1},{4,6},{5,7},{6,4},{7,5},{8,10},{9,11},{10,... | collective-permute-start | bytes 294920 | tf_op jit(solution)/shard_map/ppermute | solution.py:260
  55.9 18.3 %collective-permute-start.10 = (bf16[8,16,640]{2,1,0:T(8,128)(2,1)S(1)}, bf16[8,16,640]{2,1,0:T(8,128)(2,1)S(1)}, u32[]{:S(2)}, u32[]{:S(2)}) collective-permute-start(bf16[8,16,640]{2,1,0:T(8,128)(2,1)S(1)} %get-tuple-element.84), channel_id=1, source_target_pairs={{0,8},{1,9},{2,10},{3,11},{4,12},{5,13},{6,14},{7,15},{8,0},{9,1},... | collective-permute-start | bytes 491528 | tf_op jit(solution)/shard_map/ppermute | solution.py:260
  59.2 18.9 %collective-permute-start.12 = (bf16[8,16,1024]{2,1,0:T(8,128)(2,1)S(1)}, bf16[8,16,1024]{2,1,0:T(8,128)(2,1)S(1)}, u32[]{:S(2)}, u32[]{:S(2)}) collective-permute-start(bf16[8,16,1024]{2,1,0:T(8,128)(2,1)S(1)} %get-tuple-element.88), channel_id=1, source_target_pairs={{0,15},{1,14},{2,13},{3,12},{4,11},{5,10},{6,9},{7,8},{8,7},{9,6},... | collective-permute-start | bytes 786440 | tf_op jit(solution)/shard_map/ppermute | solution.py:260
  59.3 36.6 %collective-permute-start.8 = (bf16[8,16,1024]{2,1,0:T(8,128)(2,1)S(1)}, bf16[8,16,1024]{2,1,0:T(8,128)(2,1)S(1)}, u32[]{:S(2)}, u32[]{:S(2)}) collective-permute-start(bf16[8,16,1024]{2,1,0:T(8,128)(2,1)S(1)} %get-tuple-element.80), channel_id=1, source_target_pairs={{0,5},{1,4},{2,7},{3,6},{4,1},{5,0},{6,3},{7,2},{8,13},{9,12},{10,... | collective-permute-start | bytes 786440 | tf_op jit(solution)/shard_map/ppermute | solution.py:260
  74.3 21.6 %collective-permute-start.11 = (bf16[8,16,1024]{2,1,0:T(8,128)(2,1)S(1)}, bf16[8,16,1024]{2,1,0:T(8,128)(2,1)S(1)}, u32[]{:S(2)}, u32[]{:S(2)}) collective-permute-start(bf16[8,16,1024]{2,1,0:T(8,128)(2,1)S(1)} %get-tuple-element.85), channel_id=1, source_target_pairs={{0,7},{1,6},{2,5},{3,4},{4,3},{5,2},{6,1},{7,0},{8,15},{9,14},{10,... | collective-permute-start | bytes 786440 | tf_op jit(solution)/shard_map/ppermute | solution.py:260
  74.8 21.1 %collective-permute-start.9 = (bf16[8,16,1024]{2,1,0:T(8,128)(2,1)S(1)}, bf16[8,16,1024]{2,1,0:T(8,128)(2,1)S(1)}, u32[]{:S(2)}, u32[]{:S(2)}) collective-permute-start(bf16[8,16,1024]{2,1,0:T(8,128)(2,1)S(1)} %get-tuple-element.82), channel_id=1, source_target_pairs={{0,6},{1,7},{2,4},{3,5},{4,2},{5,3},{6,0},{7,1},{8,14},{9,15},{10,... | collective-permute-start | bytes 786440 | tf_op jit(solution)/shard_map/ppermute | solution.py:260
  76.0 12.3 %collective-permute-start.16 = (bf16[8,16,384]{2,1,0:T(8,128)(2,1)S(1)}, bf16[8,16,384]{2,1,0:T(8,128)(2,1)S(1)}, u32[]{:S(2)}, u32[]{:S(2)}) collective-permute-start(bf16[8,16,384]{2,1,0:T(8,128)(2,1)S(1)} %get-tuple-element.94), channel_id=1, source_target_pairs={{0,3},{1,2},{2,1},{3,0},{4,7},{5,6},{6,5},{7,4},{8,11},{9,10},{10,... | collective-permute-start | bytes 294920 | tf_op jit(solution)/shard_map/ppermute | solution.py:260
  78.1 18.8 %collective-permute-start.13 = (bf16[8,16,640]{2,1,0:T(8,128)(2,1)S(1)}, bf16[8,16,640]{2,1,0:T(8,128)(2,1)S(1)}, u32[]{:S(2)}, u32[]{:S(2)}) collective-permute-start(bf16[8,16,640]{2,1,0:T(8,128)(2,1)S(1)} %get-tuple-element.89), channel_id=1, source_target_pairs={{0,9},{1,8},{2,11},{3,10},{4,13},{5,12},{6,15},{7,14},{8,1},{9,0},... | collective-permute-start | bytes 491528 | tf_op jit(solution)/shard_map/ppermute | solution.py:260
  88.3 19.6 %collective-permute-start.17 = (bf16[8,16,640]{2,1,0:T(8,128)(2,1)S(1)}, bf16[8,16,640]{2,1,0:T(8,128)(2,1)S(1)}, u32[]{:S(2)}, u32[]{:S(2)}) collective-permute-start(bf16[8,16,640]{2,1,0:T(8,128)(2,1)S(1)} %get-tuple-element.95), channel_id=1, source_target_pairs={{0,10},{1,11},{2,8},{3,9},{4,14},{5,15},{6,12},{7,13},{8,2},{9,3},... | collective-permute-start | bytes 491528 | tf_op jit(solution)/shard_map/ppermute | solution.py:260
  95.9 14.6 %collective-permute-start.18 = (bf16[8,16,640]{2,1,0:T(8,128)(2,1)S(1)}, bf16[8,16,640]{2,1,0:T(8,128)(2,1)S(1)}, u32[]{:S(2)}, u32[]{:S(2)}) collective-permute-start(bf16[8,16,640]{2,1,0:T(8,128)(2,1)S(1)} %get-tuple-element.96), channel_id=1, source_target_pairs={{0,11},{1,10},{2,9},{3,8},{4,15},{5,14},{6,13},{7,12},{8,3},{9,2},... | collective-permute-start | bytes 491528 | tf_op jit(solution)/shard_map/ppermute | solution.py:260

commit v5 on v4

--- a/solution.py
+++ b/solution.py
@@ -16,7 +16,7 @@
 AXES = ("row", "col")
 LANES = 128
 FRAME_GROUP = 16
-TILE = 128
+TILE = 256
 VMEM = 40 * 1024 * 1024
 
 
@@ -162,7 +162,7 @@
     )(*inputs)
 
 
-def correlate_kernel(in_dev, blocks, start, count, chunks, *refs):
+def correlate_kernel(in_dev, blocks, places, start, count, chunks, *refs):
     parts = refs[:blocks]
     per_block = parts[0].shape[0]
     inputs = in_dev * blocks
@@ -184,8 +184,7 @@
     for channel in range(per_block):
         power = jnp.zeros((in_dev, count), jnp.float32)
         for other in range(blocks):
-            place = start if parts[other].shape[2] == SPECTRA else 0
-            wide = parts[other][channel, :, place : place + count].astype(jnp.float32)
+            wide = parts[other][channel, :, places[other] : places[other] + count].astype(jnp.float32)
             real_part, imag_part = wide[:in_dev], wide[in_dev:]
             power = power + (real_part * real_part + imag_part * imag_part)
             source = me ^ other
@@ -214,6 +213,7 @@
 
 
 def correlate(parts, start, count, blocks, before=None, chunks=(), beams=()):
+    parts, places = zip(*parts)
     per_block, rows, _ = parts[0].shape
     in_dev = rows // 2
     inputs = in_dev * blocks
@@ -226,7 +226,7 @@
     ]
     operands = [*parts, *([] if before is None else [before]), *beams]
     return pl.pallas_call(
-        functools.partial(correlate_kernel, in_dev, blocks, start, count, chunks),
+        functools.partial(correlate_kernel, in_dev, blocks, places, start, count, chunks),
         in_specs=[pl.BlockSpec(memory_space=pltpu.VMEM)] * len(operands),
         out_specs=[pl.BlockSpec(memory_space=space)] * 2,
         scratch_shapes=(staged if chunks else [])
@@ -239,8 +239,10 @@
     )(*operands)
 
 
-LEAD = 4
-LEAD_FRAMES = 384
+LEAD = 6
+LEAD_FRAMES = 256
+NEAR_ORDER = (4,5,1,2,6,3,7)
+NEARS_AHEAD = (0, 1, 1, 1, 2, 1, 1, 0)
 IN_FLIGHT = 5
 
 
@@ -255,8 +257,9 @@
 
     def send(target, block, other):
         if len(sent) >= IN_FLIGHT:
-            before = sent[-IN_FLIGHT]
-            block, taken[before] = lax.optimization_barrier((block, taken[before]))
+            before = sent[: 1 - IN_FLIGHT]
+            block, *held = lax.optimization_barrier((block, *(taken[key] for key in before)))
+            taken.update(zip(before, held))
         taken[target] = lax.ppermute(block, AXES, [(s, s ^ other) for s in range(blocks)])
         sent.append(target)
 
@@ -269,19 +272,26 @@
     targets = across + last + close
     ready = dict(zip(targets, make_spectra(made[1:], SPECTRA, in_dev, blocks, targets, False)))
     taken[close[0]] = ready[close[0]]
-    distant, others = across + last, close[1:]
-    handed = first[1:]
-    for index, target in enumerate(distant):
-        send(target, ready[target], target[0])
-        if index < len(others):
-            send(others[index], ready[others[index]], others[index][0])
-        if index >= 1 and index - 1 < len(handed):
-            offset = index * per_block
-            send(handed[index - 1], taken[first[0]][offset : offset + per_block], handed[index - 1][0] - half)
-
-    visibility, beam = correlate([taken[target] for target in close + first + across], 0, LEAD_FRAMES, blocks)
+    distant, others = list(across + last), [close[step] for step in NEAR_ORDER if step < half]
+    others += [target for target in close[1:] if target not in others]
+    order = []
+    for near_before in NEARS_AHEAD:
+        order += others[:near_before] + distant[:1]
+        others, distant = others[near_before:], distant[1:]
+    for target in order + others + distant:
+        block, step = ready[target], target[0]
+        if 0 < step < LEAD:
+            handed = taken[first[0]][step * per_block : (step + 1) * per_block]
+            block = jnp.concatenate([block, handed], axis=2)
+        send(target, block, step)
+
+    places = {first[0]: (taken[first[0]], 0)}
+    places.update((first[step], (taken[close[step]], SPECTRA)) for step in range(1, LEAD))
+    early = [(taken[target], 0) for target in close] + [places[target] for target in first]
+    late = [(taken[target], LEAD_FRAMES) for target in close] + [(taken[target], 0) for target in last]
+    visibility, beam = correlate(early + [(taken[target], 0) for target in across], 0, LEAD_FRAMES, blocks)
     visibility, beam = correlate(
-        [taken[target] for target in close + last + across], LEAD_FRAMES, SPECTRA - LEAD_FRAMES, blocks,
+        late + [(taken[target], LEAD_FRAMES) for target in across], LEAD_FRAMES, SPECTRA - LEAD_FRAMES, blocks,
         visibility, ((0, LEAD_FRAMES),), (beam,),
     )
     return (visibility[None], beam[None])

time: 113 us -> 102 us (0.903)
  the two profiles are of different devices: /device:TPU:0 before, /device:TPU:9 now
where the time goes in v5:
time: 102 us; the launch traced here: 101 us
  waiting for transfers between devices  48.4 us (47%)
  starting transfers between devices  33.3 us (33%)
  Pallas kernels  18.8 us (18%)
    ppermute x16, waiting for transfers between devices, send(): lax.ppermute(block, AXES, [(s, s ^ other) for s in range(blocks)])  48.4 us
    ppermute x16, starting transfers between devices, send(): lax.ppermute(block, AXES, [(s, s ^ other) for s in range(blocks)])  33.3 us
    pallas_call x2, Pallas kernels, make_spectra(): pl.pallas_call(kernel, in_specs=in_specs, out_specs=[vmem] * len(out_shap...  15.7 us
    pallas_call x2, Pallas kernels, correlate(): pl.pallas_call(functools.partial(correlate_kernel, in_dev, blocks, places...  3.1 us
  transfers between devices with their start and end apart: 16, of which 10 were waited for; matrix products, arithmetic and copies ran while one was open for 0% of the time, Pallas kernels for 13%

profile of v5, /device:TPU:9, one launch (start us, length us, event | category | flops | bytes accessed | tf_op | source)
XLA Modules:
  0.0 101.4 jit_solution(6871710066286720235)
XLA Ops:
  0.6 3.6 %shard_map.59 = (bf16[48,16,256]{2,1,0:T(8,128)(2,1)S(1)}, bf16[1031,8,256]{2,1,0:T(8,128)(2,1)S(1)}, f32[8,256]{1,0:T(8,128)S(1)}, bf16[256,256]{1,0:T(8,128)(2,1)S(1)}, s32[16]{0:T(128)S(1)}) custom-call(s32[16]{0:T(128)} %refs_0_.1, bf16[1031,8,256]{2,1,0:T(8,128)(2,1)} %bitcast.5, f32[8,256]{1,0:T(8,128)} %constant.4.clone.refs_2_, ...), custom_call_target="tpu_custom_call" | custom-call | tf_op jit(solution)/shard_map/pallas_call | solution.py:155
  4.2 2.4 %collective-permute-start = (bf16[48,16,256]{2,1,0:T(8,128)(2,1)S(1)}, bf16[48,16,256]{2,1,0:T(8,128)(2,1)S(1)}, u32[]{:S(2)}, u32[]{:S(2)}) collective-permute-start(bf16[48,16,256]{2,1,0:T(8,128)(2,1)S(1)} %get-tuple-element.120), channel_id=1, source_target_pairs={{0,8},{1,9},{2,10},{3,11},{4,12},{5,13},{6,14},{7,15},{8,0},{9,1},... | collective-permute-start | bytes 1179656 | tf_op jit(solution)/shard_map/ppermute | solution.py:263
  6.6 12.1 %shard_map.60 = (bf16[8,16,1024]{2,1,0:T(8,128)(2,1)S(1)}, bf16[8,16,1024]{2,1,0:T(8,128)(2,1)S(1)}, bf16[8,16,768]{2,1,0:T(8,128)(2,1)S(1)}, bf16[8,16,768]{2,1...) custom-call(bf16[1031,8,256]{2,1,0:T(8,128)(2,1)S(1)} %get-tuple-ele, ...), custom_call_target="tpu_custom_call" | custom-call | tf_op jit(solution)/shard_map/pallas_call | solution.py:155
  18.7 0.1 collective-permute-start.1
  18.8 3.5 %collective-permute-start.3 = (bf16[8,16,1024]{2,1,0:T(8,128)(2,1)S(1)}, bf16[8,16,1024]{2,1,0:T(8,128)(2,1)S(1)}, u32[]{:S(2)}, u32[]{:S(2)}) collective-permute-start(bf16[8,16,1024]{2,1,0:T(8,128)(2,1)S(1)} %get-tuple-element.129), channel_id=1, source_target_pairs={{0,15},{1,14},{2,13},{3,12},{4,11},{5,10},{6,9},{7,8},{8,7},{9,6},... | collective-permute-start | bytes 786440 | tf_op jit(solution)/shard_map/ppermute | solution.py:263
  22.3 12.7 %collective-permute-done.refs_8_ = bf16[48,16,256]{2,1,0:T(8,128)(2,1)S(1)} collective-permute-done((bf16[48,16,256]{2,1,0:T(8,128)(2,1)S(1)}, bf16[48,16,256]{2,1,0:T(8,128)(2,1)S(1)}, u32[]{:S(2)}, u32[]{:S(2)}) %collective-permute-start) | collective-permute-done | bytes 393248 | tf_op jit(solution)/shard_map/ppermute | solution.py:263
  35.0 0.1 collective-permute-start.2
  35.1 2.3 %collective-permute-start.4 = (bf16[8,16,1280]{2,1,0:T(8,128)(2,1)S(1)}, bf16[8,16,1280]{2,1,0:T(8,128)(2,1)S(1)}, u32[]{:S(2)}, u32[]{:S(2)}) collective-permute-start(bf16[8,16,1280]{2,1,0:T(8,128)(2,1)S(1)} %pad_maximum_fusion.3), channel_id=1, source_target_pairs={{0,5},{1,4},{2,7},{3,6},{4,1},{5,0},{6,3},{7,2},{8,13},{9,12},{10,... | collective-permute-start | bytes 983048 | tf_op jit(solution)/shard_map/ppermute | solution.py:263
  37.4 3.1 %collective-permute-done.1.refs_14_ = bf16[8,16,1024]{2,1,0:T(8,128)(2,1)S(1)} collective-permute-done((bf16[8,16,1024]{2,1,0:T(8,128)(2,1)S(1)}, bf16[8,16,1024]{2,1,0:T(8,128)(2,1)S(1)}, u32[]{:S(2)}, u32[]{:S(2)}) %collective-permute-start.1) | collective-permute-done | bytes 262176 | tf_op jit(solution)/shard_map/ppermute | solution.py:263
  40.6 0.0 collective-permute-start.5
  40.6 2.5 %collective-permute-start.6 = (bf16[8,16,1280]{2,1,0:T(8,128)(2,1)S(1)}, bf16[8,16,1280]{2,1,0:T(8,128)(2,1)S(1)}, u32[]{:S(2)}, u32[]{:S(2)}) collective-permute-start(bf16[8,16,1280]{2,1,0:T(8,128)(2,1)S(1)} %pad_maximum_fusion), channel_id=1, source_target_pairs={{0,1},{1,0},{2,3},{3,2},{4,5},{5,4},{6,7},{7,6},{8,9},{9,8},{10,11... | collective-permute-start | bytes 983048 | tf_op jit(solution)/shard_map/ppermute | solution.py:263
  43.0 0.7 collective-permute-done.2.refs_4_.refs_12_
  43.7 4.2 %collective-permute-done.3.refs_15_ = bf16[8,16,1024]{2,1,0:T(8,128)(2,1)S(1)} collective-permute-done((bf16[8,16,1024]{2,1,0:T(8,128)(2,1)S(1)}, bf16[8,16,1024]{2,1,0:T(8,128)(2,1)S(1)}, u32[]{:S(2)}, u32[]{:S(2)}) %collective-permute-start.3) | collective-permute-done | bytes 262176 | tf_op jit(solution)/shard_map/ppermute | solution.py:263
  48.0 0.0 collective-permute-start.8
  48.0 2.9 %collective-permute-start.7 = (bf16[8,16,768]{2,1,0:T(8,128)(2,1)S(1)}, bf16[8,16,768]{2,1,0:T(8,128)(2,1)S(1)}, u32[]{:S(2)}, u32[]{:S(2)}) collective-permute-start(bf16[8,16,768]{2,1,0:T(8,128)(2,1)S(1)} %get-tuple-element.155), channel_id=1, source_target_pairs={{0,9},{1,8},{2,11},{3,10},{4,13},{5,12},{6,15},{7,14},{8,1},{9,0},... | collective-permute-start | bytes 589832 | tf_op jit(solution)/shard_map/ppermute | solution.py:263
  50.8 1.7 %collective-permute-done.4.refs_5_.refs_13_ = bf16[8,16,1280]{2,1,0:T(8,128)(2,1)S(1)} collective-permute-done((bf16[8,16,1280]{2,1,0:T(8,128)(2,1)S(1)}, bf16[8,16,1280]{2,1,0:T(8,128)(2,1)S(1)}, u32[]{:S(2)}, u32[]{:S(2)}) %collective-permute-start.4) | collective-permute-done | bytes 327712 | tf_op jit(solution)/shard_map/ppermute | solution.py:263
  52.6 4.4 %collective-permute-done.5.refs_8_ = bf16[8,16,768]{2,1,0:T(8,128)(2,1)S(1)} collective-permute-done((bf16[8,16,768]{2,1,0:T(8,128)(2,1)S(1)}, bf16[8,16,768]{2,1,0:T(8,128)(2,1)S(1)}, u32[]{:S(2)}, u32[]{:S(2)}) %collective-permute-start.5) | collective-permute-done | bytes 196640 | tf_op jit(solution)/shard_map/ppermute | solution.py:263
  57.0 3.5 %collective-permute-start.10 = (bf16[8,16,768]{2,1,0:T(8,128)(2,1)S(1)}, bf16[8,16,768]{2,1,0:T(8,128)(2,1)S(1)}, u32[]{:S(2)}, u32[]{:S(2)}) collective-permute-start(bf16[8,16,768]{2,1,0:T(8,128)(2,1)S(1)} %get-tuple-element.185), channel_id=1, source_target_pairs={{0,10},{1,11},{2,8},{3,9},{4,14},{5,15},{6,12},{7,13},{8,2},{9,3},... | collective-permute-start | bytes 589832 | tf_op jit(solution)/shard_map/ppermute | solution.py:263
  60.5 0.0 collective-permute-start.9
  60.5 0.0 collective-permute-done.6.refs_1_.refs_9_
  60.5 2.5 %collective-permute-start.11 = (bf16[8,16,1280]{2,1,0:T(8,128)(2,1)S(1)}, bf16[8,16,1280]{2,1,0:T(8,128)(2,1)S(1)}, u32[]{:S(2)}, u32[]{:S(2)}) collective-permute-start(bf16[8,16,1280]{2,1,0:T(8,128)(2,1)S(1)} %pad_maximum_fusion.4), channel_id=1, source_target_pairs={{0,3},{1,2},{2,1},{3,0},{4,7},{5,6},{6,5},{7,4},{8,11},{9,10},{10,... | collective-permute-start | bytes 983048 | tf_op jit(solution)/shard_map/ppermute | solution.py:263
  63.0 4.0 %collective-permute-done.7.refs_9_ = bf16[8,16,768]{2,1,0:T(8,128)(2,1)S(1)} collective-permute-done((bf16[8,16,768]{2,1,0:T(8,128)(2,1)S(1)}, bf16[8,16,768]{2,1,0:T(8,128)(2,1)S(1)}, u32[]{:S(2)}, u32[]{:S(2)}) %collective-permute-start.7) | collective-permute-done | bytes 196640 | tf_op jit(solution)/shard_map/ppermute | solution.py:263
  67.0 0.0 collective-permute-done.8.refs_2_.refs_10_
  67.0 5.9 %collective-permute-start.12 = (bf16[8,16,1024]{2,1,0:T(8,128)(2,1)S(1)}, bf16[8,16,1024]{2,1,0:T(8,128)(2,1)S(1)}, u32[]{:S(2)}, u32[]{:S(2)}) collective-permute-start(bf16[8,16,1024]{2,1,0:T(8,128)(2,1)S(1)} %get-tuple-element.192), channel_id=1, source_target_pairs={{0,7},{1,6},{2,5},{3,4},{4,3},{5,2},{6,1},{7,0},{8,15},{9,14},{10,... | collective-permute-start | bytes 786440 | tf_op jit(solution)/shard_map/ppermute | solution.py:263
  72.9 0.0 collective-permute-start.13
  72.9 7.8 %collective-permute-start.15 = (bf16[8,16,768]{2,1,0:T(8,128)(2,1)S(1)}, bf16[8,16,768]{2,1,0:T(8,128)(2,1)S(1)}, u32[]{:S(2)}, u32[]{:S(2)}) collective-permute-start(bf16[8,16,768]{2,1,0:T(8,128)(2,1)S(1)} %get-tuple-element.198), channel_id=1, source_target_pairs={{0,13},{1,12},{2,15},{3,14},{4,9},{5,8},{6,11},{7,10},{8,5},{9,4},... | collective-permute-start | bytes 589832 | tf_op jit(solution)/shard_map/ppermute | solution.py:263
  80.7 0.0 collective-permute-start.14
  80.7 8.9 %collective-permute-done.11.refs_3_.refs_11_ = bf16[8,16,1280]{2,1,0:T(8,128)(2,1)S(1)} collective-permute-done((bf16[8,16,1280]{2,1,0:T(8,128)(2,1)S(1)}, bf16[8,16,1280]{2,1,0:T(8,128)(2,1)S(1)}, u32[]{:S(2)}, u32[]{:S(2)}) %collective-permute-start.11) | collective-permute-done | bytes 327712 | tf_op jit(solution)/shard_map/ppermute | solution.py:263
  89.6 0.6 shard_map.61
  90.2 4.5 %collective-permute-done.15.refs_13_ = bf16[8,16,768]{2,1,0:T(8,128)(2,1)S(1)} collective-permute-done((bf16[8,16,768]{2,1,0:T(8,128)(2,1)S(1)}, bf16[8,16,768]{2,1,0:T(8,128)(2,1)S(1)}, u32[]{:S(2)}, u32[]{:S(2)}) %collective-permute-start.15) | collective-permute-done | bytes 196640 | tf_op jit(solution)/shard_map/ppermute | solution.py:263
  94.7 4.2 %collective-permute-done.14.refs_12_ = bf16[8,16,768]{2,1,0:T(8,128)(2,1)S(1)} collective-permute-done((bf16[8,16,768]{2,1,0:T(8,128)(2,1)S(1)}, bf16[8,16,768]{2,1,0:T(8,128)(2,1)S(1)}, u32[]{:S(2)}, u32[]{:S(2)}) %collective-permute-start.14) | collective-permute-done | bytes 196640 | tf_op jit(solution)/shard_map/ppermute | solution.py:263
  98.9 2.5 %shard_map.62 = (f32[8,2,128,128]{3,2,1,0:T(8,128)}, f32[8,1024]{1,0:T(8,128)}) custom-call(bf16[8,16,1024]{2,1,0:T(8,128)(2,1)S(1)} %get-tuple-element.108.refs_0_, bf16[8,16,1280]{2,1,0:T(8,128)(2,1)S(1)} %collective-permute-done.6.refs_1_.refs_9_, bf16[8,16,1280]{2,1,0:T(8,128)(2,1)S(1)} %collective-permute-done.8.refs_2_.refs_10_, ...), custom_call_target="tpu_custom_call" | custom-call | tf_op jit(solution)/shard_map/pallas_call | solution.py:228
  (13 shorter events, 0.2 us)
Async XLA Ops:
  4.2 30.8 %collective-permute-start = (bf16[48,16,256]{2,1,0:T(8,128)(2,1)S(1)}, bf16[48,16,256]{2,1,0:T(8,128)(2,1)S(1)}, u32[]{:S(2)}, u32[]{:S(2)}) collective-permute-start(bf16[48,16,256]{2,1,0:T(8,128)(2,1)S(1)} %get-tuple-element.120), channel_id=1, source_target_pairs={{0,8},{1,9},{2,10},{3,11},{4,12},{5,13},{6,14},{7,15},{8,0},{9,1},... | collective-permute-start | bytes 1179656 | tf_op jit(solution)/shard_map/ppermute | solution.py:263
  18.7 21.9 %collective-permute-start.1 = (bf16[8,16,1024]{2,1,0:T(8,128)(2,1)S(1)}, bf16[8,16,1024]{2,1,0:T(8,128)(2,1)S(1)}, u32[]{:S(2)}, u32[]{:S(2)}) collective-permute-start(bf16[8,16,1024]{2,1,0:T(8,128)(2,1)S(1)} %get-tuple-element.122), channel_id=1, source_target_pairs={{0,14},{1,15},{2,12},{3,13},{4,10},{5,11},{6,8},{7,9},{8,6},{9,7},... | collective-permute-start | bytes 786440 | tf_op jit(solution)/shard_map/ppermute | solution.py:263
  18.8 29.2 %collective-permute-start.3 = (bf16[8,16,1024]{2,1,0:T(8,128)(2,1)S(1)}, bf16[8,16,1024]{2,1,0:T(8,128)(2,1)S(1)}, u32[]{:S(2)}, u32[]{:S(2)}) collective-permute-start(bf16[8,16,1024]{2,1,0:T(8,128)(2,1)S(1)} %get-tuple-element.129), channel_id=1, source_target_pairs={{0,15},{1,14},{2,13},{3,12},{4,11},{5,10},{6,9},{7,8},{8,7},{9,6},... | collective-permute-start | bytes 786440 | tf_op jit(solution)/shard_map/ppermute | solution.py:263
  35.0 8.7 %collective-permute-start.2 = (bf16[8,16,1280]{2,1,0:T(8,128)(2,1)S(1)}, bf16[8,16,1280]{2,1,0:T(8,128)(2,1)S(1)}, u32[]{:S(2)}, u32[]{:S(2)}) collective-permute-start(bf16[8,16,1280]{2,1,0:T(8,128)(2,1)S(1)} %pad_maximum_fusion.1), channel_id=1, source_target_pairs={{0,4},{1,5},{2,6},{3,7},{4,0},{5,1},{6,2},{7,3},{8,12},{9,13},{10,... | collective-permute-start | bytes 983048 | tf_op jit(solution)/shard_map/ppermute | solution.py:263
  35.1 17.5 %collective-permute-start.4 = (bf16[8,16,1280]{2,1,0:T(8,128)(2,1)S(1)}, bf16[8,16,1280]{2,1,0:T(8,128)(2,1)S(1)}, u32[]{:S(2)}, u32[]{:S(2)}) collective-permute-start(bf16[8,16,1280]{2,1,0:T(8,128)(2,1)S(1)} %pad_maximum_fusion.3), channel_id=1, source_target_pairs={{0,5},{1,4},{2,7},{3,6},{4,1},{5,0},{6,3},{7,2},{8,13},{9,12},{10,... | collective-permute-start | bytes 983048 | tf_op jit(solution)/shard_map/ppermute | solution.py:263
  40.6 16.4 %collective-permute-start.5 = (bf16[8,16,768]{2,1,0:T(8,128)(2,1)S(1)}, bf16[8,16,768]{2,1,0:T(8,128)(2,1)S(1)}, u32[]{:S(2)}, u32[]{:S(2)}) collective-permute-start(bf16[8,16,768]{2,1,0:T(8,128)(2,1)S(1)} %get-tuple-element.140), channel_id=1, source_target_pairs={{0,8},{1,9},{2,10},{3,11},{4,12},{5,13},{6,14},{7,15},{8,0},{9,1},... | collective-permute-start | bytes 589832 | tf_op jit(solution)/shard_map/ppermute | solution.py:263
  40.6 20.0 %collective-permute-start.6 = (bf16[8,16,1280]{2,1,0:T(8,128)(2,1)S(1)}, bf16[8,16,1280]{2,1,0:T(8,128)(2,1)S(1)}, u32[]{:S(2)}, u32[]{:S(2)}) collective-permute-start(bf16[8,16,1280]{2,1,0:T(8,128)(2,1)S(1)} %pad_maximum_fusion), channel_id=1, source_target_pairs={{0,1},{1,0},{2,3},{3,2},{4,5},{5,4},{6,7},{7,6},{8,9},{9,8},{10,11... | collective-permute-start | bytes 983048 | tf_op jit(solution)/shard_map/ppermute | solution.py:263
  48.0 19.1 %collective-permute-start.8 = (bf16[8,16,1280]{2,1,0:T(8,128)(2,1)S(1)}, bf16[8,16,1280]{2,1,0:T(8,128)(2,1)S(1)}, u32[]{:S(2)}, u32[]{:S(2)}) collective-permute-start(bf16[8,16,1280]{2,1,0:T(8,128)(2,1)S(1)} %pad_maximum_fusion.2), channel_id=1, source_target_pairs={{0,2},{1,3},{2,0},{3,1},{4,6},{5,7},{6,4},{7,5},{8,10},{9,11},{10,... | collective-permute-start | bytes 983048 | tf_op jit(solution)/shard_map/ppermute | solution.py:263
  48.0 19.1 %collective-permute-start.7 = (bf16[8,16,768]{2,1,0:T(8,128)(2,1)S(1)}, bf16[8,16,768]{2,1,0:T(8,128)(2,1)S(1)}, u32[]{:S(2)}, u32[]{:S(2)}) collective-permute-start(bf16[8,16,768]{2,1,0:T(8,128)(2,1)S(1)} %get-tuple-element.155), channel_id=1, source_target_pairs={{0,9},{1,8},{2,11},{3,10},{4,13},{5,12},{6,15},{7,14},{8,1},{9,0},... | collective-permute-start | bytes 589832 | tf_op jit(solution)/shard_map/ppermute | solution.py:263
  57.0 15.9 %collective-permute-start.10 = (bf16[8,16,768]{2,1,0:T(8,128)(2,1)S(1)}, bf16[8,16,768]{2,1,0:T(8,128)(2,1)S(1)}, u32[]{:S(2)}, u32[]{:S(2)}) collective-permute-start(bf16[8,16,768]{2,1,0:T(8,128)(2,1)S(1)} %get-tuple-element.185), channel_id=1, source_target_pairs={{0,10},{1,11},{2,8},{3,9},{4,14},{5,15},{6,12},{7,13},{8,2},{9,3},... | collective-permute-start | bytes 589832 | tf_op jit(solution)/shard_map/ppermute | solution.py:263
  60.5 12.4 %collective-permute-start.9 = (bf16[8,16,1024]{2,1,0:T(8,128)(2,1)S(1)}, bf16[8,16,1024]{2,1,0:T(8,128)(2,1)S(1)}, u32[]{:S(2)}, u32[]{:S(2)}) collective-permute-start(bf16[8,16,1024]{2,1,0:T(8,128)(2,1)S(1)} %get-tuple-element.174), channel_id=1, source_target_pairs={{0,6},{1,7},{2,4},{3,5},{4,2},{5,3},{6,0},{7,1},{8,14},{9,15},{10,... | collective-permute-start | bytes 786440 | tf_op jit(solution)/shard_map/ppermute | solution.py:263
  60.5 29.1 %collective-permute-start.11 = (bf16[8,16,1280]{2,1,0:T(8,128)(2,1)S(1)}, bf16[8,16,1280]{2,1,0:T(8,128)(2,1)S(1)}, u32[]{:S(2)}, u32[]{:S(2)}) collective-permute-start(bf16[8,16,1280]{2,1,0:T(8,128)(2,1)S(1)} %pad_maximum_fusion.4), channel_id=1, source_target_pairs={{0,3},{1,2},{2,1},{3,0},{4,7},{5,6},{6,5},{7,4},{8,11},{9,10},{10,... | collective-permute-start | bytes 983048 | tf_op jit(solution)/shard_map/ppermute | solution.py:263
  67.0 22.6 %collective-permute-start.12 = (bf16[8,16,1024]{2,1,0:T(8,128)(2,1)S(1)}, bf16[8,16,1024]{2,1,0:T(8,128)(2,1)S(1)}, u32[]{:S(2)}, u32[]{:S(2)}) collective-permute-start(bf16[8,16,1024]{2,1,0:T(8,128)(2,1)S(1)} %get-tuple-element.192), channel_id=1, source_target_pairs={{0,7},{1,6},{2,5},{3,4},{4,3},{5,2},{6,1},{7,0},{8,15},{9,14},{10,... | collective-permute-start | bytes 786440 | tf_op jit(solution)/shard_map/ppermute | solution.py:263
  72.9 17.3 %collective-permute-start.13 = (bf16[8,16,768]{2,1,0:T(8,128)(2,1)S(1)}, bf16[8,16,768]{2,1,0:T(8,128)(2,1)S(1)}, u32[]{:S(2)}, u32[]{:S(2)}) collective-permute-start(bf16[8,16,768]{2,1,0:T(8,128)(2,1)S(1)} %get-tuple-element.196), channel_id=1, source_target_pairs={{0,11},{1,10},{2,9},{3,8},{4,15},{5,14},{6,13},{7,12},{8,3},{9,2},... | collective-permute-start | bytes 589832 | tf_op jit(solution)/shard_map/ppermute | solution.py:263
  72.9 21.8 %collective-permute-start.15 = (bf16[8,16,768]{2,1,0:T(8,128)(2,1)S(1)}, bf16[8,16,768]{2,1,0:T(8,128)(2,1)S(1)}, u32[]{:S(2)}, u32[]{:S(2)}) collective-permute-start(bf16[8,16,768]{2,1,0:T(8,128)(2,1)S(1)} %get-tuple-element.198), channel_id=1, source_target_pairs={{0,13},{1,12},{2,15},{3,14},{4,9},{5,8},{6,11},{7,10},{8,5},{9,4},... | collective-permute-start | bytes 589832 | tf_op jit(solution)/shard_map/ppermute | solution.py:263
  80.7 18.2 %collective-permute-start.14 = (bf16[8,16,768]{2,1,0:T(8,128)(2,1)S(1)}, bf16[8,16,768]{2,1,0:T(8,128)(2,1)S(1)}, u32[]{:S(2)}, u32[]{:S(2)}) collective-permute-start(bf16[8,16,768]{2,1,0:T(8,128)(2,1)S(1)} %get-tuple-element.197), channel_id=1, source_target_pairs={{0,12},{1,13},{2,14},{3,15},{4,8},{5,9},{6,10},{7,11},{8,4},{9,5},... | collective-permute-start | bytes 589832 | tf_op jit(solution)/shard_map/ppermute | solution.py:263

commit v6 on v5

--- a/solution.py
+++ b/solution.py
@@ -16,6 +16,7 @@
 AXES = ("row", "col")
 LANES = 128
 FRAME_GROUP = 16
+FIRST_TILE = 128
 TILE = 256
 VMEM = 40 * 1024 * 1024
 
@@ -35,11 +36,13 @@
     freqs = np.arange(CHANS)
     phase = 2 * math.pi * ((freqs[:, None] * times[None, :]) % LENGTH) / LENGTH
     table = np.concatenate([np.cos(phase), -np.sin(phase)], 0) / math.sqrt(LENGTH)
-    return table.astype(np.float32).astype(jnp.bfloat16)
-
-
-def spectra_tile(start, first_row, in_dev, targets, base_of, outs, frames, window, fourier, filtered, spectra):
-    @pl.loop(0, TILE // FRAME_GROUP)
+    return table.astype(np.float32).astype(jnp.bfloat16).astype(np.float32)
+
+
+def spectra_tile(start, in_dev, targets, base_of, outs, frames, window, fourier, filtered, spectra):
+    tile = filtered.shape[1] // in_dev
+
+    @pl.loop(0, tile // FRAME_GROUP)
     def _(group):
         first = start + group * FRAME_GROUP
         for half in range(LENGTH // LANES):
@@ -52,26 +55,27 @@
                 FRAME_GROUP * in_dev, LANES
             )
 
-    first_row()
+    table = fourier()
+    height = table.shape[0]
     for i in range(in_dev):
         rows = jnp.concatenate(
-            [filtered[half, pl.ds(i, TILE, stride=in_dev), :] for half in range(LENGTH // LANES)], axis=1
+            [filtered[half, pl.ds(i, tile, stride=in_dev), :] for half in range(LENGTH // LANES)], axis=1
         ).astype(jnp.bfloat16)
         product = lax.dot_general(
-            fourier[...], rows, (((1,), (1,)), ((), ())), preferred_element_type=jnp.float32
+            table, rows, (((1,), (1,)), ((), ())), preferred_element_type=jnp.float32
         )
-        for part in range(TILE // LANES):
-            spectra[part, pl.ds(i * 2 * CHANS, 2 * CHANS), :] = product[:, part * LANES : (part + 1) * LANES]
+        for part in range(tile // LANES):
+            spectra[part, pl.ds(i * height, height), :] = product[:, part * LANES : (part + 1) * LANES]
     for (other, low, width), out in zip(targets, outs):
         if not low <= start < low + width:
             continue
-        base = base_of(other)
+        bases = base_of(other)
         offset = start - low
         for channel in range(out.shape[0]):
-            for part in range(TILE // LANES):
+            for part in range(tile // LANES):
                 pair = [
-                    spectra[part, pl.ds(base + plane * CHANS + channel, in_dev, stride=2 * CHANS), :]
-                    for plane in range(2)
+                    spectra[part, pl.ds(base + channel, in_dev, stride=height), :]
+                    for base in bases
                 ]
                 out[channel, :, offset + part * LANES : offset + (part + 1) * LANES] = jnp.concatenate(
                     pair, axis=0
@@ -84,12 +88,13 @@
     outs = [refs[4].at[pl.ds(index * per_block, per_block)] for index in range(len(targets))]
     frames, window, fourier, owner_held, filtered, spectra, owner, arrived = refs[5:]
     me = lax.axis_index(AXES)
+    aligned, order = per_block % 8 == 0, [other for other, _, _ in targets]
     needed, total = count + TAPS - 1, SPECTRA + TAPS - 1
     window_copy = pltpu.make_async_copy(window_in, window, arrived.at[0])
     fourier_copy = pltpu.make_async_copy(fourier_in, fourier, arrived.at[1])
     owner_copy = pltpu.make_async_copy(owner_in, owner, arrived.at[2])
     held_copy = pltpu.make_async_copy(owner_in, owner_held, arrived.at[3])
-    edges = sorted({0, TILE + TAPS - 1, needed, total})
+    edges = sorted({0, FIRST_TILE + TAPS - 1, needed, total})
     frame_copies = [
         pltpu.make_async_copy(frames_in.at[pl.ds(low, high - low)], frames.at[pl.ds(low, high - low)], arrived.at[4 + index])
         for index, (low, high) in enumerate(zip(edges, edges[1:]))
@@ -98,19 +103,32 @@
     for copy in copies:
         copy.start()
     window_copy.wait()
-    for start in range(0, count, TILE):
-        if start < 2 * TILE:
-            frame_copies[start // TILE].wait()
-
-        def tables_here():
+    for start in range(0, count, FIRST_TILE):
+        if start < 2 * FIRST_TILE:
+            frame_copies[start // FIRST_TILE].wait()
+
+        def needed_rows():
             if start == 0:
                 fourier_copy.wait()
                 owner_copy.wait()
-
-        spectra_tile(
-            start, tables_here, in_dev, targets, lambda other: owner[me ^ other] * (CHANS // blocks),
-            outs, frames, window, fourier, filtered, spectra,
-        )
+            if not aligned:
+                return fourier[...].astype(jnp.bfloat16)
+            return jnp.concatenate(
+                [
+                    fourier[pl.ds(pl.multiple_of(owner[me ^ other] * per_block + plane * CHANS, per_block), per_block), :]
+                    for other, _, _ in targets
+                    for plane in range(2)
+                ],
+                axis=0,
+            ).astype(jnp.bfloat16)
+
+        def base_of(other):
+            if aligned:
+                index = order.index(other)
+                return 2 * index * per_block, (2 * index + 1) * per_block
+            return tuple(owner[me ^ other] * per_block + plane * CHANS for plane in range(2))
+
+        spectra_tile(start, in_dev, targets, base_of, outs, frames, window, needed_rows, filtered, spectra)
     held_copy.wait()
     frame_copies[-1].wait()
 
@@ -123,10 +141,13 @@
     owner_copy = pltpu.make_async_copy(owner_held, owner, arrived.at[0])
     owner_copy.start()
     owner_copy.wait()
+
+    def base_of(other):
+        return tuple(owner[me ^ other] * (CHANS // blocks) + plane * CHANS for plane in range(2))
+
     for start in range(0, count, TILE):
         spectra_tile(
-            start, lambda: None, in_dev, targets, lambda other: owner[me ^ other] * (CHANS // blocks),
-            outs, frames, window, fourier, filtered, spectra,
+            start, in_dev, targets, base_of, outs, frames, window, lambda: fourier[...].astype(jnp.bfloat16), filtered, spectra
         )
 
 
@@ -135,9 +156,10 @@
     rows = 2 * in_dev
     vmem, hbm = pl.BlockSpec(memory_space=pltpu.VMEM), pl.BlockSpec(memory_space=pltpu.HBM)
     out_shape = [jax.ShapeDtypeStruct((per_block, rows, width), jnp.bfloat16) for _, _, width in targets]
+    tile = FIRST_TILE if first else TILE
     scratch = [
-        pltpu.VMEM((LENGTH // LANES, TILE * in_dev, LANES), jnp.float32),
-        pltpu.VMEM((TILE // LANES, in_dev * 2 * CHANS, LANES), jnp.float32),
+        pltpu.VMEM((LENGTH // LANES, tile * in_dev, LANES), jnp.float32),
+        pltpu.VMEM((tile // LANES, in_dev * 2 * CHANS, LANES), jnp.float32),
         pltpu.SMEM((blocks,), jnp.int32),
     ]
     if first:
@@ -147,7 +169,7 @@
         out_shape += [jax.ShapeDtypeStruct(x.shape, x.dtype) for x in (frames, window, fourier, owner_block)]
         in_specs = [hbm] * 4
         inputs = [pltpu.with_memory_space_constraint(x, pltpu.HBM) for x in inputs]
-        scratch.append(pltpu.SemaphoreType.DMA((7,)))
+        scratch.append(pltpu.SemaphoreType.DMA((8,)))
     else:
         kernel = functools.partial(spectra_kernel, count, in_dev, blocks, targets)
         in_specs = [vmem] * 4
@@ -181,31 +203,41 @@
         before = refs[blocks] if len(refs) == blocks + 3 + per_block else None
         visibility, beam = refs[-per_block - 2 : -per_block]
         planes = refs[-per_block:]
-    for channel in range(per_block):
+    def leave(channel):
+        return pltpu.make_async_copy(visibility.at[channel], visibility_out.at[channel], left.at[channel])
+
+    def arrange(channel, odd):
         power = jnp.zeros((in_dev, count), jnp.float32)
-        for other in range(blocks):
-            wide = parts[other][channel, :, places[other] : places[other] + count].astype(jnp.float32)
-            real_part, imag_part = wide[:in_dev], wide[in_dev:]
-            power = power + (real_part * real_part + imag_part * imag_part)
-            source = me ^ other
-            planes[channel][0, source] = real_part
-            planes[channel][1, source] = imag_part
+        for pair in range(blocks // 2):
+            halves = []
+            for other in (2 * pair + odd, 2 * pair + 1 - odd):
+                wide = parts[other][channel, :, places[other] : places[other] + count].astype(jnp.float32)
+                real_part, imag_part = wide[:in_dev], wide[in_dev:]
+                power = power + (real_part * real_part + imag_part * imag_part)
+                halves.append((real_part, imag_part))
+            for plane, values in enumerate(zip(*halves)):
+                planes[channel][plane, (me // 2) ^ pair] = jnp.concatenate(values, axis=0).astype(jnp.bfloat16)
         beam[channel : channel + 1, :] = jnp.sum(power, axis=0, keepdims=True) * (1.0 / inputs)
-        both = planes[channel][...].reshape(2 * inputs, count).astype(jnp.bfloat16)
-        gram = lax.dot_general(both, both, (((1,), (1,)), ((), ())), preferred_element_type=jnp.float32)
-        straight = (gram[:inputs, :inputs] + gram[inputs:, inputs:]) * (1.0 / SPECTRA)
-        crossed = (gram[inputs:, :inputs] - gram[:inputs, inputs:]) * (1.0 / SPECTRA)
-        if before is not None:
-            straight = before[channel, 0] + straight
-            crossed = before[channel, 1] + crossed
-        visibility[channel, 0] = straight
-        visibility[channel, 1] = crossed
-        if chunks:
-            copies.append(
-                pltpu.make_async_copy(visibility.at[channel], visibility_out.at[channel], left.at[channel])
-            )
-            copies[-1].start()
+
+    for odd in range(2):
+
+        @pl.when(me % 2 == odd)
+        def _():
+            for channel in range(per_block):
+                arrange(channel, odd)
+                both = planes[channel][...].reshape(2 * inputs, count)
+                gram = lax.dot_general(both, both, (((1,), (1,)), ((), ())), preferred_element_type=jnp.float32)
+                straight = (gram[:inputs, :inputs] + gram[inputs:, inputs:]) * (1.0 / SPECTRA)
+                crossed = (gram[inputs:, :inputs] - gram[:inputs, inputs:]) * (1.0 / SPECTRA)
+                if before is not None:
+                    straight = before[channel, 0] + straight
+                    crossed = before[channel, 1] + crossed
+                visibility[channel, 0] = straight
+                visibility[channel, 1] = crossed
+                if chunks:
+                    leave(channel).start()
     if chunks:
+        copies += [leave(channel) for channel in range(per_block)]
         copies.append(pltpu.make_async_copy(beam, beam_out.at[:, pl.ds(start, count)], left.at[per_block]))
         copies[-1].start()
         for copy in copies:
@@ -230,7 +262,7 @@
         in_specs=[pl.BlockSpec(memory_space=pltpu.VMEM)] * len(operands),
         out_specs=[pl.BlockSpec(memory_space=space)] * 2,
         scratch_shapes=(staged if chunks else [])
-        + [pltpu.VMEM((2, blocks, in_dev, count), jnp.float32) for _ in range(per_block)],
+        + [pltpu.VMEM((2, blocks // 2, 2 * in_dev, count), jnp.bfloat16) for _ in range(per_block)],
         out_shape=[
             jax.ShapeDtypeStruct(visibility, jnp.float32),
             jax.ShapeDtypeStruct((per_block, SPECTRA if chunks else count), jnp.float32),

time: 102 us -> 101 us (level)
  transfers between devices with their start and end apart: 16 -> 16, of which waited for: 10 -> 10; matrix products, arithmetic and copies ran while one was open for 0% -> 0% of each run, Pallas kernels for 13% -> 12%
where the time goes in v6:
time: 101 us
  waiting for transfers between devices  48.5 us (48%)
  starting transfers between devices  33.3 us (33%)
  Pallas kernels  18.3 us (18%)
    ppermute x16, waiting for transfers between devices, send(): lax.ppermute(block, AXES, [(s, s ^ other) for s in range(blocks)])  48.5 us
    ppermute x16, starting transfers between devices, send(): lax.ppermute(block, AXES, [(s, s ^ other) for s in range(blocks)])  33.3 us
    pallas_call x2, Pallas kernels, make_spectra(): pl.pallas_call(kernel, in_specs=in_specs, out_specs=[vmem] * len(out_shap...  15.5 us
    pallas_call x2, Pallas kernels, correlate(): pl.pallas_call(functools.partial(correlate_kernel, in_dev, blocks, places...  2.78 us
  transfers between devices with their start and end apart: 16, of which 10 were waited for; matrix products, arithmetic and copies ran while one was open for 0% of the time, Pallas kernels for 12%

profile of v6, /device:TPU:9, one launch (start us, length us, event | category | flops | bytes accessed | tf_op | source)
XLA Modules:
  0.0 101.1 jit_solution(5421135576922716554)
XLA Ops:
  0.6 3.4 %shard_map.59 = (bf16[48,16,256]{2,1,0:T(8,128)(2,1)S(1)}, bf16[1031,8,256]{2,1,0:T(8,128)(2,1)S(1)}, f32[8,256]{1,0:T(8,128)S(1)}, f32[256,256]{1,0:T(8,128)S(1)}, s32[16]{0:T(128)S(1)}) custom-call(s32[16]{0:T(128)} %refs_0_.1, bf16[1031,8,256]{2,1,0:T(8,128)(2,1)} %bitcast.5, f32[8,256]{1,0:T(8,128)} %constant.4.clone.refs_2_, ...), custom_call_target="tpu_custom_call" | custom-call | tf_op jit(solution)/shard_map/pallas_call | solution.py:177
  4.0 2.4 %collective-permute-start = (bf16[48,16,256]{2,1,0:T(8,128)(2,1)S(1)}, bf16[48,16,256]{2,1,0:T(8,128)(2,1)S(1)}, u32[]{:S(2)}, u32[]{:S(2)}) collective-permute-start(bf16[48,16,256]{2,1,0:T(8,128)(2,1)S(1)} %get-tuple-element.120), channel_id=1, source_target_pairs={{0,8},{1,9},{2,10},{3,11},{4,12},{5,13},{6,14},{7,15},{8,0},{9,1},... | collective-permute-start | bytes 1179656 | tf_op jit(solution)/shard_map/ppermute | solution.py:295
  6.4 12.1 %shard_map.60 = (bf16[8,16,1024]{2,1,0:T(8,128)(2,1)S(1)}, bf16[8,16,1024]{2,1,0:T(8,128)(2,1)S(1)}, bf16[8,16,768]{2,1,0:T(8,128)(2,1)S(1)}, bf16[8,16,768]{2,1...) custom-call(bf16[1031,8,256]{2,1,0:T(8,128)(2,1)S(1)} %get-tuple-ele, ...), custom_call_target="tpu_custom_call" | custom-call | tf_op jit(solution)/shard_map/pallas_call | solution.py:177
  18.5 0.1 collective-permute-start.1
  18.6 3.5 %collective-permute-start.3 = (bf16[8,16,1024]{2,1,0:T(8,128)(2,1)S(1)}, bf16[8,16,1024]{2,1,0:T(8,128)(2,1)S(1)}, u32[]{:S(2)}, u32[]{:S(2)}) collective-permute-start(bf16[8,16,1024]{2,1,0:T(8,128)(2,1)S(1)} %get-tuple-element.129), channel_id=1, source_target_pairs={{0,15},{1,14},{2,13},{3,12},{4,11},{5,10},{6,9},{7,8},{8,7},{9,6},... | collective-permute-start | bytes 786440 | tf_op jit(solution)/shard_map/ppermute | solution.py:295
  22.0 12.7 %collective-permute-done.refs_8_ = bf16[48,16,256]{2,1,0:T(8,128)(2,1)S(1)} collective-permute-done((bf16[48,16,256]{2,1,0:T(8,128)(2,1)S(1)}, bf16[48,16,256]{2,1,0:T(8,128)(2,1)S(1)}, u32[]{:S(2)}, u32[]{:S(2)}) %collective-permute-start) | collective-permute-done | bytes 393248 | tf_op jit(solution)/shard_map/ppermute | solution.py:295
  34.8 0.1 collective-permute-start.2
  34.9 2.3 %collective-permute-start.4 = (bf16[8,16,1280]{2,1,0:T(8,128)(2,1)S(1)}, bf16[8,16,1280]{2,1,0:T(8,128)(2,1)S(1)}, u32[]{:S(2)}, u32[]{:S(2)}) collective-permute-start(bf16[8,16,1280]{2,1,0:T(8,128)(2,1)S(1)} %pad_maximum_fusion.3), channel_id=1, source_target_pairs={{0,5},{1,4},{2,7},{3,6},{4,1},{5,0},{6,3},{7,2},{8,13},{9,12},{10,... | collective-permute-start | bytes 983048 | tf_op jit(solution)/shard_map/ppermute | solution.py:295
  37.3 3.1 %collective-permute-done.1.refs_14_ = bf16[8,16,1024]{2,1,0:T(8,128)(2,1)S(1)} collective-permute-done((bf16[8,16,1024]{2,1,0:T(8,128)(2,1)S(1)}, bf16[8,16,1024]{2,1,0:T(8,128)(2,1)S(1)}, u32[]{:S(2)}, u32[]{:S(2)}) %collective-permute-start.1) | collective-permute-done | bytes 262176 | tf_op jit(solution)/shard_map/ppermute | solution.py:295
  40.4 0.0 collective-permute-start.5
  40.4 2.5 %collective-permute-start.6 = (bf16[8,16,1280]{2,1,0:T(8,128)(2,1)S(1)}, bf16[8,16,1280]{2,1,0:T(8,128)(2,1)S(1)}, u32[]{:S(2)}, u32[]{:S(2)}) collective-permute-start(bf16[8,16,1280]{2,1,0:T(8,128)(2,1)S(1)} %pad_maximum_fusion), channel_id=1, source_target_pairs={{0,1},{1,0},{2,3},{3,2},{4,5},{5,4},{6,7},{7,6},{8,9},{9,8},{10,11... | collective-permute-start | bytes 983048 | tf_op jit(solution)/shard_map/ppermute | solution.py:295
  42.8 0.7 collective-permute-done.2.refs_4_.refs_12_
  43.6 4.2 %collective-permute-done.3.refs_15_ = bf16[8,16,1024]{2,1,0:T(8,128)(2,1)S(1)} collective-permute-done((bf16[8,16,1024]{2,1,0:T(8,128)(2,1)S(1)}, bf16[8,16,1024]{2,1,0:T(8,128)(2,1)S(1)}, u32[]{:S(2)}, u32[]{:S(2)}) %collective-permute-start.3) | collective-permute-done | bytes 262176 | tf_op jit(solution)/shard_map/ppermute | solution.py:295
  47.8 0.0 collective-permute-start.8
  47.8 2.9 %collective-permute-start.7 = (bf16[8,16,768]{2,1,0:T(8,128)(2,1)S(1)}, bf16[8,16,768]{2,1,0:T(8,128)(2,1)S(1)}, u32[]{:S(2)}, u32[]{:S(2)}) collective-permute-start(bf16[8,16,768]{2,1,0:T(8,128)(2,1)S(1)} %get-tuple-element.155), channel_id=1, source_target_pairs={{0,9},{1,8},{2,11},{3,10},{4,13},{5,12},{6,15},{7,14},{8,1},{9,0},... | collective-permute-start | bytes 589832 | tf_op jit(solution)/shard_map/ppermute | solution.py:295
  50.7 1.7 %collective-permute-done.4.refs_5_.refs_13_ = bf16[8,16,1280]{2,1,0:T(8,128)(2,1)S(1)} collective-permute-done((bf16[8,16,1280]{2,1,0:T(8,128)(2,1)S(1)}, bf16[8,16,1280]{2,1,0:T(8,128)(2,1)S(1)}, u32[]{:S(2)}, u32[]{:S(2)}) %collective-permute-start.4) | collective-permute-done | bytes 327712 | tf_op jit(solution)/shard_map/ppermute | solution.py:295
  52.4 4.4 %collective-permute-done.5.refs_8_ = bf16[8,16,768]{2,1,0:T(8,128)(2,1)S(1)} collective-permute-done((bf16[8,16,768]{2,1,0:T(8,128)(2,1)S(1)}, bf16[8,16,768]{2,1,0:T(8,128)(2,1)S(1)}, u32[]{:S(2)}, u32[]{:S(2)}) %collective-permute-start.5) | collective-permute-done | bytes 196640 | tf_op jit(solution)/shard_map/ppermute | solution.py:295
  56.8 3.5 %collective-permute-start.10 = (bf16[8,16,768]{2,1,0:T(8,128)(2,1)S(1)}, bf16[8,16,768]{2,1,0:T(8,128)(2,1)S(1)}, u32[]{:S(2)}, u32[]{:S(2)}) collective-permute-start(bf16[8,16,768]{2,1,0:T(8,128)(2,1)S(1)} %get-tuple-element.185), channel_id=1, source_target_pairs={{0,10},{1,11},{2,8},{3,9},{4,14},{5,15},{6,12},{7,13},{8,2},{9,3},... | collective-permute-start | bytes 589832 | tf_op jit(solution)/shard_map/ppermute | solution.py:295
  60.3 0.0 collective-permute-start.9
  60.3 0.0 collective-permute-done.6.refs_1_.refs_9_
  60.4 2.5 %collective-permute-start.11 = (bf16[8,16,1280]{2,1,0:T(8,128)(2,1)S(1)}, bf16[8,16,1280]{2,1,0:T(8,128)(2,1)S(1)}, u32[]{:S(2)}, u32[]{:S(2)}) collective-permute-start(bf16[8,16,1280]{2,1,0:T(8,128)(2,1)S(1)} %pad_maximum_fusion.4), channel_id=1, source_target_pairs={{0,3},{1,2},{2,1},{3,0},{4,7},{5,6},{6,5},{7,4},{8,11},{9,10},{10,... | collective-permute-start | bytes 983048 | tf_op jit(solution)/shard_map/ppermute | solution.py:295
  62.9 4.0 %collective-permute-done.7.refs_9_ = bf16[8,16,768]{2,1,0:T(8,128)(2,1)S(1)} collective-permute-done((bf16[8,16,768]{2,1,0:T(8,128)(2,1)S(1)}, bf16[8,16,768]{2,1,0:T(8,128)(2,1)S(1)}, u32[]{:S(2)}, u32[]{:S(2)}) %collective-permute-start.7) | collective-permute-done | bytes 196640 | tf_op jit(solution)/shard_map/ppermute | solution.py:295
  66.8 0.0 collective-permute-done.8.refs_2_.refs_10_
  66.8 5.9 %collective-permute-start.12 = (bf16[8,16,1024]{2,1,0:T(8,128)(2,1)S(1)}, bf16[8,16,1024]{2,1,0:T(8,128)(2,1)S(1)}, u32[]{:S(2)}, u32[]{:S(2)}) collective-permute-start(bf16[8,16,1024]{2,1,0:T(8,128)(2,1)S(1)} %get-tuple-element.192), channel_id=1, source_target_pairs={{0,7},{1,6},{2,5},{3,4},{4,3},{5,2},{6,1},{7,0},{8,15},{9,14},{10,... | collective-permute-start | bytes 786440 | tf_op jit(solution)/shard_map/ppermute | solution.py:295
  72.7 7.8 %collective-permute-start.15 = (bf16[8,16,768]{2,1,0:T(8,128)(2,1)S(1)}, bf16[8,16,768]{2,1,0:T(8,128)(2,1)S(1)}, u32[]{:S(2)}, u32[]{:S(2)}) collective-permute-start(bf16[8,16,768]{2,1,0:T(8,128)(2,1)S(1)} %get-tuple-element.198), channel_id=1, source_target_pairs={{0,13},{1,12},{2,15},{3,14},{4,9},{5,8},{6,11},{7,10},{8,5},{9,4},... | collective-permute-start | bytes 589832 | tf_op jit(solution)/shard_map/ppermute | solution.py:295
  80.5 8.9 %collective-permute-done.11.refs_3_.refs_11_ = bf16[8,16,1280]{2,1,0:T(8,128)(2,1)S(1)} collective-permute-done((bf16[8,16,1280]{2,1,0:T(8,128)(2,1)S(1)}, bf16[8,16,1280]{2,1,0:T(8,128)(2,1)S(1)}, u32[]{:S(2)}, u32[]{:S(2)}) %collective-permute-start.11) | collective-permute-done | bytes 327712 | tf_op jit(solution)/shard_map/ppermute | solution.py:295
  89.4 0.0 collective-permute-done.12.refs_7_
  89.4 0.5 shard_map.61
  90.0 0.0 collective-permute-done.13.refs_11_
  90.0 4.5 %collective-permute-done.15.refs_13_ = bf16[8,16,768]{2,1,0:T(8,128)(2,1)S(1)} collective-permute-done((bf16[8,16,768]{2,1,0:T(8,128)(2,1)S(1)}, bf16[8,16,768]{2,1,0:T(8,128)(2,1)S(1)}, u32[]{:S(2)}, u32[]{:S(2)}) %collective-permute-start.15) | collective-permute-done | bytes 196640 | tf_op jit(solution)/shard_map/ppermute | solution.py:295
  94.5 4.2 %collective-permute-done.14.refs_12_ = bf16[8,16,768]{2,1,0:T(8,128)(2,1)S(1)} collective-permute-done((bf16[8,16,768]{2,1,0:T(8,128)(2,1)S(1)}, bf16[8,16,768]{2,1,0:T(8,128)(2,1)S(1)}, u32[]{:S(2)}, u32[]{:S(2)}) %collective-permute-start.14) | collective-permute-done | bytes 196640 | tf_op jit(solution)/shard_map/ppermute | solution.py:295
  98.7 2.3 %shard_map.62 = (f32[8,2,128,128]{3,2,1,0:T(8,128)}, f32[8,1024]{1,0:T(8,128)}) custom-call(bf16[8,16,1024]{2,1,0:T(8,128)(2,1)S(1)} %get-tuple-element.108.refs_0_, bf16[8,16,1280]{2,1,0:T(8,128)(2,1)S(1)} %collective-permute-done.6.refs_1_.refs_9_, bf16[8,16,1280]{2,1,0:T(8,128)(2,1)S(1)} %collective-permute-done.8.refs_2_.refs_10_, ...), custom_call_target="tpu_custom_call" | custom-call | tf_op jit(solution)/shard_map/pallas_call | solution.py:260
  (13 shorter events, 0.2 us)
Async XLA Ops:
  4.0 30.8 %collective-permute-start = (bf16[48,16,256]{2,1,0:T(8,128)(2,1)S(1)}, bf16[48,16,256]{2,1,0:T(8,128)(2,1)S(1)}, u32[]{:S(2)}, u32[]{:S(2)}) collective-permute-start(bf16[48,16,256]{2,1,0:T(8,128)(2,1)S(1)} %get-tuple-element.120), channel_id=1, source_target_pairs={{0,8},{1,9},{2,10},{3,11},{4,12},{5,13},{6,14},{7,15},{8,0},{9,1},... | collective-permute-start | bytes 1179656 | tf_op jit(solution)/shard_map/ppermute | solution.py:295
  18.5 21.9 %collective-permute-start.1 = (bf16[8,16,1024]{2,1,0:T(8,128)(2,1)S(1)}, bf16[8,16,1024]{2,1,0:T(8,128)(2,1)S(1)}, u32[]{:S(2)}, u32[]{:S(2)}) collective-permute-start(bf16[8,16,1024]{2,1,0:T(8,128)(2,1)S(1)} %get-tuple-element.122), channel_id=1, source_target_pairs={{0,14},{1,15},{2,12},{3,13},{4,10},{5,11},{6,8},{7,9},{8,6},{9,7},... | collective-permute-start | bytes 786440 | tf_op jit(solution)/shard_map/ppermute | solution.py:295
  18.6 29.2 %collective-permute-start.3 = (bf16[8,16,1024]{2,1,0:T(8,128)(2,1)S(1)}, bf16[8,16,1024]{2,1,0:T(8,128)(2,1)S(1)}, u32[]{:S(2)}, u32[]{:S(2)}) collective-permute-start(bf16[8,16,1024]{2,1,0:T(8,128)(2,1)S(1)} %get-tuple-element.129), channel_id=1, source_target_pairs={{0,15},{1,14},{2,13},{3,12},{4,11},{5,10},{6,9},{7,8},{8,7},{9,6},... | collective-permute-start | bytes 786440 | tf_op jit(solution)/shard_map/ppermute | solution.py:295
  34.8 8.7 %collective-permute-start.2 = (bf16[8,16,1280]{2,1,0:T(8,128)(2,1)S(1)}, bf16[8,16,1280]{2,1,0:T(8,128)(2,1)S(1)}, u32[]{:S(2)}, u32[]{:S(2)}) collective-permute-start(bf16[8,16,1280]{2,1,0:T(8,128)(2,1)S(1)} %pad_maximum_fusion.1), channel_id=1, source_target_pairs={{0,4},{1,5},{2,6},{3,7},{4,0},{5,1},{6,2},{7,3},{8,12},{9,13},{10,... | collective-permute-start | bytes 983048 | tf_op jit(solution)/shard_map/ppermute | solution.py:295
  34.9 17.5 %collective-permute-start.4 = (bf16[8,16,1280]{2,1,0:T(8,128)(2,1)S(1)}, bf16[8,16,1280]{2,1,0:T(8,128)(2,1)S(1)}, u32[]{:S(2)}, u32[]{:S(2)}) collective-permute-start(bf16[8,16,1280]{2,1,0:T(8,128)(2,1)S(1)} %pad_maximum_fusion.3), channel_id=1, source_target_pairs={{0,5},{1,4},{2,7},{3,6},{4,1},{5,0},{6,3},{7,2},{8,13},{9,12},{10,... | collective-permute-start | bytes 983048 | tf_op jit(solution)/shard_map/ppermute | solution.py:295
  40.4 16.4 %collective-permute-start.5 = (bf16[8,16,768]{2,1,0:T(8,128)(2,1)S(1)}, bf16[8,16,768]{2,1,0:T(8,128)(2,1)S(1)}, u32[]{:S(2)}, u32[]{:S(2)}) collective-permute-start(bf16[8,16,768]{2,1,0:T(8,128)(2,1)S(1)} %get-tuple-element.140), channel_id=1, source_target_pairs={{0,8},{1,9},{2,10},{3,11},{4,12},{5,13},{6,14},{7,15},{8,0},{9,1},... | collective-permute-start | bytes 589832 | tf_op jit(solution)/shard_map/ppermute | solution.py:295
  40.4 20.0 %collective-permute-start.6 = (bf16[8,16,1280]{2,1,0:T(8,128)(2,1)S(1)}, bf16[8,16,1280]{2,1,0:T(8,128)(2,1)S(1)}, u32[]{:S(2)}, u32[]{:S(2)}) collective-permute-start(bf16[8,16,1280]{2,1,0:T(8,128)(2,1)S(1)} %pad_maximum_fusion), channel_id=1, source_target_pairs={{0,1},{1,0},{2,3},{3,2},{4,5},{5,4},{6,7},{7,6},{8,9},{9,8},{10,11... | collective-permute-start | bytes 983048 | tf_op jit(solution)/shard_map/ppermute | solution.py:295
  47.8 19.1 %collective-permute-start.8 = (bf16[8,16,1280]{2,1,0:T(8,128)(2,1)S(1)}, bf16[8,16,1280]{2,1,0:T(8,128)(2,1)S(1)}, u32[]{:S(2)}, u32[]{:S(2)}) collective-permute-start(bf16[8,16,1280]{2,1,0:T(8,128)(2,1)S(1)} %pad_maximum_fusion.2), channel_id=1, source_target_pairs={{0,2},{1,3},{2,0},{3,1},{4,6},{5,7},{6,4},{7,5},{8,10},{9,11},{10,... | collective-permute-start | bytes 983048 | tf_op jit(solution)/shard_map/ppermute | solution.py:295
  47.8 19.1 %collective-permute-start.7 = (bf16[8,16,768]{2,1,0:T(8,128)(2,1)S(1)}, bf16[8,16,768]{2,1,0:T(8,128)(2,1)S(1)}, u32[]{:S(2)}, u32[]{:S(2)}) collective-permute-start(bf16[8,16,768]{2,1,0:T(8,128)(2,1)S(1)} %get-tuple-element.155), channel_id=1, source_target_pairs={{0,9},{1,8},{2,11},{3,10},{4,13},{5,12},{6,15},{7,14},{8,1},{9,0},... | collective-permute-start | bytes 589832 | tf_op jit(solution)/shard_map/ppermute | solution.py:295
  56.8 15.9 %collective-permute-start.10 = (bf16[8,16,768]{2,1,0:T(8,128)(2,1)S(1)}, bf16[8,16,768]{2,1,0:T(8,128)(2,1)S(1)}, u32[]{:S(2)}, u32[]{:S(2)}) collective-permute-start(bf16[8,16,768]{2,1,0:T(8,128)(2,1)S(1)} %get-tuple-element.185), channel_id=1, source_target_pairs={{0,10},{1,11},{2,8},{3,9},{4,14},{5,15},{6,12},{7,13},{8,2},{9,3},... | collective-permute-start | bytes 589832 | tf_op jit(solution)/shard_map/ppermute | solution.py:295
  60.3 12.4 %collective-permute-start.9 = (bf16[8,16,1024]{2,1,0:T(8,128)(2,1)S(1)}, bf16[8,16,1024]{2,1,0:T(8,128)(2,1)S(1)}, u32[]{:S(2)}, u32[]{:S(2)}) collective-permute-start(bf16[8,16,1024]{2,1,0:T(8,128)(2,1)S(1)} %get-tuple-element.174), channel_id=1, source_target_pairs={{0,6},{1,7},{2,4},{3,5},{4,2},{5,3},{6,0},{7,1},{8,14},{9,15},{10,... | collective-permute-start | bytes 786440 | tf_op jit(solution)/shard_map/ppermute | solution.py:295
  60.4 29.1 %collective-permute-start.11 = (bf16[8,16,1280]{2,1,0:T(8,128)(2,1)S(1)}, bf16[8,16,1280]{2,1,0:T(8,128)(2,1)S(1)}, u32[]{:S(2)}, u32[]{:S(2)}) collective-permute-start(bf16[8,16,1280]{2,1,0:T(8,128)(2,1)S(1)} %pad_maximum_fusion.4), channel_id=1, source_target_pairs={{0,3},{1,2},{2,1},{3,0},{4,7},{5,6},{6,5},{7,4},{8,11},{9,10},{10,... | collective-permute-start | bytes 983048 | tf_op jit(solution)/shard_map/ppermute | solution.py:295
  66.8 22.6 %collective-permute-start.12 = (bf16[8,16,1024]{2,1,0:T(8,128)(2,1)S(1)}, bf16[8,16,1024]{2,1,0:T(8,128)(2,1)S(1)}, u32[]{:S(2)}, u32[]{:S(2)}) collective-permute-start(bf16[8,16,1024]{2,1,0:T(8,128)(2,1)S(1)} %get-tuple-element.192), channel_id=1, source_target_pairs={{0,7},{1,6},{2,5},{3,4},{4,3},{5,2},{6,1},{7,0},{8,15},{9,14},{10,... | collective-permute-start | bytes 786440 | tf_op jit(solution)/shard_map/ppermute | solution.py:295
  72.7 17.3 %collective-permute-start.13 = (bf16[8,16,768]{2,1,0:T(8,128)(2,1)S(1)}, bf16[8,16,768]{2,1,0:T(8,128)(2,1)S(1)}, u32[]{:S(2)}, u32[]{:S(2)}) collective-permute-start(bf16[8,16,768]{2,1,0:T(8,128)(2,1)S(1)} %get-tuple-element.196), channel_id=1, source_target_pairs={{0,11},{1,10},{2,9},{3,8},{4,15},{5,14},{6,13},{7,12},{8,3},{9,2},... | collective-permute-start | bytes 589832 | tf_op jit(solution)/shard_map/ppermute | solution.py:295
  72.7 21.8 %collective-permute-start.15 = (bf16[8,16,768]{2,1,0:T(8,128)(2,1)S(1)}, bf16[8,16,768]{2,1,0:T(8,128)(2,1)S(1)}, u32[]{:S(2)}, u32[]{:S(2)}) collective-permute-start(bf16[8,16,768]{2,1,0:T(8,128)(2,1)S(1)} %get-tuple-element.198), channel_id=1, source_target_pairs={{0,13},{1,12},{2,15},{3,14},{4,9},{5,8},{6,11},{7,10},{8,5},{9,4},... | collective-permute-start | bytes 589832 | tf_op jit(solution)/shard_map/ppermute | solution.py:295
  80.5 18.2 %collective-permute-start.14 = (bf16[8,16,768]{2,1,0:T(8,128)(2,1)S(1)}, bf16[8,16,768]{2,1,0:T(8,128)(2,1)S(1)}, u32[]{:S(2)}, u32[]{:S(2)}) collective-permute-start(bf16[8,16,768]{2,1,0:T(8,128)(2,1)S(1)} %get-tuple-element.197), channel_id=1, source_target_pairs={{0,12},{1,13},{2,14},{3,15},{4,8},{5,9},{6,10},{7,11},{8,4},{9,5},... | collective-permute-start | bytes 589832 | tf_op jit(solution)/shard_map/ppermute | solution.py:295

commit v7 on v6

--- a/solution.py
+++ b/solution.py
@@ -15,7 +15,7 @@
 LENGTH = 2 * CHANS
 AXES = ("row", "col")
 LANES = 128
-FRAME_GROUP = 16
+FRAME_GROUP = 32
 FIRST_TILE = 128
 TILE = 256
 VMEM = 40 * 1024 * 1024
@@ -304,7 +304,7 @@
     targets = across + last + close
     ready = dict(zip(targets, make_spectra(made[1:], SPECTRA, in_dev, blocks, targets, False)))
     taken[close[0]] = ready[close[0]]
-    distant, others = list(across + last), [close[step] for step in NEAR_ORDER if step < half]
+    distant, others = list(across[::-1] + last), [close[step] for step in NEAR_ORDER if step < half]
     others += [target for target in close[1:] if target not in others]
     order = []
     for near_before in NEARS_AHEAD:

time: 101 us -> 101 us (level)
  waiting for transfers between devices: 48.5 us -> 49.8 us
    ppermute x16, waiting for transfers between devices: 48.5 us -> 49.8 us  [send(): lax.ppermute(block, AXES, [(s, s ^ other) for s in range(blocks)])]
where the time goes in v7:
time: 101 us
  waiting for transfers between devices  49.8 us (49%)
  starting transfers between devices  32.4 us (32%)
  Pallas kernels  17.8 us (18%)
    ppermute x16, waiting for transfers between devices, send(): lax.ppermute(block, AXES, [(s, s ^ other) for s in range(blocks)])  49.8 us
    ppermute x16, starting transfers between devices, send(): lax.ppermute(block, AXES, [(s, s ^ other) for s in range(blocks)])  32.4 us
    pallas_call x2, Pallas kernels, make_spectra(): pl.pallas_call(kernel, in_specs=in_specs, out_specs=[vmem] * len(out_shap...  15.1 us
    pallas_call x2, Pallas kernels, correlate(): pl.pallas_call(functools.partial(correlate_kernel, in_dev, blocks, places...  2.78 us
  transfers between devices with their start and end apart: 16, of which 10 were waited for; matrix products, arithmetic and copies ran while one was open for 0% of the time, Pallas kernels for 12%

profile of v7, /device:TPU:9, one launch (start us, length us, event | category | flops | bytes accessed | tf_op | source)
XLA Modules:
  0.0 101.0 jit_solution(11041891019112202171)
XLA Ops:
  0.6 3.3 %shard_map.59 = (bf16[48,16,256]{2,1,0:T(8,128)(2,1)S(1)}, bf16[1031,8,256]{2,1,0:T(8,128)(2,1)S(1)}, f32[8,256]{1,0:T(8,128)S(1)}, f32[256,256]{1,0:T(8,128)S(1)}, s32[16]{0:T(128)S(1)}) custom-call(s32[16]{0:T(128)} %refs_0_.1, bf16[1031,8,256]{2,1,0:T(8,128)(2,1)} %bitcast.5, f32[8,256]{1,0:T(8,128)} %constant.4.clone.refs_2_, ...), custom_call_target="tpu_custom_call" | custom-call | tf_op jit(solution)/shard_map/pallas_call | solution.py:177
  3.9 2.4 %collective-permute-start = (bf16[48,16,256]{2,1,0:T(8,128)(2,1)S(1)}, bf16[48,16,256]{2,1,0:T(8,128)(2,1)S(1)}, u32[]{:S(2)}, u32[]{:S(2)}) collective-permute-start(bf16[48,16,256]{2,1,0:T(8,128)(2,1)S(1)} %get-tuple-element.120), channel_id=1, source_target_pairs={{0,8},{1,9},{2,10},{3,11},{4,12},{5,13},{6,14},{7,15},{8,0},{9,1},... | collective-permute-start | bytes 1179656 | tf_op jit(solution)/shard_map/ppermute | solution.py:295
  6.3 11.8 %shard_map.60 = (bf16[8,16,1024]{2,1,0:T(8,128)(2,1)S(1)}, bf16[8,16,1024]{2,1,0:T(8,128)(2,1)S(1)}, bf16[8,16,768]{2,1,0:T(8,128)(2,1)S(1)}, bf16[8,16,768]{2,1...) custom-call(bf16[1031,8,256]{2,1,0:T(8,128)(2,1)S(1)} %get-tuple-ele, ...), custom_call_target="tpu_custom_call" | custom-call | tf_op jit(solution)/shard_map/pallas_call | solution.py:177
  18.1 0.9 collective-permute-start.1
  19.0 2.4 %collective-permute-start.3 = (bf16[8,16,1024]{2,1,0:T(8,128)(2,1)S(1)}, bf16[8,16,1024]{2,1,0:T(8,128)(2,1)S(1)}, u32[]{:S(2)}, u32[]{:S(2)}) collective-permute-start(bf16[8,16,1024]{2,1,0:T(8,128)(2,1)S(1)} %get-tuple-element.129), channel_id=1, source_target_pairs={{0,14},{1,15},{2,12},{3,13},{4,10},{5,11},{6,8},{7,9},{8,6},{9,7},... | collective-permute-start | bytes 786440 | tf_op jit(solution)/shard_map/ppermute | solution.py:295
  21.4 13.3 %collective-permute-done.refs_8_ = bf16[48,16,256]{2,1,0:T(8,128)(2,1)S(1)} collective-permute-done((bf16[48,16,256]{2,1,0:T(8,128)(2,1)S(1)}, bf16[48,16,256]{2,1,0:T(8,128)(2,1)S(1)}, u32[]{:S(2)}, u32[]{:S(2)}) %collective-permute-start) | collective-permute-done | bytes 393248 | tf_op jit(solution)/shard_map/ppermute | solution.py:295
  34.7 0.1 collective-permute-start.2
  34.9 2.3 %collective-permute-start.4 = (bf16[8,16,1280]{2,1,0:T(8,128)(2,1)S(1)}, bf16[8,16,1280]{2,1,0:T(8,128)(2,1)S(1)}, u32[]{:S(2)}, u32[]{:S(2)}) collective-permute-start(bf16[8,16,1280]{2,1,0:T(8,128)(2,1)S(1)} %pad_maximum_fusion.3), channel_id=1, source_target_pairs={{0,5},{1,4},{2,7},{3,6},{4,1},{5,0},{6,3},{7,2},{8,13},{9,12},{10,... | collective-permute-start | bytes 983048 | tf_op jit(solution)/shard_map/ppermute | solution.py:295
  37.2 4.9 %collective-permute-done.1.refs_15_ = bf16[8,16,1024]{2,1,0:T(8,128)(2,1)S(1)} collective-permute-done((bf16[8,16,1024]{2,1,0:T(8,128)(2,1)S(1)}, bf16[8,16,1024]{2,1,0:T(8,128)(2,1)S(1)}, u32[]{:S(2)}, u32[]{:S(2)}) %collective-permute-start.1) | collective-permute-done | bytes 262176 | tf_op jit(solution)/shard_map/ppermute | solution.py:295
  42.1 0.0 collective-permute-start.5
  42.1 0.0 collective-permute-start.6
  42.1 1.4 %collective-permute-done.2.refs_4_.refs_12_ = bf16[8,16,1280]{2,1,0:T(8,128)(2,1)S(1)} collective-permute-done((bf16[8,16,1280]{2,1,0:T(8,128)(2,1)S(1)}, bf16[8,16,1280]{2,1,0:T(8,128)(2,1)S(1)}, u32[]{:S(2)}, u32[]{:S(2)}) %collective-permute-start.2) | collective-permute-done | bytes 327712 | tf_op jit(solution)/shard_map/ppermute | solution.py:295
  43.5 2.4 %collective-permute-done.3.refs_14_ = bf16[8,16,1024]{2,1,0:T(8,128)(2,1)S(1)} collective-permute-done((bf16[8,16,1024]{2,1,0:T(8,128)(2,1)S(1)}, bf16[8,16,1024]{2,1,0:T(8,128)(2,1)S(1)}, u32[]{:S(2)}, u32[]{:S(2)}) %collective-permute-start.3) | collective-permute-done | bytes 262176 | tf_op jit(solution)/shard_map/ppermute | solution.py:295
  45.9 1.2 %collective-permute-start.8 = (bf16[8,16,1280]{2,1,0:T(8,128)(2,1)S(1)}, bf16[8,16,1280]{2,1,0:T(8,128)(2,1)S(1)}, u32[]{:S(2)}, u32[]{:S(2)}) collective-permute-start(bf16[8,16,1280]{2,1,0:T(8,128)(2,1)S(1)} %pad_maximum_fusion.2), channel_id=1, source_target_pairs={{0,2},{1,3},{2,0},{3,1},{4,6},{5,7},{6,4},{7,5},{8,10},{9,11},{10,... | collective-permute-start | bytes 983048 | tf_op jit(solution)/shard_map/ppermute | solution.py:295
  47.2 3.4 %collective-permute-start.7 = (bf16[8,16,768]{2,1,0:T(8,128)(2,1)S(1)}, bf16[8,16,768]{2,1,0:T(8,128)(2,1)S(1)}, u32[]{:S(2)}, u32[]{:S(2)}) collective-permute-start(bf16[8,16,768]{2,1,0:T(8,128)(2,1)S(1)} %get-tuple-element.155), channel_id=1, source_target_pairs={{0,9},{1,8},{2,11},{3,10},{4,13},{5,12},{6,15},{7,14},{8,1},{9,0},... | collective-permute-start | bytes 589832 | tf_op jit(solution)/shard_map/ppermute | solution.py:295
  50.6 1.7 %collective-permute-done.4.refs_5_.refs_13_ = bf16[8,16,1280]{2,1,0:T(8,128)(2,1)S(1)} collective-permute-done((bf16[8,16,1280]{2,1,0:T(8,128)(2,1)S(1)}, bf16[8,16,1280]{2,1,0:T(8,128)(2,1)S(1)}, u32[]{:S(2)}, u32[]{:S(2)}) %collective-permute-start.4) | collective-permute-done | bytes 327712 | tf_op jit(solution)/shard_map/ppermute | solution.py:295
  52.3 4.4 %collective-permute-done.5.refs_8_ = bf16[8,16,768]{2,1,0:T(8,128)(2,1)S(1)} collective-permute-done((bf16[8,16,768]{2,1,0:T(8,128)(2,1)S(1)}, bf16[8,16,768]{2,1,0:T(8,128)(2,1)S(1)}, u32[]{:S(2)}, u32[]{:S(2)}) %collective-permute-start.5) | collective-permute-done | bytes 196640 | tf_op jit(solution)/shard_map/ppermute | solution.py:295
  56.7 3.5 %collective-permute-start.10 = (bf16[8,16,768]{2,1,0:T(8,128)(2,1)S(1)}, bf16[8,16,768]{2,1,0:T(8,128)(2,1)S(1)}, u32[]{:S(2)}, u32[]{:S(2)}) collective-permute-start(bf16[8,16,768]{2,1,0:T(8,128)(2,1)S(1)} %get-tuple-element.185), channel_id=1, source_target_pairs={{0,10},{1,11},{2,8},{3,9},{4,14},{5,15},{6,12},{7,13},{8,2},{9,3},... | collective-permute-start | bytes 589832 | tf_op jit(solution)/shard_map/ppermute | solution.py:295
  60.3 0.0 collective-permute-start.9
  60.3 2.5 %collective-permute-start.11 = (bf16[8,16,1280]{2,1,0:T(8,128)(2,1)S(1)}, bf16[8,16,1280]{2,1,0:T(8,128)(2,1)S(1)}, u32[]{:S(2)}, u32[]{:S(2)}) collective-permute-start(bf16[8,16,1280]{2,1,0:T(8,128)(2,1)S(1)} %pad_maximum_fusion.4), channel_id=1, source_target_pairs={{0,3},{1,2},{2,1},{3,0},{4,7},{5,6},{6,5},{7,4},{8,11},{9,10},{10,... | collective-permute-start | bytes 983048 | tf_op jit(solution)/shard_map/ppermute | solution.py:295
  62.8 4.0 %collective-permute-done.7.refs_9_ = bf16[8,16,768]{2,1,0:T(8,128)(2,1)S(1)} collective-permute-done((bf16[8,16,768]{2,1,0:T(8,128)(2,1)S(1)}, bf16[8,16,768]{2,1,0:T(8,128)(2,1)S(1)}, u32[]{:S(2)}, u32[]{:S(2)}) %collective-permute-start.7) | collective-permute-done | bytes 196640 | tf_op jit(solution)/shard_map/ppermute | solution.py:295
  66.8 0.0 collective-permute-done.8.refs_2_.refs_10_
  66.8 5.8 %collective-permute-start.12 = (bf16[8,16,1024]{2,1,0:T(8,128)(2,1)S(1)}, bf16[8,16,1024]{2,1,0:T(8,128)(2,1)S(1)}, u32[]{:S(2)}, u32[]{:S(2)}) collective-permute-start(bf16[8,16,1024]{2,1,0:T(8,128)(2,1)S(1)} %get-tuple-element.192), channel_id=1, source_target_pairs={{0,7},{1,6},{2,5},{3,4},{4,3},{5,2},{6,1},{7,0},{8,15},{9,14},{10,... | collective-permute-start | bytes 786440 | tf_op jit(solution)/shard_map/ppermute | solution.py:295
  72.6 0.0 collective-permute-start.13
  72.6 0.0 collective-permute-done.9.refs_6_
  72.6 0.0 collective-permute-done.10.refs_10_
  72.7 7.9 %collective-permute-start.15 = (bf16[8,16,768]{2,1,0:T(8,128)(2,1)S(1)}, bf16[8,16,768]{2,1,0:T(8,128)(2,1)S(1)}, u32[]{:S(2)}, u32[]{:S(2)}) collective-permute-start(bf16[8,16,768]{2,1,0:T(8,128)(2,1)S(1)} %get-tuple-element.198), channel_id=1, source_target_pairs={{0,13},{1,12},{2,15},{3,14},{4,9},{5,8},{6,11},{7,10},{8,5},{9,4},... | collective-permute-start | bytes 589832 | tf_op jit(solution)/shard_map/ppermute | solution.py:295
  80.5 8.9 %collective-permute-done.11.refs_3_.refs_11_ = bf16[8,16,1280]{2,1,0:T(8,128)(2,1)S(1)} collective-permute-done((bf16[8,16,1280]{2,1,0:T(8,128)(2,1)S(1)}, bf16[8,16,1280]{2,1,0:T(8,128)(2,1)S(1)}, u32[]{:S(2)}, u32[]{:S(2)}) %collective-permute-start.11) | collective-permute-done | bytes 327712 | tf_op jit(solution)/shard_map/ppermute | solution.py:295
  89.4 0.5 shard_map.61
  89.9 4.5 %collective-permute-done.15.refs_13_ = bf16[8,16,768]{2,1,0:T(8,128)(2,1)S(1)} collective-permute-done((bf16[8,16,768]{2,1,0:T(8,128)(2,1)S(1)}, bf16[8,16,768]{2,1,0:T(8,128)(2,1)S(1)}, u32[]{:S(2)}, u32[]{:S(2)}) %collective-permute-start.15) | collective-permute-done | bytes 196640 | tf_op jit(solution)/shard_map/ppermute | solution.py:295
  94.5 4.1 %collective-permute-done.14.refs_12_ = bf16[8,16,768]{2,1,0:T(8,128)(2,1)S(1)} collective-permute-done((bf16[8,16,768]{2,1,0:T(8,128)(2,1)S(1)}, bf16[8,16,768]{2,1,0:T(8,128)(2,1)S(1)}, u32[]{:S(2)}, u32[]{:S(2)}) %collective-permute-start.14) | collective-permute-done | bytes 196640 | tf_op jit(solution)/shard_map/ppermute | solution.py:295
  98.6 2.3 %shard_map.62 = (f32[8,2,128,128]{3,2,1,0:T(8,128)}, f32[8,1024]{1,0:T(8,128)}) custom-call(bf16[8,16,1024]{2,1,0:T(8,128)(2,1)S(1)} %get-tuple-element.108.refs_0_, bf16[8,16,1280]{2,1,0:T(8,128)(2,1)S(1)} %collective-permute-done.6.refs_1_.refs_9_, bf16[8,16,1280]{2,1,0:T(8,128)(2,1)S(1)} %collective-permute-done.8.refs_2_.refs_10_, ...), custom_call_target="tpu_custom_call" | custom-call | tf_op jit(solution)/shard_map/pallas_call | solution.py:260
  (13 shorter events, 0.2 us)
Async XLA Ops:
  3.9 30.8 %collective-permute-start = (bf16[48,16,256]{2,1,0:T(8,128)(2,1)S(1)}, bf16[48,16,256]{2,1,0:T(8,128)(2,1)S(1)}, u32[]{:S(2)}, u32[]{:S(2)}) collective-permute-start(bf16[48,16,256]{2,1,0:T(8,128)(2,1)S(1)} %get-tuple-element.120), channel_id=1, source_target_pairs={{0,8},{1,9},{2,10},{3,11},{4,12},{5,13},{6,14},{7,15},{8,0},{9,1},... | collective-permute-start | bytes 1179656 | tf_op jit(solution)/shard_map/ppermute | solution.py:295
  18.1 24.0 %collective-permute-start.1 = (bf16[8,16,1024]{2,1,0:T(8,128)(2,1)S(1)}, bf16[8,16,1024]{2,1,0:T(8,128)(2,1)S(1)}, u32[]{:S(2)}, u32[]{:S(2)}) collective-permute-start(bf16[8,16,1024]{2,1,0:T(8,128)(2,1)S(1)} %get-tuple-element.122), channel_id=1, source_target_pairs={{0,15},{1,14},{2,13},{3,12},{4,11},{5,10},{6,9},{7,8},{8,7},{9,6},... | collective-permute-start | bytes 786440 | tf_op jit(solution)/shard_map/ppermute | solution.py:295
  19.0 26.9 %collective-permute-start.3 = (bf16[8,16,1024]{2,1,0:T(8,128)(2,1)S(1)}, bf16[8,16,1024]{2,1,0:T(8,128)(2,1)S(1)}, u32[]{:S(2)}, u32[]{:S(2)}) collective-permute-start(bf16[8,16,1024]{2,1,0:T(8,128)(2,1)S(1)} %get-tuple-element.129), channel_id=1, source_target_pairs={{0,14},{1,15},{2,12},{3,13},{4,10},{5,11},{6,8},{7,9},{8,6},{9,7},... | collective-permute-start | bytes 786440 | tf_op jit(solution)/shard_map/ppermute | solution.py:295
  34.7 8.7 %collective-permute-start.2 = (bf16[8,16,1280]{2,1,0:T(8,128)(2,1)S(1)}, bf16[8,16,1280]{2,1,0:T(8,128)(2,1)S(1)}, u32[]{:S(2)}, u32[]{:S(2)}) collective-permute-start(bf16[8,16,1280]{2,1,0:T(8,128)(2,1)S(1)} %pad_maximum_fusion.1), channel_id=1, source_target_pairs={{0,4},{1,5},{2,6},{3,7},{4,0},{5,1},{6,2},{7,3},{8,12},{9,13},{10,... | collective-permute-start | bytes 983048 | tf_op jit(solution)/shard_map/ppermute | solution.py:295
  34.9 17.4 %collective-permute-start.4 = (bf16[8,16,1280]{2,1,0:T(8,128)(2,1)S(1)}, bf16[8,16,1280]{2,1,0:T(8,128)(2,1)S(1)}, u32[]{:S(2)}, u32[]{:S(2)}) collective-permute-start(bf16[8,16,1280]{2,1,0:T(8,128)(2,1)S(1)} %pad_maximum_fusion.3), channel_id=1, source_target_pairs={{0,5},{1,4},{2,7},{3,6},{4,1},{5,0},{6,3},{7,2},{8,13},{9,12},{10,... | collective-permute-start | bytes 983048 | tf_op jit(solution)/shard_map/ppermute | solution.py:295
  42.1 14.6 %collective-permute-start.5 = (bf16[8,16,768]{2,1,0:T(8,128)(2,1)S(1)}, bf16[8,16,768]{2,1,0:T(8,128)(2,1)S(1)}, u32[]{:S(2)}, u32[]{:S(2)}) collective-permute-start(bf16[8,16,768]{2,1,0:T(8,128)(2,1)S(1)} %get-tuple-element.140), channel_id=1, source_target_pairs={{0,8},{1,9},{2,10},{3,11},{4,12},{5,13},{6,14},{7,15},{8,0},{9,1},... | collective-permute-start | bytes 589832 | tf_op jit(solution)/shard_map/ppermute | solution.py:295
  42.1 18.2 %collective-permute-start.6 = (bf16[8,16,1280]{2,1,0:T(8,128)(2,1)S(1)}, bf16[8,16,1280]{2,1,0:T(8,128)(2,1)S(1)}, u32[]{:S(2)}, u32[]{:S(2)}) collective-permute-start(bf16[8,16,1280]{2,1,0:T(8,128)(2,1)S(1)} %pad_maximum_fusion), channel_id=1, source_target_pairs={{0,1},{1,0},{2,3},{3,2},{4,5},{5,4},{6,7},{7,6},{8,9},{9,8},{10,11... | collective-permute-start | bytes 983048 | tf_op jit(solution)/shard_map/ppermute | solution.py:295
  45.9 20.9 %collective-permute-start.8 = (bf16[8,16,1280]{2,1,0:T(8,128)(2,1)S(1)}, bf16[8,16,1280]{2,1,0:T(8,128)(2,1)S(1)}, u32[]{:S(2)}, u32[]{:S(2)}) collective-permute-start(bf16[8,16,1280]{2,1,0:T(8,128)(2,1)S(1)} %pad_maximum_fusion.2), channel_id=1, source_target_pairs={{0,2},{1,3},{2,0},{3,1},{4,6},{5,7},{6,4},{7,5},{8,10},{9,11},{10,... | collective-permute-start | bytes 983048 | tf_op jit(solution)/shard_map/ppermute | solution.py:295
  47.2 19.6 %collective-permute-start.7 = (bf16[8,16,768]{2,1,0:T(8,128)(2,1)S(1)}, bf16[8,16,768]{2,1,0:T(8,128)(2,1)S(1)}, u32[]{:S(2)}, u32[]{:S(2)}) collective-permute-start(bf16[8,16,768]{2,1,0:T(8,128)(2,1)S(1)} %get-tuple-element.155), channel_id=1, source_target_pairs={{0,9},{1,8},{2,11},{3,10},{4,13},{5,12},{6,15},{7,14},{8,1},{9,0},... | collective-permute-start | bytes 589832 | tf_op jit(solution)/shard_map/ppermute | solution.py:295
  56.7 15.9 %collective-permute-start.10 = (bf16[8,16,768]{2,1,0:T(8,128)(2,1)S(1)}, bf16[8,16,768]{2,1,0:T(8,128)(2,1)S(1)}, u32[]{:S(2)}, u32[]{:S(2)}) collective-permute-start(bf16[8,16,768]{2,1,0:T(8,128)(2,1)S(1)} %get-tuple-element.185), channel_id=1, source_target_pairs={{0,10},{1,11},{2,8},{3,9},{4,14},{5,15},{6,12},{7,13},{8,2},{9,3},... | collective-permute-start | bytes 589832 | tf_op jit(solution)/shard_map/ppermute | solution.py:295
  60.3 12.4 %collective-permute-start.9 = (bf16[8,16,1024]{2,1,0:T(8,128)(2,1)S(1)}, bf16[8,16,1024]{2,1,0:T(8,128)(2,1)S(1)}, u32[]{:S(2)}, u32[]{:S(2)}) collective-permute-start(bf16[8,16,1024]{2,1,0:T(8,128)(2,1)S(1)} %get-tuple-element.174), channel_id=1, source_target_pairs={{0,6},{1,7},{2,4},{3,5},{4,2},{5,3},{6,0},{7,1},{8,14},{9,15},{10,... | collective-permute-start | bytes 786440 | tf_op jit(solution)/shard_map/ppermute | solution.py:295
  60.3 29.1 %collective-permute-start.11 = (bf16[8,16,1280]{2,1,0:T(8,128)(2,1)S(1)}, bf16[8,16,1280]{2,1,0:T(8,128)(2,1)S(1)}, u32[]{:S(2)}, u32[]{:S(2)}) collective-permute-start(bf16[8,16,1280]{2,1,0:T(8,128)(2,1)S(1)} %pad_maximum_fusion.4), channel_id=1, source_target_pairs={{0,3},{1,2},{2,1},{3,0},{4,7},{5,6},{6,5},{7,4},{8,11},{9,10},{10,... | collective-permute-start | bytes 983048 | tf_op jit(solution)/shard_map/ppermute | solution.py:295
  66.8 22.6 %collective-permute-start.12 = (bf16[8,16,1024]{2,1,0:T(8,128)(2,1)S(1)}, bf16[8,16,1024]{2,1,0:T(8,128)(2,1)S(1)}, u32[]{:S(2)}, u32[]{:S(2)}) collective-permute-start(bf16[8,16,1024]{2,1,0:T(8,128)(2,1)S(1)} %get-tuple-element.192), channel_id=1, source_target_pairs={{0,7},{1,6},{2,5},{3,4},{4,3},{5,2},{6,1},{7,0},{8,15},{9,14},{10,... | collective-permute-start | bytes 786440 | tf_op jit(solution)/shard_map/ppermute | solution.py:295
  72.6 17.3 %collective-permute-start.13 = (bf16[8,16,768]{2,1,0:T(8,128)(2,1)S(1)}, bf16[8,16,768]{2,1,0:T(8,128)(2,1)S(1)}, u32[]{:S(2)}, u32[]{:S(2)}) collective-permute-start(bf16[8,16,768]{2,1,0:T(8,128)(2,1)S(1)} %get-tuple-element.196), channel_id=1, source_target_pairs={{0,11},{1,10},{2,9},{3,8},{4,15},{5,14},{6,13},{7,12},{8,3},{9,2},... | collective-permute-start | bytes 589832 | tf_op jit(solution)/shard_map/ppermute | solution.py:295
  72.7 21.8 %collective-permute-start.15 = (bf16[8,16,768]{2,1,0:T(8,128)(2,1)S(1)}, bf16[8,16,768]{2,1,0:T(8,128)(2,1)S(1)}, u32[]{:S(2)}, u32[]{:S(2)}) collective-permute-start(bf16[8,16,768]{2,1,0:T(8,128)(2,1)S(1)} %get-tuple-element.198), channel_id=1, source_target_pairs={{0,13},{1,12},{2,15},{3,14},{4,9},{5,8},{6,11},{7,10},{8,5},{9,4},... | collective-permute-start | bytes 589832 | tf_op jit(solution)/shard_map/ppermute | solution.py:295
  80.5 18.1 %collective-permute-start.14 = (bf16[8,16,768]{2,1,0:T(8,128)(2,1)S(1)}, bf16[8,16,768]{2,1,0:T(8,128)(2,1)S(1)}, u32[]{:S(2)}, u32[]{:S(2)}) collective-permute-start(bf16[8,16,768]{2,1,0:T(8,128)(2,1)S(1)} %get-tuple-element.197), channel_id=1, source_target_pairs={{0,12},{1,13},{2,14},{3,15},{4,8},{5,9},{6,10},{7,11},{8,4},{9,5},... | collective-permute-start | bytes 589832 | tf_op jit(solution)/shard_map/ppermute | solution.py:295
